TPU v7x, 32 devices: a whole 2x2x4 slice. The times are simulated.
32 devices in a mesh: dp: 2 (over x), pipe: 4 (over z), expert: 4 (over y, core).
Axes of the slice: x: 2, y: 2, z: 4, core: 2. Of those that a mesh axis runs over, the one named last changes fastest.
Arguments:
- output_grads: bfloat16 [2, 4, 512, 4096], P('dp', 'pipe', 'expert'), may hold values from -4 to 4
- gate_values: float32 [2, 4, 512, 8], P('dp', 'pipe', 'expert'), may hold values from 0.1 to 1
- routing: int32 [2, 4, 512, 8], P('dp', 'pipe', 'expert'), may hold values from 0 to 127, as said below
- saved_inputs: bfloat16 [2, 4, 1, 4, 16, 4096], P('dp', 'pipe'), may hold values from -6 to 6
- expert_weights: bfloat16 [4, 3, 1536, 4096], P('pipe', None, 'expert'), may hold values from -0.09375 to 0.09375
Outputs:
- passed_grads: bfloat16 [2, 4, 512, 4096], P('dp', 'pipe', 'expert')
- weight_grads: bfloat16 [4, 3, 1536, 4096], P('pipe', None, 'expert', 'dp')
Inputs may be any that keep to these rules, and one draw needn't show every extreme that they name: `routing`: each token names 8 different experts. Among the 128 tokens of one device (each aligned block of 128 tokens of a micro-batch), every expert below 1 is named by 1 to 16 tokens. In some replica and section, one such expert is named by exactly 16 tokens of every device of the expert axis.
All inputs are finite; a program needn't handle non-finite values.
Results may differ from a plain program's by a relative error of at most 0.014.
Values may be sent and summed in bfloat16 or wider, within the bound.
No kernel may reach another device: no remote copies, remote signals or barrier semaphores. Data moves between devices by JAX's collectives and lax.ppermute only.
A program may use at most 64 MiB of HBM per device.

v0:
```python
import jax
import jax.numpy as jnp
from jax import lax
from jax.sharding import PartitionSpec as P


def shifted(value, axis, by):
    devices = lax.axis_size(axis)
    return lax.ppermute(value, axis, [(i, (i + by) % devices) for i in range(devices)])


def route_tables(routing, gate_values, flight, capacity):
    expert_index = jnp.arange(flight, dtype=jnp.int32)
    matches = routing[:, :, None] == expert_index[None, None, :]
    member = jnp.any(matches, axis=1)
    gate_share = jnp.sum(jnp.where(matches, gate_values[:, :, None], jnp.float32(0.0)), axis=1)
    member_count = member.astype(jnp.int32)
    slot_index = jnp.cumsum(member_count, axis=0) - member_count
    chooser = (
        slot_index[None, :, :] == jnp.arange(capacity, dtype=jnp.int32)[:, None, None]
    ) & member[None, :, :]
    selector = jnp.transpose(chooser, (2, 0, 1))
    return (member, slot_index, gate_share, selector)


def shards(output_grads, gate_values, routing, saved_inputs, expert_weights):
    owners = lax.axis_size("expert")
    flight = max(1, owners // 16)
    per_expert = owners // flight
    own_expert = lax.axis_index("expert") // per_expert
    capacity = saved_inputs.shape[4]
    incoming = output_grads[0, 0]
    width = incoming.shape[1]
    member, slot_index, gate_share, selector = route_tables(
        routing[0, 0], gate_values[0, 0], flight, capacity
    )
    picked = jnp.einsum(
        "ect,td->ecd", selector.astype(jnp.bfloat16), incoming, preferred_element_type=jnp.float32
    )
    weighting = jnp.sum(
        jnp.where(selector, jnp.transpose(gate_share)[:, None, :], jnp.float32(0.0)), axis=-1
    )
    routed = (picked * weighting[:, :, None]).astype(jnp.bfloat16)
    full_weights = expert_weights[0]
    copies = lax.all_gather(routed, "expert", axis=0, tiled=True)
    arrived = lax.dynamic_index_in_dim(
        copies.reshape(owners, flight, capacity, width), own_expert, 1, keepdims=False
    )
    rows_count = owners * capacity
    own_inputs = lax.dynamic_index_in_dim(
        saved_inputs[0, 0], own_expert, 0, keepdims=False
    ).reshape(rows_count, width)
    routed_rows = arrived.reshape(rows_count, width)
    gate_weight = full_weights[0]
    up_weight = full_weights[1]
    down_weight = full_weights[2]
    contract = (((1,), (1,)), ((), ()))
    gate_pre = lax.dot_general(
        own_inputs, gate_weight, contract, preferred_element_type=jnp.float32
    )
    up_pre = lax.dot_general(own_inputs, up_weight, contract, preferred_element_type=jnp.float32)
    sigmoid_gate = jax.nn.sigmoid(gate_pre)
    activated = gate_pre * sigmoid_gate
    hidden = (activated * up_pre).astype(jnp.bfloat16)
    hidden_grad = lax.dot_general(
        routed_rows, down_weight, contract, preferred_element_type=jnp.float32
    )
    gate_grad = (
        hidden_grad * up_pre * sigmoid_gate * (1.0 + gate_pre * (1.0 - sigmoid_gate))
    ).astype(jnp.bfloat16)
    up_grad = (hidden_grad * activated).astype(jnp.bfloat16)
    partial_value = jnp.dot(gate_grad, gate_weight, preferred_element_type=jnp.float32) + jnp.dot(
        up_grad, up_weight, preferred_element_type=jnp.float32
    )
    partial_value = partial_value.astype(jnp.bfloat16).reshape(owners, capacity, width)
    returned = lax.all_to_all(partial_value, "expert", split_axis=0, concat_axis=0, tiled=True)
    summed = jnp.sum(
        returned.reshape(flight, per_expert, capacity, width).astype(jnp.float32), axis=1
    )
    summed_rows = summed.reshape(flight * capacity, width)
    lookup = jnp.arange(flight, dtype=jnp.int32)[None, :] * capacity + jnp.minimum(
        slot_index, capacity - 1
    )
    gathered = jnp.take(summed_rows, lookup, axis=0)
    added = jnp.sum(jnp.where(member[:, :, None], gathered, jnp.float32(0.0)), axis=1)
    input_grads = (incoming.astype(jnp.float32) + added).astype(jnp.bfloat16)
    passed_grads = shifted(input_grads, "pipe", -1)[None, None]
    by_rows = (((0,), (0,)), ((), ()))
    stacked = jnp.stack(
        [
            lax.dot_general(gate_grad, own_inputs, by_rows, preferred_element_type=jnp.float32),
            lax.dot_general(up_grad, own_inputs, by_rows, preferred_element_type=jnp.float32),
            lax.dot_general(hidden, routed_rows, by_rows, preferred_element_type=jnp.float32),
        ]
    )
    weight_total = lax.psum_scatter(
        stacked.astype(jnp.bfloat16), "dp", scatter_dimension=2, tiled=True
    )
    weight_grads = weight_total[None]
    return (passed_grads, weight_grads)


def solution(mesh):
    placed = (
        P("dp", "pipe", "expert", None),
        P("dp", "pipe", "expert", None),
        P("dp", "pipe", "expert", None),
        P("dp", "pipe", None, None, None, None),
        P("pipe", None, "expert", None),
    )
    return jax.shard_map(
        shards,
        mesh=mesh,
        in_specs=placed,
        out_specs=(P("dp", "pipe", "expert", None), P("pipe", None, "expert", "dp")),
        check_vma=False,
    )
```

profile of v0, /device:TPU:0, one launch (start us, length us, event | category | flops | bytes accessed | tf_op | source)
XLA Modules:
  0.0 153.5 jit_solution(8383239294788798772)
XLA Ops:
  7.2 0.0 copy-start
  7.2 0.0 reduce-scatter.2.cloned.1.call-start
  7.2 1.0 copy-done
  8.2 0.0 copy-start.2
  8.2 3.0 %fusion.10 = f32[64,384]{1,0:T(8,128)S(1)} fusion(bf16[64,4096]{1,0:T(8,128)(2,1)S(1)} %bitcast.54, bf16[1,3,384,4096]{3,2,1,0:T(8,128)(2,1)} %param.9), kind=kOutput, calls=%fused_computation.17 | convolution fusion | flops 201326592 | bytes 3768320 | tf_op jit(solution)/shard_map/dot_general | solution.py:61
  11.2 0.0 copy-start.3
  11.2 0.0 copy-start.1
  11.2 3.1 %fusion.7 = f32[64,384]{1,0:T(8,128)S(1)} fusion(bf16[64,4096]{1,0:T(8,128)(2,1)S(1)} %bitcast.55, bf16[1,3,384,4096]{3,2,1,0:T(8,128)(2,1)} %param.9), kind=kOutput, calls=%fused_computation.14 | convolution fusion | flops 201326592 | bytes 3768320 | tf_op jit(solution)/shard_map/dot_general | solution.py:58
  14.3 0.0 copy-done.2
  14.3 0.1 copy.9
  14.5 0.2 reduce_window_sum.15
  14.6 0.1 reduce.7
  14.8 0.0 copy-done.3
  14.8 0.1 select_reduce_fusion
  14.9 0.0 copy-done.1
  14.9 0.3 fusion.4
  15.2 8.6 %all-gather = bf16[64,4096]{1,0:T(8,128)(2,1)S(1)} all-gather(bf16[16,4096]{1,0:T(8,128)(2,1)S(1)} %fusion.4), channel_id=2, replica_groups=mesh['dp'=2,'pipe'=4,'expert'=4] {'expert'}, dimensions={0}, use_global_device_ids=true | all-gather | bytes 655360 | tf_op jit(solution)/shard_map/all_gather | solution.py:45
  23.8 1.0 fusion.2
  24.8 3.0 %multiply_convert_fusion.1 = (bf16[64,384]{1,0:T(8,128)(2,1)S(1)}, bf16[64,384]{1,0:T(8,128)(2,1)S(1)}) fusion(f32[64,384]{1,0:T(8,128)S(1)} %fusion.7, f32[64,384]{1,0:T(8,128)S(1)} %fusion.10, bf16[64,4096]{1,0:T(8,128)(2,1)S(1)} %all-gather, bf16[1,3,384,4096]{3,2,1,0:T(8,128)(2,1)} %param.9), kind=kOutput, calls=%fused_computation.30 | convolution fusion | flops 201646080 | bytes 3964928 | tf_op jit(solution)/shard_map/dot_general | solution.py:65
  27.8 1.0 fusion
  28.8 1.0 fusion.1
  29.8 4.3 %pad_maximum_fusion = bf16[3,384,4096]{2,1,0:T(8,128)(2,1)} fusion(bf16[1,384,4096]{2,1,0:T(8,128)(2,1)S(1)} %fusion.2, bf16[1,384,4096]{2,1,0:T(8,128)(2,1)S(1)} %fusion.1, bf16[1,384,4096]{2,1,0:T(8,128)(2,1)S(1)} %fusion), kind=kLoop, calls=%fused_computation.1 | loop fusion | flops 9437184 | bytes 18874368 | tf_op jit(solution)/shard_map/stack | solution.py:89
  34.1 0.0 reduce-scatter.2.cloned.1.call-update
  34.1 2.6 %fusion.5 = f32[64,4096]{1,0:T(8,128)S(1)} fusion(bf16[64,384]{1,0:T(8,128)(2,1)S(1)} %get-tuple-element.7, bf16[1,3,384,4096]{3,2,1,0:T(8,128)(2,1)} %param.9), kind=kOutput, calls=%fused_computation.12 | convolution fusion | flops 201326592 | bytes 4243456 | tf_op jit(solution)/shard_map/dot_general | solution.py:72
  36.7 3.4 %fusion.3 = bf16[64,4096]{1,0:T(8,128)(2,1)} fusion(f32[64,4096]{1,0:T(8,128)S(1)} %fusion.5, bf16[64,384]{1,0:T(8,128)(2,1)S(1)} %get-tuple-element.6, bf16[1,3,384,4096]{3,2,1,0:T(8,128)(2,1)} %param.9), kind=kOutput, calls=%fused_computation.9 | convolution fusion | flops 201850880 | bytes 4767744 | tf_op jit(solution)/shard_map/dot_general | solution.py:72
  40.1 3.5 %all-to-all-start = ((bf16[4,16,4096]{2,1,0:T(8,128)(2,1)}), bf16[4,16,4096]{2,1,0:T(8,128)(2,1)S(1)}, u32[]{:S(2)}, u32[]{:S(2)}) async-start(bf16[4,16,4096]{2,1,0:T(8,128)(2,1)} %bitcast.7), calls=%async_computation | async-start | bytes 1048576 | tf_op jit(solution)/shard_map/all_to_all | solution.py:76
  43.6 8.8 %all-to-all-done = bf16[4,16,4096]{2,1,0:T(8,128)(2,1)S(1)} async-done(((bf16[4,16,4096]{2,1,0:T(8,128)(2,1)}), bf16[4,16,4096]{2,1,0:T(8,128)(2,1)S(1)}, u32[]{:S(2)}, u32[]{:S(2)}) %all-to-all-start) | async-done | bytes 524320 | tf_op jit(solution)/shard_map/all_to_all | solution.py:76
  52.4 0.1 convert_reduce_fusion
  52.4 1.3 gather_fusion
  53.8 1.7 %add_convert_fusion = bf16[128,4096]{1,0:T(8,128)(2,1)S(1)} fusion(f32[128,4096]{1,0:T(8,128)S(1)} %gather_fusion, bf16[1,1,128,4096]{3,2,1,0:T(8,128)(2,1)} %param.5, pred[128]{0:T(512)(128)(4,1)S(1)} %get-tuple-element.2, pred[128]{0:T(512)(128)(4,1)S(1)} %get-tuple-element.4), kind=kLoop, calls=%fused_computation.26 | loop fusion | flops 2621440 | bytes 4194560 | tf_op jit(solution)/shard_map/convert_element_type | solution.py:86
  55.5 3.7 %collective-permute-start = (bf16[128,4096]{1,0:T(8,128)(2,1)S(1)}, bf16[128,4096]{1,0:T(8,128)(2,1)S(1)}, u32[]{:S(2)}, u32[]{:S(2)}) collective-permute-start(bf16[128,4096]{1,0:T(8,128)(2,1)S(1)} %add_convert_fusion), channel_id=1, source_target_pairs={{0,12},{4,0},{8,4},{12,8},{1,13},{5,1},{9,5},{13,9},{2,14},{6,2},{... | collective-permute-start | bytes 3145736 | tf_op jit(solution)/shard_map/ppermute | solution.py:9
  59.1 22.3 %collective-permute-done = bf16[128,4096]{1,0:T(8,128)(2,1)S(1)} collective-permute-done((bf16[128,4096]{1,0:T(8,128)(2,1)S(1)}, bf16[128,4096]{1,0:T(8,128)(2,1)S(1)}, u32[]{:S(2)}, u32[]{:S(2)}) %collective-permute-start) | collective-permute-done | bytes 1048608 | tf_op jit(solution)/shard_map/ppermute | solution.py:9
  81.5 64.2 %reduce-scatter.2.cloned.1.call-done = bf16[3,384,2048]{2,1,0:T(8,128)(2,1)} async-done(((bf16[3,384,4096]{2,1,0:T(8,128)(2,1)}), bf16[3,384,2048]{2,1,0:T(8,128)(2,1)}) %reduce-scatter.2.cloned.1.call-update) | async-done | bytes 4718608 | tf_op jit(solution)/shard_map/reduce_scatter | solution.py:96
  145.7 1.0 copy.11
  (6 shorter events, 0.1 us)
Async XLA Ops:
  7.2 1.0 copy-start
  7.2 138.5 %reduce-scatter.2.cloned.1.call-start = ((), (), s32[]{:S(2)}) async-start(), calls=%async_computation.2 | async-start | bytes 14155776 | tf_op jit(solution)/shard_map/reduce_scatter | solution.py:96
  8.2 6.1 %copy-start.2 = (s32[1,1,128,8]{2,3,1,0:T(8,128)S(1)}, s32[1,1,128,8]{2,3,1,0:T(8,128)}, u32[]{:S(2)}) copy-start(s32[1,1,128,8]{2,3,1,0:T(8,128)} %param.7) | copy-start | bytes 12292
  11.2 3.5 %copy-start.3 = (f32[1,1,128,8]{2,3,1,0:T(8,128)S(1)}, f32[1,1,128,8]{2,3,1,0:T(8,128)}, u32[]{:S(2)}) copy-start(f32[1,1,128,8]{2,3,1,0:T(8,128)} %param.6) | copy-start | bytes 12292
  11.2 3.7 %copy-start.1 = (bf16[1,1,128,4096]{3,2,1,0:T(8,128)(2,1)S(1)}, bf16[1,1,128,4096]{3,2,1,0:T(8,128)(2,1)}, u32[]{:S(2)}) copy-start(bf16[1,1,128,4096]{3,2,1,0:T(8,128)(2,1)} %param.5) | copy-start | bytes 3145732
  40.1 12.3 %all-to-all-start = ((bf16[4,16,4096]{2,1,0:T(8,128)(2,1)}), bf16[4,16,4096]{2,1,0:T(8,128)(2,1)S(1)}, u32[]{:S(2)}, u32[]{:S(2)}) async-start(bf16[4,16,4096]{2,1,0:T(8,128)(2,1)} %bitcast.7), calls=%async_computation | async-start | bytes 1048576 | tf_op jit(solution)/shard_map/all_to_all | solution.py:76
  55.5 26.0 %collective-permute-start = (bf16[128,4096]{1,0:T(8,128)(2,1)S(1)}, bf16[128,4096]{1,0:T(8,128)(2,1)S(1)}, u32[]{:S(2)}, u32[]{:S(2)}) collective-permute-start(bf16[128,4096]{1,0:T(8,128)(2,1)S(1)} %add_convert_fusion), channel_id=1, source_target_pairs={{0,12},{4,0},{8,4},{12,8},{1,13},{5,1},{9,5},{13,9},{2,14},{6,2},{... | collective-permute-start | bytes 3145736 | tf_op jit(solution)/shard_map/ppermute | solution.py:9
Sparse Core Ops, SparseCore 0:
  34.2 111.4 reduce-scatter.1
where the time goes:
time: 154 us
  waiting for transfers between devices  95.4 us (62%)
  matrix products  18.3 us (12%)
  between operations  14.2 us (9%)
  blocking collectives  8.65 us (6%)
  starting transfers between devices  7.17 us (5%)
  other arithmetic  6.49 us (4%)
  local copies, waits for them, and re-layouts  3.42 us (2%)
    reduce_scatter x1, waiting for transfers between devices, shards(): lax.psum_scatter(stacked.astype(jnp.bfloat16), 'dp', scatter_dimension=2,...  64.2 us
    ppermute x1, waiting for transfers between devices, shifted(): lax.ppermute(value, axis, [(i, (i + by) % devices) for i in range(devices)])  22.3 us
    all_to_all x1, waiting for transfers between devices, shards(): lax.all_to_all(partial_value, 'expert', split_axis=0, concat_axis=0, tile...  8.78 us
    all_gather x1, blocking collectives, shards(): copies = lax.all_gather(routed, 'expert', axis=0, tiled=True)  8.65 us
    another operation x1, other arithmetic, shards(): jnp.stack([lax.dot_general(gate_grad, own_inputs, by_rows, preferred_elem...  4.27 us
    ppermute x1, starting transfers between devices, shifted(): lax.ppermute(value, axis, [(i, (i + by) % devices) for i in range(devices)])  3.66 us
    all_to_all x1, starting transfers between devices, shards(): lax.all_to_all(partial_value, 'expert', split_axis=0, concat_axis=0, tile...  3.47 us
    dot_general x1, matrix products, shards(): jnp.dot(up_grad, up_weight, preferred_element_type=jnp.float32)  3.39 us
  transfers between devices with their start and end apart: 3, of which 3 were waited for; matrix products, arithmetic and copies ran while one was open for 6% of the time, Pallas kernels for 0%

commit v1 on v0

v1 whole, which is shorter than its diff:
```python
import jax
import jax.numpy as jnp
from jax import lax
from jax.sharding import PartitionSpec as P


def partner(index, step, count):
    if count & (count - 1) == 0:
        return index ^ step
    return (index + step) % count


def origin(index, step, count):
    if count & (count - 1) == 0:
        return index ^ step
    return (index - step) % count


def exchange(value, axis, step):
    count = lax.axis_size(axis)
    return lax.ppermute(value, axis, [(i, partner(i, step, count)) for i in range(count)])


def to_previous(value):
    count = lax.axis_size("pipe")
    return lax.ppermute(value, "pipe", [(i, (i - 1) % count) for i in range(count)])


def route_tables(routing, gate_values, capacity):
    matches = routing == 0
    member = jnp.any(matches, axis=1)
    count = member.astype(jnp.int32)
    slot = jnp.cumsum(count) - count
    share = jnp.sum(jnp.where(matches, gate_values, jnp.float32(0.0)), axis=1)
    selector = (slot[None, :] == jnp.arange(capacity, dtype=jnp.int32)[:, None]) & member[None, :]
    return member, slot, share, selector


def shards(output_grads, gate_values, routing, saved_inputs, expert_weights):
    owners = lax.axis_size("expert")
    replicas = lax.axis_size("dp")
    capacity = saved_inputs.shape[4]
    incoming = output_grads[0, 0]
    width = incoming.shape[1]
    part = width // replicas
    me = lax.axis_index("expert")
    replica = lax.axis_index("dp")

    shifted = to_previous(incoming)
    next_routing = to_previous(routing[0, 0])

    saved = saved_inputs[0, 0, 0]
    own_inputs = jnp.concatenate(
        [lax.dynamic_index_in_dim(saved, origin(me, k, owners), 0, keepdims=False) for k in range(owners)]
    )

    def columns_of(rows, who):
        return lax.dynamic_slice_in_dim(rows, who * part, part, axis=1)

    def across(rows):
        return [
            exchange(columns_of(rows, partner(replica, k, replicas)), "dp", k) for k in range(1, replicas)
        ]

    far_inputs = across(own_inputs)

    member, slot, share, selector = route_tables(routing[0, 0], gate_values[0, 0], capacity)
    picked = jnp.dot(selector.astype(jnp.bfloat16), incoming, preferred_element_type=jnp.float32)
    weighting = jnp.sum(jnp.where(selector, share[None, :], jnp.float32(0.0)), axis=-1)
    routed = (picked * weighting[:, None]).astype(jnp.bfloat16)
    arrived = [routed] + [exchange(routed, "expert", k) for k in range(1, owners)]

    gate_weight, up_weight, down_weight = expert_weights[0, 0], expert_weights[0, 1], expert_weights[0, 2]
    contract = (((1,), (1,)), ((), ()))
    gate_pre = lax.dot_general(own_inputs, gate_weight, contract, preferred_element_type=jnp.float32)
    up_pre = lax.dot_general(own_inputs, up_weight, contract, preferred_element_type=jnp.float32)
    sigmoid_gate = jax.nn.sigmoid(gate_pre)
    activated = gate_pre * sigmoid_gate
    hidden = (activated * up_pre).astype(jnp.bfloat16)
    slope = up_pre * sigmoid_gate * (1.0 + gate_pre * (1.0 - sigmoid_gate))

    routed_rows = jnp.concatenate(arrived)
    hidden_grad = lax.dot_general(
        routed_rows, down_weight, contract, preferred_element_type=jnp.float32
    )
    gate_grad = (hidden_grad * slope).astype(jnp.bfloat16)
    up_grad = (hidden_grad * activated).astype(jnp.bfloat16)
    partial_value = (
        jnp.dot(gate_grad, gate_weight, preferred_element_type=jnp.float32)
        + jnp.dot(up_grad, up_weight, preferred_element_type=jnp.float32)
    ).astype(jnp.bfloat16)
    blocks = partial_value.reshape(owners, capacity, width)
    summed = blocks[0].astype(jnp.float32)
    for k in range(1, owners):
        summed = summed + exchange(blocks[k], "expert", k).astype(jnp.float32)
    changed = (picked + summed).astype(jnp.bfloat16)
    next_changed = to_previous(changed)

    far_rows = across(routed_rows)
    factors = jnp.concatenate([gate_grad, up_grad, hidden], axis=1)
    far_factors = [exchange(factors, "dp", k) for k in range(1, replicas)]
    inputs_all = jnp.concatenate([columns_of(own_inputs, replica)] + far_inputs)
    rows_all = jnp.concatenate([columns_of(routed_rows, replica)] + far_rows)
    factors_all = jnp.concatenate([factors] + far_factors)
    hid = gate_weight.shape[0]
    by_rows = (((0,), (0,)), ((), ()))
    weight_grads = jnp.stack(
        [
            lax.dot_general(
                factors_all[:, i * hid : (i + 1) * hid],
                rows_all if i == 2 else inputs_all,
                by_rows,
                preferred_element_type=jnp.float32,
            ).astype(jnp.bfloat16)
            for i in range(3)
        ]
    )[None]

    next_member, next_slot, _, next_selector = route_tables(
        next_routing, jnp.zeros(next_routing.shape, jnp.float32), capacity
    )
    placed = jnp.dot(
        jnp.transpose(next_selector).astype(jnp.bfloat16), next_changed, preferred_element_type=jnp.float32
    ).astype(jnp.bfloat16)
    passed_grads = jnp.where(next_member[:, None], placed, shifted)[None, None]
    return (passed_grads, weight_grads)


def solution(mesh):
    placed = (
        P("dp", "pipe", "expert", None),
        P("dp", "pipe", "expert", None),
        P("dp", "pipe", "expert", None),
        P("dp", "pipe", None, None, None, None),
        P("pipe", None, "expert", None),
    )
    return jax.shard_map(
        shards,
        mesh=mesh,
        in_specs=placed,
        out_specs=(P("dp", "pipe", "expert", None), P("pipe", None, "expert", "dp")),
        check_vma=False,
    )
```

time: 154 us -> 50 us (0.32)
  waiting for transfers between devices: 95.4 us -> 9.29 us
  between operations: 14.2 us -> 0.82 us
  blocking collectives: 8.65 us -> 0 us
  starting transfers between devices: 7.17 us -> 12.5 us
  matrix products: 18.3 us -> 20.4 us
  local copies, waits for them, and re-layouts: 3.42 us -> 1.49 us
    reduce_scatter x1 -> x0, waiting for transfers between devices: 64.2 us -> none  [shards(): lax.psum_scatter(stacked.astype(jnp.bfloat16), 'dp', scatter_dimension=2,...]
    ppermute x1 -> x12, waiting for transfers between devices: 22.3 us -> 9.29 us  [the longest x9 8.96 us: exchange(): lax.ppermute(value, axis, [(i, partner(i, step, count)) for i in range(co...]
    ppermute x1 -> x12, starting transfers between devices: 3.66 us -> 12.5 us  [the longest x9 8 us: exchange(): lax.ppermute(value, axis, [(i, partner(i, step, count)) for i in range(co...]
    all_to_all x1 -> x0, waiting for transfers between devices: 8.78 us -> none  [shards(): lax.all_to_all(partial_value, 'expert', split_axis=0, concat_axis=0, tile...]
    all_gather x1 -> x0, blocking collectives: 8.65 us -> none  [shards(): copies = lax.all_gather(routed, 'expert', axis=0, tiled=True)]
    another operation x3 -> x4, other arithmetic: 4.55 us -> 0.55 us  [the longest x1 4.27 us: shards(): jnp.stack([lax.dot_general(gate_grad, own_inputs, by_rows, preferred_elem...]
    all_to_all x1 -> x0, starting transfers between devices: 3.47 us -> none  [shards(): lax.all_to_all(partial_value, 'expert', split_axis=0, concat_axis=0, tile...]
    broadcast_in_dim x0 -> x1, other arithmetic: none -> 2.46 us  [shards(): jnp.stack([lax.dot_general(factors_all[:, i * hid:(i + 1) * hid], rows_al...]
  transfers between devices with their start and end apart: 3 -> 12, of which waited for: 3 -> 4; matrix products, arithmetic and copies ran while one was open for 6% -> 46% of each run, Pallas kernels for 0% -> 0%
where the time goes in v1:
time: 50 us; the launch traced here: 49.7 us
  matrix products  20.4 us (41%)
  starting transfers between devices  12.5 us (25%)
  waiting for transfers between devices  9.29 us (19%)
  other arithmetic  5.12 us (10%)
  local copies, waits for them, and re-layouts  1.49 us (3%)
  between operations  0.82 us (2%)
    ppermute x9, waiting for transfers between devices, exchange(): lax.ppermute(value, axis, [(i, partner(i, step, count)) for i in range(co...  8.96 us
    ppermute x9, starting transfers between devices, exchange(): lax.ppermute(value, axis, [(i, partner(i, step, count)) for i in range(co...  8 us
    ppermute x3, starting transfers between devices, to_previous(): lax.ppermute(value, 'pipe', [(i, (i - 1) % count) for i in range(count)])  4.55 us
    dot_general x1, matrix products, shards(): lax.dot_general(own_inputs, up_weight, contract, preferred_element_type=j...  3.72 us
    dot_general x1, matrix products, shards(): lax.dot_general(own_inputs, gate_weight, contract, preferred_element_type...  3.63 us
    dot_general x1, matrix products, shards(): lax.dot_general(routed_rows, down_weight, contract, preferred_element_typ...  3.18 us
    dot_general x1, matrix products, shards(): jnp.dot(up_grad, up_weight, preferred_element_type=jnp.float32)  2.61 us
    dot_general x1, matrix products, shards(): jnp.dot(gate_grad, gate_weight, preferred_element_type=jnp.float32)  2.58 us
  transfers between devices with their start and end apart: 12, of which 4 were waited for; matrix products, arithmetic and copies ran while one was open for 46% of the time, Pallas kernels for 0%

profile of v1, /device:TPU:0, one launch (start us, length us, event | category | flops | bytes accessed | tf_op | source)
XLA Modules:
  0.0 49.7 jit_solution(4982753083030442813)
XLA Ops:
  0.6 0.0 copy-start.1
  0.6 0.8 %fusion.32 = (f32[128]{0:T(128)S(1)}, pred[128,8]{0,1:T(8,128)(4,1)S(1)}) fusion(f32[1,1,128,8]{2,3,1,0:T(8,128)} %param.6, s32[1,1,128,8]{2,3,1,0:T(8,128)} %param.7), kind=kLoop, calls=%fused_computation.54 | loop fusion | flops 2944 | bytes 9728 | tf_op jit(solution)/shard_map/reduce_sum | solution.py:34
  1.4 0.1 copy.12
  1.6 0.2 reduce-window.17
  1.7 0.1 reduce.1
  1.8 0.1 select_reduce_fusion
  2.0 1.5 %multiply_convert_fusion = (bf16[16,4096]{1,0:T(8,128)(2,1)S(1)}, f32[16,4096]{1,0:T(8,128)S(1)}) fusion(f32[16]{0:T(128)S(1)} %select_reduce_fusion, bf16[1,1,128,4096]{3,2,1,0:T(8,128)(2,1)} %param.5, s32[128]{0:T(128)S(1)} %convert_subtract_fusion, pred[128]{0:T(512)(128)(4,1)S(1)} %reduce_or.19), kind=kOutput, calls=%fused_computation.33 | convolution fusion | flops 16912384 | bytes 1442496 | tf_op jit(solution)/shard_map/dot_general | solution.py:68
  3.4 0.5 %collective-permute-start.1 = (bf16[16,4096]{1,0:T(8,128)(2,1)S(1)}, bf16[16,4096]{1,0:T(8,128)(2,1)S(1)}, u32[]{:S(2)}, u32[]{:S(2)}) collective-permute-start(bf16[16,4096]{1,0:T(8,128)(2,1)S(1)} %get-tuple-element.18), channel_id=1, source_target_pairs={{0,1},{1,0},{2,3},{3,2},{4,5},{5,4},{6,7},{7,6},{8,9},{9,8},{10,11... | collective-permute-start | bytes 393224 | tf_op jit(solution)/shard_map/ppermute | solution.py:21
  4.0 2.6 %collective-permute-start.2 = (bf16[16,4096]{1,0:T(8,128)(2,1)S(1)}, bf16[16,4096]{1,0:T(8,128)(2,1)}, u32[]{:S(2)}, u32[]{:S(2)}) collective-permute-start(bf16[16,4096]{1,0:T(8,128)(2,1)S(1)} %get-tuple-element.18), channel_id=1, source_target_pairs={{0,2},{1,3},{2,0},{3,1},{4,6},{5,7},{6,4},{7,5},{8,10},{9,11},{10,... | collective-permute-start | bytes 393224 | tf_op jit(solution)/shard_map/ppermute | solution.py:21
  6.6 0.1 collective-permute-start.3
  6.6 1.1 %dynamic-slice_bitcast_fusion.3 = (bf16[16,4096]{1,0:T(8,128)(2,1)S(1)}, bf16[16,4096]{1,0:T(8,128)(2,1)S(1)}, bf16[16,4096]{1,0:T(8,128)(2,1)S(1)}, bf16[16,4096]{1,0:T(8,128)(2,1)S(1)}) fusion(bf16[1,1,1,4,16,4096]{5,4,3,2,1,0:T(8,128)(2,1)} %param.8, s32[]{:T(128)S(6)} %select_n.35, s32[]{:T(128)S(6)} %select_n.36, s32[]{:T(128)S(6)} %select_n.38, ...), kind=kLoop, calls=%fused_computation.38 | loop fusion | bytes 1048592 | tf_op jit(solution)/shard_map/jit(dynamic_index_in_dim)/squeeze | solution.py:54
  7.8 0.1 constant_dynamic-slice_fusion.3
  7.9 1.8 %collective-permute-start.10 = (bf16[64,2048]{1,0:T(8,128)(2,1)S(1)}, bf16[64,2048]{1,0:T(8,128)(2,1)S(1)}, u32[]{:S(2)}, u32[]{:S(2)}) collective-permute-start(bf16[64,2048]{1,0:T(8,128)(2,1)S(1)} %get-tuple-element.5), channel_id=1, source_target_pairs={{0,16},{16,0},{1,17},{17,1},{2,18},{18,2},{3,19},{19,3},{4,20},{20... | collective-permute-start | bytes 786440 | tf_op jit(solution)/shard_map/ppermute | solution.py:21
  9.6 3.6 %collective-permute-start = (s32[128,8]{0,1:T(8,128)S(1)}, s32[128,8]{0,1:T(8,128)S(1)}, u32[]{:S(2)}, u32[]{:S(2)}) collective-permute-start(s32[128,8]{0,1:T(8,128)S(1)} %bitcast.53), channel_id=1, source_target_pairs={{0,12},{4,0},{8,4},{12,8},{1,13},{5,1},{9,5},{13,9},{2,14},{6,2},{... | collective-permute-start | bytes 12296 | tf_op jit(solution)/shard_map/ppermute | solution.py:26
  13.2 3.6 %fusion.3 = f32[64,384]{1,0:T(8,128)} fusion(bf16[1,3,384,4096]{3,2,1,0:T(8,128)(2,1)} %param.9, bf16[16,4096]{1,0:T(8,128)(2,1)S(1)} %get-tuple-element.13, bf16[16,4096]{1,0:T(8,128)(2,1)S(1)} %get-tuple-element.14, bf16[16,4096]{1,0:T(8,128)(2,1)S(1)} %get-tuple-element.12, bf16[16,4096]{1,0:T(8,128)(2,1)S(1)} %get-tuple-element.11), kind=kOutput, calls=%fused_computation.6 | convolution fusion | flops 203423744 | bytes 3768320 | tf_op jit(solution)/shard_map/dot_general | solution.py:75
  16.9 3.7 %fusion.6 = f32[64,384]{1,0:T(8,128)} fusion(bf16[1,3,384,4096]{3,2,1,0:T(8,128)(2,1)} %param.9, bf16[16,4096]{1,0:T(8,128)(2,1)S(1)} %get-tuple-element.13, bf16[16,4096]{1,0:T(8,128)(2,1)S(1)} %get-tuple-element.14, bf16[16,4096]{1,0:T(8,128)(2,1)S(1)} %get-tuple-element.12, bf16[16,4096]{1,0:T(8,128)(2,1)S(1)} %get-tuple-element.11), kind=kOutput, calls=%fused_computation.9 | convolution fusion | flops 203423744 | bytes 3768320 | tf_op jit(solution)/shard_map/dot_general | solution.py:76
  20.6 0.0 collective-permute-done
  20.6 0.4 collective-permute-start.8
  21.1 0.1 copy.11
  21.2 0.2 reduce-window.16
  21.3 0.1 reduce
  21.5 0.0 collective-permute-done.1
  21.5 0.0 collective-permute-done.2
  21.5 0.0 collective-permute-done.3
  21.5 1.0 %pad_maximum_fusion = bf16[64,4096]{1,0:T(8,128)(2,1)S(1)} fusion(bf16[16,4096]{1,0:T(8,128)(2,1)} %collective-permute-done.3, bf16[16,4096]{1,0:T(8,128)(2,1)} %collective-permute-done.2, bf16[16,4096]{1,0:T(8,128)(2,1)S(1)} %collective-permute-done.1, bf16[16,4096]{1,0:T(8,128)(2,1)S(1)} %get-tuple-element.18), kind=kLoop, calls=%fused_computation.25 | loop fusion | flops 2097152 | bytes 1048576 | tf_op jit(solution)/shard_map/concatenate | solution.py:82
  22.6 3.2 %multiply_convert_fusion.1 = (bf16[64,384]{1,0:T(8,128)(2,1)S(1)}, bf16[64,384]{1,0:T(8,128)(2,1)S(1)}, bf16[64,384]{1,0:T(8,128)(2,1)S(1)}) fusion(f32[64,384]{1,0:T(8,128)} %fusion.6, f32[64,384]{1,0:T(8,128)} %fusion.3, bf16[1,3,384,4096]{3,2,1,0:T(8,128)(2,1)} %param.9, bf16[16,4096]{1,0:T(8,128)(2,1)} %collective-permute-done.3, ...), kind=kOutput, calls=%fused_computation.42 | convolution fusion | flops 203792384 | bytes 4014080 | tf_op jit(solution)/shard_map/dot_general | solution.py:83
  25.8 2.6 %fusion.1 = f32[64,4096]{1,0:T(8,128)S(1)} fusion(bf16[64,384]{1,0:T(8,128)(2,1)S(1)} %get-tuple-element.16, bf16[1,3,384,4096]{3,2,1,0:T(8,128)(2,1)} %param.9), kind=kOutput, calls=%fused_computation.4 | convolution fusion | flops 201326592 | bytes 4243456 | tf_op jit(solution)/shard_map/dot_general | solution.py:89
  28.3 2.6 %fusion = bf16[64,4096]{1,0:T(8,128)(2,1)S(1)} fusion(f32[64,4096]{1,0:T(8,128)S(1)} %fusion.1, bf16[64,384]{1,0:T(8,128)(2,1)S(1)} %get-tuple-element.17, bf16[1,3,384,4096]{3,2,1,0:T(8,128)(2,1)} %param.9), kind=kOutput, calls=%fused_computation.3 | convolution fusion | flops 201850880 | bytes 4767744 | tf_op jit(solution)/shard_map/dot_general | solution.py:90
  31.0 0.1 collective-permute-start.4
  31.1 1.6 %collective-permute-start.5 = (bf16[16,4096]{1,0:T(8,128)(2,1)S(1)}, bf16[16,4096]{1,0:T(8,128)(2,1)S(1)}, u32[]{:S(2)}, u32[]{:S(2)}) collective-permute-start(bf16[16,4096]{1,0:T(8,128)(2,1)S(1)} %get-tuple-element.10), channel_id=1, source_target_pairs={{0,2},{1,3},{2,0},{3,1},{4,6},{5,7},{6,4},{7,5},{8,10},{9,11},{10,... | collective-permute-start | bytes 393224 | tf_op jit(solution)/shard_map/ppermute | solution.py:21
  32.7 0.3 collective-permute-start.6
  32.9 0.0 collective-permute-done.4
  33.0 0.6 %collective-permute-start.9 = (bf16[64,1152]{1,0:T(8,128)(2,1)S(1)}, bf16[64,1152]{1,0:T(8,128)(2,1)S(1)}, u32[]{:S(2)}, u32[]{:S(2)}) collective-permute-start(bf16[64,1152]{1,0:T(8,128)(2,1)S(1)} %pad_maximum_fusion.6), channel_id=1, source_target_pairs={{0,16},{16,0},{1,17},{17,1},{2,18},{18,2},{3,19},{19,3},{4,20},{20... | collective-permute-start | bytes 442376 | tf_op jit(solution)/shard_map/ppermute | solution.py:21
  33.6 3.9 %collective-permute-done.5 = bf16[16,4096]{1,0:T(8,128)(2,1)S(1)} collective-permute-done((bf16[16,4096]{1,0:T(8,128)(2,1)S(1)}, bf16[16,4096]{1,0:T(8,128)(2,1)S(1)}, u32[]{:S(2)}, u32[]{:S(2)}) %collective-permute-start.5) | collective-permute-done | bytes 131104 | tf_op jit(solution)/shard_map/ppermute | solution.py:21
  37.4 0.5 %collective-permute-start.11 = (bf16[64,2048]{1,0:T(8,128)(2,1)S(1)}, bf16[64,2048]{1,0:T(8,128)(2,1)S(1)}, u32[]{:S(2)}, u32[]{:S(2)}) collective-permute-start(bf16[64,2048]{1,0:T(8,128)(2,1)S(1)} %get-tuple-element.7), channel_id=1, source_target_pairs={{0,16},{16,0},{1,17},{17,1},{2,18},{18,2},{3,19},{19,3},{4,20},{20... | collective-permute-start | bytes 786440 | tf_op jit(solution)/shard_map/ppermute | solution.py:21
  38.0 1.4 %collective-permute-done.6 = bf16[16,4096]{1,0:T(8,128)(2,1)S(1)} collective-permute-done((bf16[16,4096]{1,0:T(8,128)(2,1)S(1)}, bf16[16,4096]{1,0:T(8,128)(2,1)S(1)}, u32[]{:S(2)}, u32[]{:S(2)}) %collective-permute-start.6) | collective-permute-done | bytes 131104 | tf_op jit(solution)/shard_map/ppermute | solution.py:21
  39.3 0.1 add_convert_fusion
  39.4 0.5 %collective-permute-start.7 = (bf16[16,4096]{1,0:T(8,128)(2,1)S(1)}, bf16[16,4096]{1,0:T(8,128)(2,1)S(1)}, u32[]{:S(2)}, u32[]{:S(2)}) collective-permute-start(bf16[16,4096]{1,0:T(8,128)(2,1)S(1)} %add_convert_fusion), channel_id=1, source_target_pairs={{0,12},{4,0},{8,4},{12,8},{1,13},{5,1},{9,5},{13,9},{2,14},{6,2},{... | collective-permute-start | bytes 393224 | tf_op jit(solution)/shard_map/ppermute | solution.py:26
  39.9 0.0 collective-permute-done.9
  40.0 0.0 collective-permute-done.10
  40.0 0.6 %fusion.15 = bf16[1,384,2048]{2,1,0:T(8,128)(2,1)S(1)} fusion(bf16[64,2048]{1,0:T(8,128)(2,1)S(1)} %collective-permute-done.10, bf16[64,2048]{1,0:T(8,128)(2,1)S(1)} %get-tuple-element.4, bf16[128,1152]{1,0:T(8,128)(2,1)S(1)} %pad_maximum_fusion.5), kind=kOutput, calls=%fused_computation.21 | convolution fusion | flops 203161600 | bytes 2195456 | tf_op jit(solution)/shard_map/dot_general | solution.py:109
  40.6 0.6 %fusion.16 = bf16[1,384,2048]{2,1,0:T(8,128)(2,1)S(1)} fusion(bf16[64,2048]{1,0:T(8,128)(2,1)S(1)} %collective-permute-done.10, bf16[64,2048]{1,0:T(8,128)(2,1)S(1)} %get-tuple-element.4, bf16[128,1152]{1,0:T(8,128)(2,1)S(1)} %pad_maximum_fusion.5), kind=kOutput, calls=%fused_computation.22 | convolution fusion | flops 203161600 | bytes 2195456 | tf_op jit(solution)/shard_map/dot_general | solution.py:109
  41.2 3.7 %collective-permute-done.11 = bf16[64,2048]{1,0:T(8,128)(2,1)S(1)} collective-permute-done((bf16[64,2048]{1,0:T(8,128)(2,1)S(1)}, bf16[64,2048]{1,0:T(8,128)(2,1)S(1)}, u32[]{:S(2)}, u32[]{:S(2)}) %collective-permute-start.11) | collective-permute-done | bytes 262176 | tf_op jit(solution)/shard_map/ppermute | solution.py:21
  44.9 0.6 %fusion.17 = bf16[1,384,2048]{2,1,0:T(8,128)(2,1)S(1)} fusion(bf16[64,2048]{1,0:T(8,128)(2,1)S(1)} %collective-permute-done.11, bf16[64,2048]{1,0:T(8,128)(2,1)S(1)} %get-tuple-element.6, bf16[128,1152]{1,0:T(8,128)(2,1)S(1)} %pad_maximum_fusion.5), kind=kOutput, calls=%fused_computation.23 | convolution fusion | flops 203161600 | bytes 2195456 | tf_op jit(solution)/shard_map/dot_general | solution.py:109
  45.4 2.5 %maximum_bitcast_fusion = bf16[1,3,384,2048]{3,2,1,0:T(8,128)(2,1)} fusion(bf16[1,384,2048]{2,1,0:T(8,128)(2,1)S(1)} %fusion.17, bf16[1,384,2048]{2,1,0:T(8,128)(2,1)S(1)} %fusion.16, bf16[1,384,2048]{2,1,0:T(8,128)(2,1)S(1)} %fusion.15), kind=kLoop, calls=%fused_computation.1 | loop fusion | flops 4718592 | bytes 9437184 | tf_op jit(solution)/shard_map/broadcast_in_dim | solution.py:107
  47.9 0.3 collective-permute-done.7
  48.2 0.0 collective-permute-done.8
  48.2 1.5 %select_bitcast_fusion = bf16[1,1,128,4096]{3,2,1,0:T(8,128)(2,1)} fusion(bf16[128,4096]{1,0:T(8,128)(2,1)S(1)} %collective-permute-done.8, pred[128]{0:T(512)(128)(4,1)S(1)} %compare_reduce_fusion, bf16[16,4096]{1,0:T(8,128)(2,1)S(1)} %collective-permute-done.7, s32[128]{0:T(128)S(1)} %convert_subtract_fusion.1), kind=kOutput, calls=%fused_computation.24 | convolution fusion | flops 17829888 | bytes 2228864 | tf_op jit(solution)/shard_map/dot_general | solution.py:122
  (14 shorter events, 0.2 us)
Async XLA Ops:
  0.6 9.0 %copy-start.1 = (s32[1,1,128,8]{2,3,1,0:T(8,128)S(1)}, s32[1,1,128,8]{2,3,1,0:T(8,128)}, u32[]{:S(2)}) copy-start(s32[1,1,128,8]{2,3,1,0:T(8,128)} %param.7) | copy-start | bytes 12292
  3.4 18.0 %collective-permute-start.1 = (bf16[16,4096]{1,0:T(8,128)(2,1)S(1)}, bf16[16,4096]{1,0:T(8,128)(2,1)S(1)}, u32[]{:S(2)}, u32[]{:S(2)}) collective-permute-start(bf16[16,4096]{1,0:T(8,128)(2,1)S(1)} %get-tuple-element.18), channel_id=1, source_target_pairs={{0,1},{1,0},{2,3},{3,2},{4,5},{5,4},{6,7},{7,6},{8,9},{9,8},{10,11... | collective-permute-start | bytes 393224 | tf_op jit(solution)/shard_map/ppermute | solution.py:21
  4.0 17.5 %collective-permute-start.2 = (bf16[16,4096]{1,0:T(8,128)(2,1)S(1)}, bf16[16,4096]{1,0:T(8,128)(2,1)}, u32[]{:S(2)}, u32[]{:S(2)}) collective-permute-start(bf16[16,4096]{1,0:T(8,128)(2,1)S(1)} %get-tuple-element.18), channel_id=1, source_target_pairs={{0,2},{1,3},{2,0},{3,1},{4,6},{5,7},{6,4},{7,5},{8,10},{9,11},{10,... | collective-permute-start | bytes 393224 | tf_op jit(solution)/shard_map/ppermute | solution.py:21
  6.6 14.9 %collective-permute-start.3 = (bf16[16,4096]{1,0:T(8,128)(2,1)S(1)}, bf16[16,4096]{1,0:T(8,128)(2,1)}, u32[]{:S(2)}, u32[]{:S(2)}) collective-permute-start(bf16[16,4096]{1,0:T(8,128)(2,1)S(1)} %get-tuple-element.18), channel_id=1, source_target_pairs={{0,3},{1,2},{2,1},{3,0},{4,7},{5,6},{6,5},{7,4},{8,11},{9,10},{10,... | collective-permute-start | bytes 393224 | tf_op jit(solution)/shard_map/ppermute | solution.py:21
  7.9 32.1 %collective-permute-start.10 = (bf16[64,2048]{1,0:T(8,128)(2,1)S(1)}, bf16[64,2048]{1,0:T(8,128)(2,1)S(1)}, u32[]{:S(2)}, u32[]{:S(2)}) collective-permute-start(bf16[64,2048]{1,0:T(8,128)(2,1)S(1)} %get-tuple-element.5), channel_id=1, source_target_pairs={{0,16},{16,0},{1,17},{17,1},{2,18},{18,2},{3,19},{19,3},{4,20},{20... | collective-permute-start | bytes 786440 | tf_op jit(solution)/shard_map/ppermute | solution.py:21
  9.6 11.0 %collective-permute-start = (s32[128,8]{0,1:T(8,128)S(1)}, s32[128,8]{0,1:T(8,128)S(1)}, u32[]{:S(2)}, u32[]{:S(2)}) collective-permute-start(s32[128,8]{0,1:T(8,128)S(1)} %bitcast.53), channel_id=1, source_target_pairs={{0,12},{4,0},{8,4},{12,8},{1,13},{5,1},{9,5},{13,9},{2,14},{6,2},{... | collective-permute-start | bytes 12296 | tf_op jit(solution)/shard_map/ppermute | solution.py:26
  16.9 3.7 %copy-start = (bf16[1,1,128,4096]{3,2,1,0:T(8,128)(2,1)S(1)}, bf16[1,1,128,4096]{3,2,1,0:T(8,128)(2,1)}, u32[]{:S(2)}) copy-start(bf16[1,1,128,4096]{3,2,1,0:T(8,128)(2,1)} %param.5) | copy-start | bytes 3145732
  20.6 27.7 %collective-permute-start.8 = (bf16[128,4096]{1,0:T(8,128)(2,1)S(1)}, bf16[128,4096]{1,0:T(8,128)(2,1)S(1)}, u32[]{:S(2)}, u32[]{:S(2)}) collective-permute-start(bf16[128,4096]{1,0:T(8,128)(2,1)S(1)} %bitcast.52), channel_id=1, source_target_pairs={{0,12},{4,0},{8,4},{12,8},{1,13},{5,1},{9,5},{13,9},{2,14},{6,2},{... | collective-permute-start | bytes 3145736 | tf_op jit(solution)/shard_map/ppermute | solution.py:26
  31.0 2.0 %collective-permute-start.4 = (bf16[16,4096]{1,0:T(8,128)(2,1)S(1)}, bf16[16,4096]{1,0:T(8,128)(2,1)S(1)}, u32[]{:S(2)}, u32[]{:S(2)}) collective-permute-start(bf16[16,4096]{1,0:T(8,128)(2,1)S(1)} %get-tuple-element.8), channel_id=1, source_target_pairs={{0,1},{1,0},{2,3},{3,2},{4,5},{5,4},{6,7},{7,6},{8,9},{9,8},{10,11... | collective-permute-start | bytes 393224 | tf_op jit(solution)/shard_map/ppermute | solution.py:21
  31.1 6.4 %collective-permute-start.5 = (bf16[16,4096]{1,0:T(8,128)(2,1)S(1)}, bf16[16,4096]{1,0:T(8,128)(2,1)S(1)}, u32[]{:S(2)}, u32[]{:S(2)}) collective-permute-start(bf16[16,4096]{1,0:T(8,128)(2,1)S(1)} %get-tuple-element.10), channel_id=1, source_target_pairs={{0,2},{1,3},{2,0},{3,1},{4,6},{5,7},{6,4},{7,5},{8,10},{9,11},{10,... | collective-permute-start | bytes 393224 | tf_op jit(solution)/shard_map/ppermute | solution.py:21
  32.7 6.7 %collective-permute-start.6 = (bf16[16,4096]{1,0:T(8,128)(2,1)S(1)}, bf16[16,4096]{1,0:T(8,128)(2,1)S(1)}, u32[]{:S(2)}, u32[]{:S(2)}) collective-permute-start(bf16[16,4096]{1,0:T(8,128)(2,1)S(1)} %get-tuple-element.9), channel_id=1, source_target_pairs={{0,3},{1,2},{2,1},{3,0},{4,7},{5,6},{6,5},{7,4},{8,11},{9,10},{10,... | collective-permute-start | bytes 393224 | tf_op jit(solution)/shard_map/ppermute | solution.py:21
  33.0 7.0 %collective-permute-start.9 = (bf16[64,1152]{1,0:T(8,128)(2,1)S(1)}, bf16[64,1152]{1,0:T(8,128)(2,1)S(1)}, u32[]{:S(2)}, u32[]{:S(2)}) collective-permute-start(bf16[64,1152]{1,0:T(8,128)(2,1)S(1)} %pad_maximum_fusion.6), channel_id=1, source_target_pairs={{0,16},{16,0},{1,17},{17,1},{2,18},{18,2},{3,19},{19,3},{4,20},{20... | collective-permute-start | bytes 442376 | tf_op jit(solution)/shard_map/ppermute | solution.py:21
  37.4 7.4 %collective-permute-start.11 = (bf16[64,2048]{1,0:T(8,128)(2,1)S(1)}, bf16[64,2048]{1,0:T(8,128)(2,1)S(1)}, u32[]{:S(2)}, u32[]{:S(2)}) collective-permute-start(bf16[64,2048]{1,0:T(8,128)(2,1)S(1)} %get-tuple-element.7), channel_id=1, source_target_pairs={{0,16},{16,0},{1,17},{17,1},{2,18},{18,2},{3,19},{19,3},{4,20},{20... | collective-permute-start | bytes 786440 | tf_op jit(solution)/shard_map/ppermute | solution.py:21
  39.4 8.8 %collective-permute-start.7 = (bf16[16,4096]{1,0:T(8,128)(2,1)S(1)}, bf16[16,4096]{1,0:T(8,128)(2,1)S(1)}, u32[]{:S(2)}, u32[]{:S(2)}) collective-permute-start(bf16[16,4096]{1,0:T(8,128)(2,1)S(1)} %add_convert_fusion), channel_id=1, source_target_pairs={{0,12},{4,0},{8,4},{12,8},{1,13},{5,1},{9,5},{13,9},{2,14},{6,2},{... | collective-permute-start | bytes 393224 | tf_op jit(solution)/shard_map/ppermute | solution.py:26

commit v2 on v1

v2 whole, which is shorter than its diff:
```python
import functools

import jax
import jax.numpy as jnp
from jax import lax
from jax.experimental import pallas as pl
from jax.experimental.pallas import tpu as pltpu
from jax.sharding import PartitionSpec as P

BF16 = jnp.bfloat16
F32 = jnp.float32
LANES = 128
VMEM_LIMIT = 20 * 2**20
LAST_LAST = (((1,), (1,)), ((), ()))
FIRST_FIRST = (((0,), (0,)), ((), ()))
ROWS_COLS = (((1,), (0,)), ((), ()))


def partner(index, step, count):
    if count & (count - 1) == 0:
        return index ^ step
    return (index + step) % count


def origin(index, step, count):
    if count & (count - 1) == 0:
        return index ^ step
    return (index - step) % count


def exchange(value, axis, step):
    count = lax.axis_size(axis)
    return lax.ppermute(value, axis, [(i, partner(i, step, count)) for i in range(count)])


def to_previous(value):
    count = lax.axis_size("pipe")
    return lax.ppermute(value, "pipe", [(i, (i - 1) % count) for i in range(count)])


def mm(left, right, dims):
    return lax.dot_general(left, right, dims, preferred_element_type=F32)


def run(body, name, outs, inputs, flops, scalars=0, grid=None, in_specs=None, out_specs=None):
    vmem = pl.BlockSpec(memory_space=pltpu.VMEM)
    smem = pl.BlockSpec(memory_space=pltpu.SMEM)
    moved = sum(v.size * v.dtype.itemsize for v in (*inputs, *outs))
    extra = {} if grid is None else {"grid": grid}
    return pl.pallas_call(
        body,
        name=name,
        out_shape=outs,
        in_specs=in_specs or [smem] * scalars + [vmem] * (len(inputs) - scalars),
        out_specs=out_specs or [vmem] * len(outs),
        compiler_params=pltpu.CompilerParams(vmem_limit_bytes=VMEM_LIMIT),
        cost_estimate=pl.CostEstimate(flops=flops, bytes_accessed=moved, transcendentals=0),
        **extra,
    )(*inputs)


def route_body(routing_ref, gates_ref, incoming_ref, routed_ref, picked_ref, ids_ref):
    capacity = routed_ref.shape[0]
    tokens = incoming_ref.shape[0]
    matches = routing_ref[...] == 0
    member = jnp.max(jnp.where(matches, F32(1.0), F32(0.0)), axis=0, keepdims=True)
    share = jnp.sum(jnp.where(matches, gates_ref[...], F32(0.0)), axis=0, keepdims=True)
    earlier = lax.broadcasted_iota(jnp.int32, (tokens, tokens), 0) < lax.broadcasted_iota(
        jnp.int32, (tokens, tokens), 1
    )
    spread = jnp.broadcast_to(member, (capacity, tokens))
    slot = mm(spread.astype(BF16), jnp.where(earlier, F32(1.0), F32(0.0)).astype(BF16), ROWS_COLS)
    wanted = lax.broadcasted_iota(jnp.int32, (capacity, tokens), 0).astype(F32)
    chosen = jnp.where((slot == wanted) & (spread > 0.5), F32(1.0), F32(0.0))
    weighting = jnp.sum(chosen * share, axis=1, keepdims=True)
    picked = mm(chosen.astype(BF16), incoming_ref[...], ROWS_COLS)
    routed_ref[...] = (picked * weighting).astype(BF16)
    picked_ref[...] = picked.astype(BF16)
    token = lax.broadcasted_iota(jnp.int32, (capacity, tokens), 1)
    filled = jnp.sum(chosen, axis=1, keepdims=True)
    high = jnp.sum(chosen * (token // LANES).astype(F32), axis=1, keepdims=True)
    low = jnp.sum(chosen * (token % LANES).astype(F32), axis=1, keepdims=True)
    high = jnp.where(filled > 0.5, high, F32(-1.0))
    lane = lax.broadcasted_iota(jnp.int32, (capacity, LANES), 1)
    ids_ref[...] = jnp.where(lane == 0, high, jnp.where(lane == 1, low, F32(0.0))).astype(BF16)


def forward_body(order, others, who_ref, inputs_ref, weights_ref, *outs):
    slope_ref, active_ref, hidden_ref, own_ref = outs[:4]
    part = own_ref.shape[1]
    rows = jnp.concatenate([inputs_ref[who_ref[k]] for k in range(order)], axis=0)
    gate_pre = mm(weights_ref[0], rows, LAST_LAST)
    up_pre = mm(weights_ref[1], rows, LAST_LAST)
    sigmoid_gate = jax.nn.sigmoid(gate_pre)
    activated = gate_pre * sigmoid_gate
    slope_ref[...] = up_pre * sigmoid_gate * (1.0 + gate_pre * (1.0 - sigmoid_gate))
    active_ref[...] = activated
    hidden = jnp.transpose(activated * up_pre).astype(BF16)
    hidden_ref[...] = hidden
    capacity = inputs_ref.shape[1]
    for r in range(others + 1):
        first = pl.multiple_of(who_ref[order + r], LANES)
        into = own_ref if r == 0 else outs[3 + r]
        for k in range(order):
            into[k * capacity : (k + 1) * capacity, :part] = inputs_ref[who_ref[k], :, pl.ds(first, part)]
        if r:
            into[:, part:] = hidden


def backward_body(order, others, who_ref, *refs):
    blocks = refs[:order]
    weights_ref, slope_ref, active_ref = refs[order : order + 3]
    outs = refs[order + 3 :]
    partials, grads_ref, own_ref, fars = outs[:order], outs[order], outs[order + 1], outs[order + 2 :]
    part = own_ref.shape[1]
    rows = jnp.concatenate([b[...] for b in blocks], axis=0)
    hidden_grad = mm(weights_ref[2], rows, LAST_LAST)
    gate_grad = jnp.transpose(hidden_grad * slope_ref[...]).astype(BF16)
    up_grad = jnp.transpose(hidden_grad * active_ref[...]).astype(BF16)
    grads = jnp.concatenate([gate_grad, up_grad], axis=1)
    grads_ref[...] = grads
    hid = weights_ref.shape[1]
    capacity = blocks[0].shape[0]
    width = blocks[0].shape[1]
    step = 512
    for c in range(width // step):
        at = slice(c * step, (c + 1) * step)
        total = mm(gate_grad, weights_ref[0, :, at], ROWS_COLS) + mm(up_grad, weights_ref[1, :, at], ROWS_COLS)
        for k in range(order):
            partials[k][:, at] = total[k * capacity : (k + 1) * capacity].astype(BF16)
    for r in range(others + 1):
        first = pl.multiple_of(who_ref[r], LANES)
        into = own_ref if r == 0 else fars[r - 1]
        for k in range(order):
            into[k * capacity : (k + 1) * capacity, :part] = blocks[k][:, pl.ds(first, part)]
        if r:
            into[:, part:] = grads


def return_body(order, *refs):
    picked_ref, ids_ref, out_ref = refs[0], refs[1], refs[-1]
    width = picked_ref.shape[1]
    total = picked_ref[...].astype(F32)
    back = refs[2][...].astype(F32)
    for ref in refs[3 : 2 + order]:
        back = back + ref[...].astype(F32)
    out_ref[:, :width] = (total + back).astype(BF16)
    out_ref[:, width:] = ids_ref[...]


def weight_body(others, hidden_ref, grads_ref, inputs_ref, rows_ref, *refs):
    fars_in, fars_out, out_ref = refs[:others], refs[others : 2 * others], refs[2 * others]
    part = inputs_ref.shape[1]
    hid = hidden_ref.shape[1]
    kind = pl.program_id(0)

    def product(lefts, rights):
        left = jnp.concatenate(lefts, axis=0)
        right = jnp.concatenate(rights, axis=0)
        out_ref[0, 0] = mm(left, right, FIRST_FIRST).astype(BF16)

    for i in range(2):

        @pl.when(kind == i)
        def _(i=i):
            product(
                [grads_ref[:, i * hid : (i + 1) * hid]]
                + [f[:, part + i * hid : part + (i + 1) * hid] for f in fars_out],
                [inputs_ref[...]] + [f[:, :part] for f in fars_in],
            )

    @pl.when(kind == 2)
    def _():
        product(
            [hidden_ref[...]] + [f[:, part:] for f in fars_in],
            [rows_ref[...]] + [f[:, :part] for f in fars_out],
        )


def merge_body(shifted_ref, changed_ref, out_ref):
    tokens, width = shifted_ref.shape
    capacity = changed_ref.shape[0]
    high = changed_ref[:, width : width + 1].astype(F32)
    low = changed_ref[:, width + 1 : width + 2].astype(F32)
    token = lax.broadcasted_iota(jnp.int32, (capacity, tokens), 1).astype(F32)
    chosen = jnp.where(token == high * F32(LANES) + low, F32(1.0), F32(0.0)).astype(BF16)
    here = mm(chosen, jnp.ones((capacity, LANES), BF16), FIRST_FIRST)[:, :1] > 0.5
    step = 1024
    for c in range(width // step):
        at = slice(c * step, (c + 1) * step)
        placed = mm(chosen, changed_ref[:, at], FIRST_FIRST)
        out_ref[0, 0, :, at] = jnp.where(here, placed, shifted_ref[:, at].astype(F32)).astype(BF16)


def shards(output_grads, gate_values, routing, saved_inputs, expert_weights):
    owners = lax.axis_size("expert")
    replicas = lax.axis_size("dp")
    others = replicas - 1
    capacity = saved_inputs.shape[4]
    incoming = output_grads[0, 0]
    tokens, width = incoming.shape
    part = width // replicas
    weights = expert_weights[0]
    hid = weights.shape[1]
    rows = owners * capacity
    me = lax.axis_index("expert")
    replica = lax.axis_index("dp")
    out = jax.ShapeDtypeStruct

    shifted = to_previous(incoming)

    routed, picked, ids = run(
        route_body,
        "route",
        [out((capacity, width), BF16), out((capacity, width), BF16), out((capacity, LANES), BF16)],
        [jnp.transpose(routing[0, 0]), jnp.transpose(gate_values[0, 0]), incoming],
        2 * capacity * tokens * width,
    )
    arrived = [exchange(routed, "expert", k) for k in reversed(range(1, owners))][::-1]

    sources = jnp.stack([origin(me, k, owners) for k in range(owners)]).astype(jnp.int32)
    columns = jnp.stack([partner(replica, k, replicas) * part for k in range(replicas)]).astype(jnp.int32)
    far_in = out((rows, part + hid), BF16)
    slope, active, hidden, own_inputs, *fars = run(
        functools.partial(forward_body, owners, others),
        "forward",
        [out((hid, rows), F32), out((hid, rows), F32), out((rows, hid), BF16), out((rows, part), BF16)]
        + [far_in] * others,
        [jnp.concatenate([sources, columns]), saved_inputs[0, 0, 0], weights],
        4 * rows * hid * width,
        scalars=1,
    )
    far_inputs = [exchange(f, "dp", k + 1) for k, f in enumerate(fars)]

    results = run(
        functools.partial(backward_body, owners, others),
        "backward",
        [out((capacity, width), BF16)] * owners
        + [out((rows, 2 * hid), BF16), out((rows, part), BF16)]
        + [out((rows, part + 2 * hid), BF16)] * others,
        [columns, routed, *arrived, weights, slope, active],
        6 * rows * hid * width,
        scalars=1,
    )
    partials, grads, own_rows, fars = (
        results[:owners],
        results[owners],
        results[owners + 1],
        results[owners + 2 :],
    )
    returned = [exchange(partials[k], "expert", k) for k in reversed(range(1, owners))][::-1]
    far_rows = [exchange(f, "dp", k + 1) for k, f in enumerate(fars)]

    changed = run(
        functools.partial(return_body, owners),
        "sum_returned",
        [out((capacity, width + LANES), BF16)],
        [picked, ids, partials[0], *returned],
        0,
    )[0]
    next_changed = to_previous(changed)

    whole = lambda v: pl.BlockSpec(v.shape, lambda i: (0,) * len(v.shape))
    operands = [hidden, grads, own_inputs, own_rows, *far_inputs, *far_rows]
    weight_grads = run(
        functools.partial(weight_body, others),
        "weight_grads",
        [out((1, 3, hid, part), BF16)],
        operands,
        6 * rows * replicas * hid * part,
        grid=(3,),
        in_specs=[whole(v) for v in operands],
        out_specs=[pl.BlockSpec((1, 1, hid, part), lambda i: (0, i, 0, 0))],
    )[0]

    passed_grads = run(
        merge_body,
        "merge",
        [out((1, 1, tokens, width), BF16)],
        [shifted, next_changed],
        2 * capacity * tokens * width,
    )[0]
    return (passed_grads, weight_grads)


def solution(mesh):
    placed = (
        P("dp", "pipe", "expert", None),
        P("dp", "pipe", "expert", None),
        P("dp", "pipe", "expert", None),
        P("dp", "pipe", None, None, None, None),
        P("pipe", None, "expert", None),
    )
    return jax.shard_map(
        shards,
        mesh=mesh,
        in_specs=placed,
        out_specs=(P("dp", "pipe", "expert", None), P("pipe", None, "expert", "dp")),
        check_vma=False,
    )
```

time: 50 us -> 46.1 us (0.922)
  matrix products: 20.4 us -> 0 us
  Pallas kernels: 0 us -> 12 us
  local copies, waits for them, and re-layouts: 1.49 us -> 8.65 us
  other arithmetic: 5.12 us -> 0.08 us
  waiting for transfers between devices: 9.29 us -> 12.6 us
  starting transfers between devices: 12.5 us -> 11.7 us
    dot_general x10 -> x0, matrix products: 20.4 us -> none  [the longest x1 3.72 us: shards(): lax.dot_general(own_inputs, up_weight, contract, preferred_element_type=j...]
    pallas_call x0 -> x6, Pallas kernels: none -> 12 us  [run(): pl.pallas_call(body, name=name, out_shape=outs, in_specs=in_specs or [sme...]
    unnamed x4 -> x12, local copies, waits for them, and re-layouts: 0.01 us -> 8.57 us
    ppermute x9 -> x8, waiting for transfers between devices: 8.96 us -> 12.6 us  [exchange(): lax.ppermute(value, axis, [(i, partner(i, step, count)) for i in range(co...]
    broadcast_in_dim x1 -> x0, other arithmetic: 2.46 us -> none  [shards(): jnp.stack([lax.dot_general(factors_all[:, i * hid:(i + 1) * hid], rows_al...]
    ppermute x9 -> x8, starting transfers between devices: 8 us -> 6.1 us  [exchange(): lax.ppermute(value, axis, [(i, partner(i, step, count)) for i in range(co...]
    squeeze x1 -> x0, local copies, waits for them, and re-layouts: 1.13 us -> none  [shards(): lax.dynamic_index_in_dim(saved, origin(me, k, owners), 0, keepdims=False)]
    concatenate x4 -> x0, other arithmetic: 1.08 us -> none  [the longest x1 1 us: shards(): routed_rows = jnp.concatenate(arrived)]
  transfers between devices with their start and end apart: 12 -> 10, of which waited for: 4 -> 3; matrix products, arithmetic and copies ran while one was open for 46% -> 0% of each run, Pallas kernels for 0% -> 23%
where the time goes in v2:
time: 46.1 us; the launch traced here: 45.8 us
  waiting for transfers between devices  12.6 us (27%)
  Pallas kernels  12 us (26%)
  starting transfers between devices  11.7 us (25%)
  local copies, waits for them, and re-layouts  8.65 us (19%)
  between operations  0.67 us (1%)
    ppermute x8, waiting for transfers between devices, exchange(): lax.ppermute(value, axis, [(i, partner(i, step, count)) for i in range(co...  12.6 us
    pallas_call x6, Pallas kernels, run(): pl.pallas_call(body, name=name, out_shape=outs, in_specs=in_specs or [sme...  12 us
    unnamed x12, local copies, waits for them, and re-layouts  8.57 us
    ppermute x8, starting transfers between devices, exchange(): lax.ppermute(value, axis, [(i, partner(i, step, count)) for i in range(co...  6.1 us
    ppermute x2, starting transfers between devices, to_previous(): lax.ppermute(value, 'pipe', [(i, (i - 1) % count) for i in range(count)])  5.6 us
  transfers between devices with their start and end apart: 10, of which 3 were waited for; matrix products, arithmetic and copies ran while one was open for 0% of the time, Pallas kernels for 23%

profile of v2, /device:TPU:0, one launch (start us, length us, event | category | flops | bytes accessed | tf_op | source)
XLA Modules:
  0.0 45.8 jit_solution(15175327313501482559)
XLA Ops:
  0.6 5.1 %collective-permute-start = (bf16[128,4096]{1,0:T(8,128)(2,1)}, bf16[128,4096]{1,0:T(8,128)(2,1)S(1)}, u32[]{:S(2)}, u32[]{:S(2)}) collective-permute-start(bf16[128,4096]{1,0:T(8,128)(2,1)} %bitcast.17), channel_id=1, source_target_pairs={{0,12},{4,0},{8,4},{12,8},{1,13},{5,1},{9,5},{13,9},{2,14},{6,2},{... | collective-permute-start | bytes 3145736 | tf_op jit(solution)/shard_map/ppermute | solution.py:38
  5.7 0.0 copy-start.2
  5.7 1.3 %copy-done.2 = bf16[1,1,128,4096]{3,2,1,0:T(8,128)(2,1)S(1)} copy-done((bf16[1,1,128,4096]{3,2,1,0:T(8,128)(2,1)S(1)}, bf16[1,1,128,4096]{3,2,1,0:T(8,128)(2,1)}, u32[]{:S(2)}) %copy-start.2) | copy-done | bytes 1048600
  7.0 0.0 copy-start.4
  7.0 0.7 %copy-done.4 = s32[1,1,128,8]{2,3,1,0:T(8,128)S(1)} copy-done((s32[1,1,128,8]{2,3,1,0:T(8,128)S(1)}, s32[1,1,128,8]{2,3,1,0:T(8,128)}, u32[]{:S(2)}) %copy-start.4) | copy-done | bytes 4120
  7.7 0.0 copy-start.5
  7.7 0.7 %copy-done.5 = f32[1,1,128,8]{2,3,1,0:T(8,128)S(1)} copy-done((f32[1,1,128,8]{2,3,1,0:T(8,128)S(1)}, f32[1,1,128,8]{2,3,1,0:T(8,128)}, u32[]{:S(2)}) %copy-start.5) | copy-done | bytes 4120
  8.4 0.4 route.1
  8.7 0.1 collective-permute-start.1
  8.8 1.6 %collective-permute-start.2 = (bf16[16,4096]{1,0:T(8,128)(2,1)S(1)}, bf16[16,4096]{1,0:T(8,128)(2,1)S(1)}, u32[]{:S(2)}, u32[]{:S(2)}) collective-permute-start(bf16[16,4096]{1,0:T(8,128)(2,1)S(1)} %get-tuple-element.19.refs_0_), channel_id=1, source_target_pairs={{0,2},{1,3},{2,0},{3,1},{4,6},{5,7},{6,4},{7,5},{8,10},{9,11},{10,... | collective-permute-start | bytes 393224 | tf_op jit(solution)/shard_map/ppermute | solution.py:33
  10.4 0.3 collective-permute-start.3
  10.7 0.1 concatenate.4.who_ref
  10.8 0.0 copy-start
  10.8 3.7 %copy-done = bf16[1,3,384,4096]{3,2,1,0:T(8,128)(2,1)S(1)} copy-done((bf16[1,3,384,4096]{3,2,1,0:T(8,128)(2,1)S(1)}, bf16[1,3,384,4096]{3,2,1,0:T(8,128)(2,1)}, u32[]{:S(2)}) %copy-start) | copy-done | bytes 9437208
  14.4 0.0 copy-start.3
  14.4 1.0 %copy-done.3 = bf16[1,1,1,4,16,4096]{5,4,3,2,1,0:T(8,128)(2,1)S(1)} copy-done((bf16[1,1,1,4,16,4096]{5,4,3,2,1,0:T(8,128)(2,1)S(1)}, bf16[1,1,1,4,16,4096]{5,4,3,2,1,0:T(8,128)(2,1)}, u32[]{:S(2)}) %copy-start.3) | copy-done | bytes 524312
  15.5 0.0 copy-start.1
  15.5 2.4 %forward.1 = (f32[384,64]{1,0:T(8,128)S(1)}, f32[384,64]{1,0:T(8,128)S(1)}, bf16[64,384]{1,0:T(8,128)(2,1)S(1)}, bf16[64,2048]{1,0:T(8,128)(2,1)S(1)}, bf16[64,2432]{1,0:T(8,128)(2,1)S(1)}) custom-call(s32[6]{0:T(128)S(1)} %concatenate.4.who_ref, bf16[4,16,4096]{2,1,0:T(8,128)(2,1)S(1)} %bitcast.19, bf16[3,384,4096]{2,1,0:T(8,128)(2,1)S(1)} %bitcast.15), custom_call_target="tpu_custom_call" | custom-call | flops 402653184 | bytes 10780696 | tf_op jit(solution)/shard_map/forward/pallas_call | solution.py:50
  17.8 0.1 pad_add_fusion.who_ref
  17.9 0.0 collective-permute-done.1.refs_1_
  17.9 0.0 collective-permute-done.2.refs_2_
  17.9 0.0 collective-permute-done.3.refs_3_
  17.9 1.2 %copy-done.1 = bf16[1,3,384,4096]{3,2,1,0:T(8,128)(2,1)S(1)} copy-done((bf16[1,3,384,4096]{3,2,1,0:T(8,128)(2,1)S(1)}, bf16[1,3,384,4096]{3,2,1,0:T(8,128)(2,1)}, u32[]{:S(2)}) %copy-start.1) | copy-done | bytes 9437208
  19.2 4.1 %backward.1 = (bf16[16,4096]{1,0:T(8,128)(2,1)S(1)}, bf16[16,4096]{1,0:T(8,128)(2,1)S(1)}, bf16[16,4096]{1,0:T(8,128)(2,1)S(1)}, bf16[16,4096]{1,0:T(8,128)(2,1)...) custom-call(s32[2]{0:T(128)S(1)} %pad_add_fusion.who_ref, ...), custom_call_target="tpu_custom_call" | custom-call | flops 603979776 | bytes 11403272 | tf_op jit(solution)/shard_map/backward/pallas_call | solution.py:50
  23.3 1.6 %collective-permute-start.9 = (bf16[64,2816]{1,0:T(8,128)(2,1)S(1)}, bf16[64,2816]{1,0:T(8,128)(2,1)S(1)}, u32[]{:S(2)}, u32[]{:S(2)}) collective-permute-start(bf16[64,2816]{1,0:T(8,128)(2,1)S(1)} %get-tuple-element.31), channel_id=1, source_target_pairs={{0,16},{16,0},{1,17},{17,1},{2,18},{18,2},{3,19},{19,3},{4,20},{20... | collective-permute-start | bytes 1081352 | tf_op jit(solution)/shard_map/ppermute | solution.py:33
  24.9 0.1 collective-permute-start.4
  24.9 0.5 %collective-permute-start.8 = (bf16[64,2432]{1,0:T(8,128)(2,1)S(1)}, bf16[64,2432]{1,0:T(8,128)(2,1)S(1)}, u32[]{:S(2)}, u32[]{:S(2)}) collective-permute-start(bf16[64,2432]{1,0:T(8,128)(2,1)S(1)} %get-tuple-element.30), channel_id=1, source_target_pairs={{0,16},{16,0},{1,17},{17,1},{2,18},{18,2},{3,19},{19,3},{4,20},{20... | collective-permute-start | bytes 933896 | tf_op jit(solution)/shard_map/ppermute | solution.py:33
  25.5 1.5 %collective-permute-start.5 = (bf16[16,4096]{1,0:T(8,128)(2,1)S(1)}, bf16[16,4096]{1,0:T(8,128)(2,1)S(1)}, u32[]{:S(2)}, u32[]{:S(2)}) collective-permute-start(bf16[16,4096]{1,0:T(8,128)(2,1)S(1)} %get-tuple-element.24), channel_id=1, source_target_pairs={{0,2},{1,3},{2,0},{3,1},{4,6},{5,7},{6,4},{7,5},{8,10},{9,11},{10,... | collective-permute-start | bytes 393224 | tf_op jit(solution)/shard_map/ppermute | solution.py:33
  27.0 0.0 collective-permute-done.4.refs_3_
  27.0 0.5 %collective-permute-start.6 = (bf16[16,4096]{1,0:T(8,128)(2,1)S(1)}, bf16[16,4096]{1,0:T(8,128)(2,1)S(1)}, u32[]{:S(2)}, u32[]{:S(2)}) collective-permute-start(bf16[16,4096]{1,0:T(8,128)(2,1)S(1)} %get-tuple-element.25), channel_id=1, source_target_pairs={{0,3},{1,2},{2,1},{3,0},{4,7},{5,6},{6,5},{7,4},{8,11},{9,10},{10,... | collective-permute-start | bytes 393224 | tf_op jit(solution)/shard_map/ppermute | solution.py:33
  27.5 4.3 %collective-permute-done.5.refs_4_ = bf16[16,4096]{1,0:T(8,128)(2,1)S(1)} collective-permute-done((bf16[16,4096]{1,0:T(8,128)(2,1)S(1)}, bf16[16,4096]{1,0:T(8,128)(2,1)S(1)}, u32[]{:S(2)}, u32[]{:S(2)}) %collective-permute-start.5) | collective-permute-done | bytes 131104 | tf_op jit(solution)/shard_map/ppermute | solution.py:33
  31.8 1.3 %collective-permute-done.6.refs_5_ = bf16[16,4096]{1,0:T(8,128)(2,1)S(1)} collective-permute-done((bf16[16,4096]{1,0:T(8,128)(2,1)S(1)}, bf16[16,4096]{1,0:T(8,128)(2,1)S(1)}, u32[]{:S(2)}, u32[]{:S(2)}) %collective-permute-start.6) | collective-permute-done | bytes 131104 | tf_op jit(solution)/shard_map/ppermute | solution.py:33
  33.1 0.1 sum_returned.1
  33.1 0.5 %collective-permute-start.7 = (bf16[16,4224]{1,0:T(8,128)(2,1)S(1)}, bf16[16,4224]{1,0:T(8,128)(2,1)S(1)}, u32[]{:S(2)}, u32[]{:S(2)}) collective-permute-start(bf16[16,4224]{1,0:T(8,128)(2,1)S(1)} %sum_returned.1), channel_id=1, source_target_pairs={{0,12},{4,0},{8,4},{12,8},{1,13},{5,1},{9,5},{13,9},{2,14},{6,2},{... | collective-permute-start | bytes 405512 | tf_op jit(solution)/shard_map/ppermute | solution.py:38
  33.6 7.0 %collective-permute-done.8.refs_0_ = bf16[64,2432]{1,0:T(8,128)(2,1)S(1)} collective-permute-done((bf16[64,2432]{1,0:T(8,128)(2,1)S(1)}, bf16[64,2432]{1,0:T(8,128)(2,1)S(1)}, u32[]{:S(2)}, u32[]{:S(2)}) %collective-permute-start.8) | collective-permute-done | bytes 311328 | tf_op jit(solution)/shard_map/ppermute | solution.py:33
  40.7 0.0 collective-permute-done.9.refs_1_
  40.7 3.5 %weight_grads.1 = bf16[1,3,384,2048]{3,2,1,0:T(8,128)(2,1)} custom-call(bf16[64,384]{1,0:T(8,128)(2,1)S(1)} %get-tuple-element.26.hidden_ref, bf16[64,768]{1,0:T(8,128)(2,1)S(1)} %get-tuple-element.27.grads_ref, bf16[64,2048]{1,0:T(8,128)(2,1)S(1)} %get-tuple-element.28.inputs_ref, bf16[64,2048]{1,0:T(8,128)(2,1)S(1)} %get-tuple-element.29.rows_ref, ...), custom_call_target="tpu_custom_call" | custom-call | flops 603979776 | bytes 6062080 | tf_op jit(solution)/shard_map/weight_grads/pallas_call | solution.py:50
  44.2 0.0 collective-permute-done.7.changed_ref
  44.2 0.0 collective-permute-done.shifted_ref
  44.2 1.6 %merge.1 = bf16[1,1,128,4096]{3,2,1,0:T(8,128)(2,1)} custom-call(bf16[128,4096]{1,0:T(8,128)(2,1)S(1)} %collective-permute-done.shifted_ref, bf16[16,4224]{1,0:T(8,128)(2,1)S(1)} %collective-permute-done.7.changed_ref), custom_call_target="tpu_custom_call" | custom-call | flops 16777216 | bytes 2232320 | tf_op jit(solution)/shard_map/merge/pallas_call | solution.py:50
Async XLA Ops:
  0.6 43.6 %collective-permute-start = (bf16[128,4096]{1,0:T(8,128)(2,1)}, bf16[128,4096]{1,0:T(8,128)(2,1)S(1)}, u32[]{:S(2)}, u32[]{:S(2)}) collective-permute-start(bf16[128,4096]{1,0:T(8,128)(2,1)} %bitcast.17), channel_id=1, source_target_pairs={{0,12},{4,0},{8,4},{12,8},{1,13},{5,1},{9,5},{13,9},{2,14},{6,2},{... | collective-permute-start | bytes 3145736 | tf_op jit(solution)/shard_map/ppermute | solution.py:38
  5.7 1.3 %copy-start.2 = (bf16[1,1,128,4096]{3,2,1,0:T(8,128)(2,1)S(1)}, bf16[1,1,128,4096]{3,2,1,0:T(8,128)(2,1)}, u32[]{:S(2)}) copy-start(bf16[1,1,128,4096]{3,2,1,0:T(8,128)(2,1)} %param.5) | copy-start | bytes 3145732
  7.0 0.7 %copy-start.4 = (s32[1,1,128,8]{2,3,1,0:T(8,128)S(1)}, s32[1,1,128,8]{2,3,1,0:T(8,128)}, u32[]{:S(2)}) copy-start(s32[1,1,128,8]{2,3,1,0:T(8,128)} %param.7) | copy-start | bytes 12292
  7.7 0.7 %copy-start.5 = (f32[1,1,128,8]{2,3,1,0:T(8,128)S(1)}, f32[1,1,128,8]{2,3,1,0:T(8,128)}, u32[]{:S(2)}) copy-start(f32[1,1,128,8]{2,3,1,0:T(8,128)} %param.6) | copy-start | bytes 12292
  8.7 9.2 %collective-permute-start.1 = (bf16[16,4096]{1,0:T(8,128)(2,1)S(1)}, bf16[16,4096]{1,0:T(8,128)(2,1)S(1)}, u32[]{:S(2)}, u32[]{:S(2)}) collective-permute-start(bf16[16,4096]{1,0:T(8,128)(2,1)S(1)} %get-tuple-element.19.refs_0_), channel_id=1, source_target_pairs={{0,1},{1,0},{2,3},{3,2},{4,5},{5,4},{6,7},{7,6},{8,9},{9,8},{10,11... | collective-permute-start | bytes 393224 | tf_op jit(solution)/shard_map/ppermute | solution.py:33
  8.8 9.1 %collective-permute-start.2 = (bf16[16,4096]{1,0:T(8,128)(2,1)S(1)}, bf16[16,4096]{1,0:T(8,128)(2,1)S(1)}, u32[]{:S(2)}, u32[]{:S(2)}) collective-permute-start(bf16[16,4096]{1,0:T(8,128)(2,1)S(1)} %get-tuple-element.19.refs_0_), channel_id=1, source_target_pairs={{0,2},{1,3},{2,0},{3,1},{4,6},{5,7},{6,4},{7,5},{8,10},{9,11},{10,... | collective-permute-start | bytes 393224 | tf_op jit(solution)/shard_map/ppermute | solution.py:33
  10.4 7.5 %collective-permute-start.3 = (bf16[16,4096]{1,0:T(8,128)(2,1)S(1)}, bf16[16,4096]{1,0:T(8,128)(2,1)S(1)}, u32[]{:S(2)}, u32[]{:S(2)}) collective-permute-start(bf16[16,4096]{1,0:T(8,128)(2,1)S(1)} %get-tuple-element.19.refs_0_), channel_id=1, source_target_pairs={{0,3},{1,2},{2,1},{3,0},{4,7},{5,6},{6,5},{7,4},{8,11},{9,10},{10,... | collective-permute-start | bytes 393224 | tf_op jit(solution)/shard_map/ppermute | solution.py:33
  10.8 3.7 %copy-start = (bf16[1,3,384,4096]{3,2,1,0:T(8,128)(2,1)S(1)}, bf16[1,3,384,4096]{3,2,1,0:T(8,128)(2,1)}, u32[]{:S(2)}) copy-start(bf16[1,3,384,4096]{3,2,1,0:T(8,128)(2,1)} %param.9) | copy-start | bytes 28311556
  14.4 1.0 %copy-start.3 = (bf16[1,1,1,4,16,4096]{5,4,3,2,1,0:T(8,128)(2,1)S(1)}, bf16[1,1,1,4,16,4096]{5,4,3,2,1,0:T(8,128)(2,1)}, u32[]{:S(2)}) copy-start(bf16[1,1,1,4,16,4096]{5,4,3,2,1,0:T(8,128)(2,1)} %param.8) | copy-start | bytes 1572868
  15.5 3.7 %copy-start.1 = (bf16[1,3,384,4096]{3,2,1,0:T(8,128)(2,1)S(1)}, bf16[1,3,384,4096]{3,2,1,0:T(8,128)(2,1)}, u32[]{:S(2)}) copy-start(bf16[1,3,384,4096]{3,2,1,0:T(8,128)(2,1)} %param.9) | copy-start | bytes 28311556
  23.3 17.4 %collective-permute-start.9 = (bf16[64,2816]{1,0:T(8,128)(2,1)S(1)}, bf16[64,2816]{1,0:T(8,128)(2,1)S(1)}, u32[]{:S(2)}, u32[]{:S(2)}) collective-permute-start(bf16[64,2816]{1,0:T(8,128)(2,1)S(1)} %get-tuple-element.31), channel_id=1, source_target_pairs={{0,16},{16,0},{1,17},{17,1},{2,18},{18,2},{3,19},{19,3},{4,20},{20... | collective-permute-start | bytes 1081352 | tf_op jit(solution)/shard_map/ppermute | solution.py:33
  24.9 2.1 %collective-permute-start.4 = (bf16[16,4096]{1,0:T(8,128)(2,1)S(1)}, bf16[16,4096]{1,0:T(8,128)(2,1)S(1)}, u32[]{:S(2)}, u32[]{:S(2)}) collective-permute-start(bf16[16,4096]{1,0:T(8,128)(2,1)S(1)} %get-tuple-element.23), channel_id=1, source_target_pairs={{0,1},{1,0},{2,3},{3,2},{4,5},{5,4},{6,7},{7,6},{8,9},{9,8},{10,11... | collective-permute-start | bytes 393224 | tf_op jit(solution)/shard_map/ppermute | solution.py:33
  24.9 15.8 %collective-permute-start.8 = (bf16[64,2432]{1,0:T(8,128)(2,1)S(1)}, bf16[64,2432]{1,0:T(8,128)(2,1)S(1)}, u32[]{:S(2)}, u32[]{:S(2)}) collective-permute-start(bf16[64,2432]{1,0:T(8,128)(2,1)S(1)} %get-tuple-element.30), channel_id=1, source_target_pairs={{0,16},{16,0},{1,17},{17,1},{2,18},{18,2},{3,19},{19,3},{4,20},{20... | collective-permute-start | bytes 933896 | tf_op jit(solution)/shard_map/ppermute | solution.py:33
  25.5 6.3 %collective-permute-start.5 = (bf16[16,4096]{1,0:T(8,128)(2,1)S(1)}, bf16[16,4096]{1,0:T(8,128)(2,1)S(1)}, u32[]{:S(2)}, u32[]{:S(2)}) collective-permute-start(bf16[16,4096]{1,0:T(8,128)(2,1)S(1)} %get-tuple-element.24), channel_id=1, source_target_pairs={{0,2},{1,3},{2,0},{3,1},{4,6},{5,7},{6,4},{7,5},{8,10},{9,11},{10,... | collective-permute-start | bytes 393224 | tf_op jit(solution)/shard_map/ppermute | solution.py:33
  27.0 6.1 %collective-permute-start.6 = (bf16[16,4096]{1,0:T(8,128)(2,1)S(1)}, bf16[16,4096]{1,0:T(8,128)(2,1)S(1)}, u32[]{:S(2)}, u32[]{:S(2)}) collective-permute-start(bf16[16,4096]{1,0:T(8,128)(2,1)S(1)} %get-tuple-element.25), channel_id=1, source_target_pairs={{0,3},{1,2},{2,1},{3,0},{4,7},{5,6},{6,5},{7,4},{8,11},{9,10},{10,... | collective-permute-start | bytes 393224 | tf_op jit(solution)/shard_map/ppermute | solution.py:33
  33.1 11.0 %collective-permute-start.7 = (bf16[16,4224]{1,0:T(8,128)(2,1)S(1)}, bf16[16,4224]{1,0:T(8,128)(2,1)S(1)}, u32[]{:S(2)}, u32[]{:S(2)}) collective-permute-start(bf16[16,4224]{1,0:T(8,128)(2,1)S(1)} %sum_returned.1), channel_id=1, source_target_pairs={{0,12},{4,0},{8,4},{12,8},{1,13},{5,1},{9,5},{13,9},{2,14},{6,2},{... | collective-permute-start | bytes 405512 | tf_op jit(solution)/shard_map/ppermute | solution.py:38

commit v3 on v2

v3 whole, which is shorter than its diff:
```python
import functools

import jax
import jax.numpy as jnp
from jax import lax
from jax.experimental import pallas as pl
from jax.experimental.pallas import tpu as pltpu
from jax.sharding import PartitionSpec as P

BF16 = jnp.bfloat16
F32 = jnp.float32
LANES = 128
VMEM_LIMIT = 20 * 2**20
SUM_COST = 0
ROUTE_COST = 10**10
LAST_LAST = (((1,), (1,)), ((), ()))
FIRST_FIRST = (((0,), (0,)), ((), ()))
ROWS_COLS = (((1,), (0,)), ((), ()))


def partner(index, step, count):
    if count & (count - 1) == 0:
        return index ^ step
    return (index + step) % count


def origin(index, step, count):
    if count & (count - 1) == 0:
        return index ^ step
    return (index - step) % count


def pairs_of(owners):
    inner = 2 if owners % 2 == 0 else 1
    return inner, owners // inner


def source(me, block, owners):
    inner, outer = pairs_of(owners)
    return origin(me // inner, block // inner, outer) * inner + (me % inner ^ block % inner)


def exchange(value, axis, step):
    count = lax.axis_size(axis)
    return lax.ppermute(value, axis, [(i, partner(i, step, count)) for i in range(count)])


def to_sibling(value):
    return lax.ppermute(value, "expert", [(i, i ^ 1) for i in range(lax.axis_size("expert"))])


def to_pair(value, step, back=False):
    owners = lax.axis_size("expert")
    inner, outer = pairs_of(owners)
    hops = [(i, partner(i // inner, step, outer) * inner + i % inner) for i in range(owners)]
    return lax.ppermute(value, "expert", [(j, i) for i, j in hops] if back else hops)


def to_previous(value):
    count = lax.axis_size("pipe")
    return lax.ppermute(value, "pipe", [(i, (i - 1) % count) for i in range(count)])


def mm(left, right, dims):
    return lax.dot_general(left, right, dims, preferred_element_type=F32)


def run(body, name, outs, inputs, flops, in_specs=None, out_specs=None, scratch=()):
    vmem = pl.BlockSpec(memory_space=pltpu.VMEM)
    moved = sum(v.size * v.dtype.itemsize for v in inputs)
    return pl.pallas_call(
        body,
        name=name,
        out_shape=outs,
        in_specs=in_specs or [vmem] * len(inputs),
        out_specs=out_specs or [vmem] * len(outs),
        scratch_shapes=scratch,
        compiler_params=pltpu.CompilerParams(vmem_limit_bytes=VMEM_LIMIT),
        cost_estimate=pl.CostEstimate(flops=flops, bytes_accessed=moved, transcendentals=0),
    )(*inputs)


def in_hbm(value):
    return pltpu.with_memory_space_constraint(value, pltpu.HBM)


def route_body(routing_hbm, gates_hbm, incoming_hbm, saved_hbm, *refs):
    others = lax.axis_size("dp") - 1
    owners = lax.axis_size("expert")
    routed_ref, picked_ref, ids_ref = refs[:3]
    fars = refs[3 : 3 + others]
    routing_ref, gates_ref, incoming_ref, sems, far_sem = refs[3 + others :]
    capacity = routed_ref.shape[0]
    tokens, width = incoming_ref.shape
    me = lax.axis_index("expert")
    replica = lax.axis_index("dp")
    fetches = [
        pltpu.make_async_copy(routing_hbm, routing_ref, sems.at[0]),
        pltpu.make_async_copy(gates_hbm, gates_ref, sems.at[1]),
        pltpu.make_async_copy(incoming_hbm, incoming_ref, sems.at[2]),
    ]
    for f in fetches:
        f.start()
    copies = []
    for r in range(others):
        part = fars[r].shape[1]
        first = pl.multiple_of(partner(replica, r + 1, others + 1) * part, LANES)
        for k in range(owners):
            copies.append(
                pltpu.make_async_copy(
                    saved_hbm.at[source(me, k, owners), :, pl.ds(first, part)],
                    fars[r].at[pl.ds(k * capacity, capacity)],
                    far_sem.at[r, k],
                )
            )
    for c in copies:
        c.start()
    fetches[0].wait()
    fetches[1].wait()
    matches = routing_ref[...] == 0
    member = jnp.max(jnp.where(matches, F32(1.0), F32(0.0)), axis=0, keepdims=True)
    share = jnp.sum(jnp.where(matches, gates_ref[...], F32(0.0)), axis=0, keepdims=True)
    earlier = lax.broadcasted_iota(jnp.int32, (tokens, tokens), 0) < lax.broadcasted_iota(
        jnp.int32, (tokens, tokens), 1
    )
    spread = jnp.broadcast_to(member, (capacity, tokens))
    slot = mm(spread.astype(BF16), jnp.where(earlier, F32(1.0), F32(0.0)).astype(BF16), ROWS_COLS)
    wanted = lax.broadcasted_iota(jnp.int32, (capacity, tokens), 0).astype(F32)
    chosen = jnp.where((slot == wanted) & (spread > 0.5), F32(1.0), F32(0.0))
    weighting = jnp.sum(chosen * share, axis=1, keepdims=True)
    token = lax.broadcasted_iota(jnp.int32, (capacity, tokens), 1)
    filled = jnp.sum(chosen, axis=1, keepdims=True)
    high = jnp.sum(chosen * (token // LANES).astype(F32), axis=1, keepdims=True)
    low = jnp.sum(chosen * (token % LANES).astype(F32), axis=1, keepdims=True)
    high = jnp.where(filled > 0.5, high, F32(-1.0))
    lane = lax.broadcasted_iota(jnp.int32, (capacity, LANES), 1)
    ids_ref[...] = jnp.where(lane == 0, high, jnp.where(lane == 1, low, F32(0.0))).astype(BF16)
    fetches[2].wait()
    picked = mm(chosen.astype(BF16), incoming_ref[...], ROWS_COLS)
    routed_ref[...] = (picked * weighting).astype(BF16)
    picked_ref[...] = picked.astype(BF16)
    for c in copies:
        c.wait()


def forward_body(saved_hbm, weights_ref, slope_ref, active_ref, hidden_ref, own_ref, rows_ref, row_sem):
    owners, capacity, width = saved_hbm.shape
    part = own_ref.shape[1]
    me = lax.axis_index("expert")
    replica = lax.axis_index("dp")
    fetches = []
    for k in range(owners):
        fetches.append(
            pltpu.make_async_copy(
                saved_hbm.at[source(me, k, owners)],
                rows_ref.at[pl.ds(k * capacity, capacity)],
                row_sem.at[k],
            )
        )
    for f in fetches:
        f.start()
    for f in fetches:
        f.wait()
    rows = rows_ref[...]
    gate_pre = mm(weights_ref[0], rows, LAST_LAST)
    up_pre = mm(weights_ref[1], rows, LAST_LAST)
    sigmoid_gate = jax.nn.sigmoid(gate_pre)
    activated = gate_pre * sigmoid_gate
    slope_ref[...] = up_pre * sigmoid_gate * (1.0 + gate_pre * (1.0 - sigmoid_gate))
    active_ref[...] = activated
    hidden_ref[...] = jnp.transpose(activated * up_pre).astype(BF16)
    own_ref[...] = rows_ref[:, pl.ds(pl.multiple_of(replica * part, LANES), part)]


def backward_body(order, *refs):
    blocks = refs[:order]
    weights_ref, slope_ref, active_ref = refs[order : order + 3]
    kept_ref, given_ref, grads_ref = refs[-3:]
    inner, outer = pairs_of(order)
    rows = jnp.concatenate([b[...] for b in blocks], axis=0)
    hidden_grad = mm(weights_ref[2], rows, LAST_LAST)
    gate_grad = jnp.transpose(hidden_grad * slope_ref[...]).astype(BF16)
    up_grad = jnp.transpose(hidden_grad * active_ref[...]).astype(BF16)
    capacity, width = blocks[0].shape
    step = 512
    for c in range(width // step):
        at = slice(c * step, (c + 1) * step)
        total = mm(gate_grad, weights_ref[0, :, at], ROWS_COLS) + mm(up_grad, weights_ref[1, :, at], ROWS_COLS)
        for k in range(order):
            into = kept_ref if k % inner == 0 else given_ref
            j = k // inner
            into[j * capacity : (j + 1) * capacity, at] = total[k * capacity : (k + 1) * capacity].astype(BF16)
    hid = weights_ref.shape[1]
    grads_ref[:, :hid] = gate_grad
    grads_ref[:, hid:] = up_grad


def pair_body(paired, kept_ref, given_ref, *outs):
    capacity = outs[0].shape[0]
    for j, ref in enumerate(outs, 1):
        at = slice(j * capacity, (j + 1) * capacity)
        total = kept_ref[at].astype(F32)
        ref[...] = (total + given_ref[at].astype(F32) if paired else total).astype(BF16)


def pack_body(order, *refs):
    blocks = refs[:order]
    hidden_ref, grads_ref, _ = refs[order : order + 3]
    own_ref, fars = refs[order + 3], refs[order + 4 :]
    capacity = blocks[0].shape[0]
    part = own_ref.shape[1]
    replica = lax.axis_index("dp")
    for r in range(len(fars) + 1):
        first = pl.multiple_of(partner(replica, r, len(fars) + 1) * part, LANES)
        into = own_ref if r == 0 else fars[r - 1]
        for k in range(order):
            into[k * capacity : (k + 1) * capacity, :part] = blocks[k][:, pl.ds(first, part)]
        if r:
            hid = hidden_ref.shape[1]
            into[:, part : part + 2 * hid] = grads_ref[...]
            into[:, part + 2 * hid :] = hidden_ref[...]


def return_body(paired, picked_ref, ids_ref, kept_ref, given_ref, *refs):
    returned, out_ref = refs[:-1], refs[-1]
    capacity, width = picked_ref.shape
    back = kept_ref[:capacity].astype(F32)
    if paired:
        back = back + given_ref[:capacity].astype(F32)
    for ref in returned:
        back = back + ref[...].astype(F32)
    out_ref[:, :width] = (picked_ref[...].astype(F32) + back).astype(BF16)
    out_ref[:, width:] = ids_ref[...]


def weight_body(others, hidden_ref, grads_ref, inputs_ref, rows_ref, *refs):
    fars_in, fars_out = refs[:others], refs[others : 2 * others]
    out_hbm, held, sems = refs[2 * others :]
    part = inputs_ref.shape[1]
    hid = hidden_ref.shape[1]
    columns = held.shape[2]
    left = [
        jnp.concatenate(
            [grads_ref[:, i * hid : (i + 1) * hid] if i < 2 else hidden_ref[...]]
            + [f[:, part + i * hid : part + (i + 1) * hid] for f in fars_out],
            axis=0,
        )
        for i in range(3)
    ]
    copies = []
    for c in range(part // columns):
        at = slice(c * columns, (c + 1) * columns)
        inputs = jnp.concatenate([inputs_ref[:, at]] + [f[:, at] for f in fars_in], axis=0)
        rows = jnp.concatenate([rows_ref[:, at]] + [f[:, at] for f in fars_out], axis=0)
        for i in range(3):
            n = len(copies)
            held[n] = mm(left[i], rows if i == 2 else inputs, FIRST_FIRST).astype(BF16)
            copies.append(pltpu.make_async_copy(held.at[n], out_hbm.at[0, i, :, pl.ds(c * columns, columns)], sems.at[n]))
            copies[-1].start()
    for c in copies:
        c.wait()


def merge_body(shifted_ref, changed_ref, out_hbm, held, sems):
    tokens, width = shifted_ref.shape
    capacity = changed_ref.shape[0]
    high = changed_ref[:, width : width + 1].astype(F32)
    low = changed_ref[:, width + 1 : width + 2].astype(F32)
    token = lax.broadcasted_iota(jnp.int32, (capacity, tokens), 1).astype(F32)
    chosen = jnp.where(token == high * F32(LANES) + low, F32(1.0), F32(0.0)).astype(BF16)
    here = mm(chosen, jnp.ones((capacity, LANES), BF16), FIRST_FIRST)[:, :1] > 0.5
    step = held.shape[2]
    copies = []
    for c in range(width // step):
        at = slice(c * step, (c + 1) * step)
        placed = mm(chosen, changed_ref[:, at], FIRST_FIRST)
        held[c] = jnp.where(here, placed, shifted_ref[:, at].astype(F32)).astype(BF16)
        copies.append(pltpu.make_async_copy(held.at[c], out_hbm.at[0, 0, :, pl.ds(c * step, step)], sems.at[c]))
        copies[-1].start()
    for c in copies:
        c.wait()


def shards(output_grads, gate_values, routing, saved_inputs, expert_weights):
    owners = lax.axis_size("expert")
    replicas = lax.axis_size("dp")
    others = replicas - 1
    capacity = saved_inputs.shape[4]
    incoming = output_grads[0, 0]
    tokens, width = incoming.shape
    part = width // replicas
    weights = expert_weights[0]
    hid = weights.shape[1]
    rows = owners * capacity
    top = routing.shape[3]
    out = jax.ShapeDtypeStruct
    hbm = pl.BlockSpec(memory_space=pltpu.HBM)
    saved = saved_inputs[0, 0, 0]

    shifted = to_previous(incoming)

    routed, picked, ids, *fars = run(
        route_body,
        "route",
        [out((capacity, width), BF16), out((capacity, width), BF16), out((capacity, LANES), BF16)]
        + [out((rows, part), BF16)] * others,
        [in_hbm(v) for v in (jnp.transpose(routing[0, 0]), jnp.transpose(gate_values[0, 0]), incoming, saved)],
        ROUTE_COST,
        in_specs=[hbm] * 4,
        scratch=[
            pltpu.VMEM((top, tokens), jnp.int32),
            pltpu.VMEM((top, tokens), F32),
            pltpu.VMEM((tokens, width), BF16),
            pltpu.SemaphoreType.DMA((3,)),
            pltpu.SemaphoreType.DMA((max(others, 1), owners)),
        ],
    )
    inner, outer = pairs_of(owners)
    distant = [to_pair(routed, j) for j in range(1, outer)]
    arrived = [to_sibling(routed)] if inner == 2 else []
    for block in distant:
        arrived.append(block)
        if inner == 2:
            arrived.append(to_sibling(block))
    far_inputs = [exchange(f, "dp", k + 1) for k, f in enumerate(fars)]

    slope, active, hidden, own_inputs = run(
        forward_body,
        "forward",
        [
            out((hid, rows), F32),
            out((hid, rows), F32),
            out((rows, hid), BF16),
            out((rows, part), BF16),
        ],
        [in_hbm(saved), weights],
        4 * rows * hid * width,
        in_specs=[hbm, pl.BlockSpec(memory_space=pltpu.VMEM)],
        scratch=[
            pltpu.VMEM((rows, width), BF16),
            pltpu.SemaphoreType.DMA((owners,)),
        ],
    )

    mine = outer * capacity
    kept, given, grads = run(
        functools.partial(backward_body, owners),
        "backward",
        [out((mine, width), BF16)] * 2 + [out((rows, 2 * hid), BF16)],
        [routed, *arrived, weights, slope, active, *far_inputs],
        6 * rows * hid * width,
    )
    if inner == 2:
        given = to_sibling(given)
    sums = run(
        functools.partial(pair_body, inner == 2),
        "pair_sums",
        [out((capacity, width), BF16)] * (outer - 1),
        [kept, given],
        0,
    )
    returned = [to_pair(v, j, back=True) for j, v in enumerate(sums, 1)]
    own_rows, *fars = run(
        functools.partial(pack_body, owners),
        "pack",
        [out((rows, part), BF16)] + [out((rows, part + 3 * hid), BF16)] * others,
        [routed, *arrived, hidden, grads, given],
        0,
    )
    far_rows = [exchange(f, "dp", k + 1) for k, f in enumerate(fars)]

    changed = run(
        functools.partial(return_body, inner == 2),
        "sum_returned",
        [out((capacity, width + LANES), BF16)],
        [picked, ids, kept, given, *returned],
        SUM_COST,
    )[0]
    next_changed = to_previous(changed)

    columns = min(part, 512)
    pieces = 3 * part // columns
    weight_grads = run(
        functools.partial(weight_body, others),
        "weight_grads",
        [out((1, 3, hid, part), BF16)],
        [hidden, grads, own_inputs, own_rows, *far_inputs, *far_rows],
        6 * rows * replicas * hid * part,
        out_specs=[hbm],
        scratch=[pltpu.VMEM((pieces, hid, columns), BF16), pltpu.SemaphoreType.DMA((pieces,))],
    )[0]

    step = min(width, 1024)
    passed_grads = run(
        merge_body,
        "merge",
        [out((1, 1, tokens, width), BF16)],
        [shifted, next_changed],
        2 * capacity * tokens * width,
        out_specs=[hbm],
        scratch=[pltpu.VMEM((width // step, tokens, step), BF16), pltpu.SemaphoreType.DMA((width // step,))],
    )[0]
    return (passed_grads, weight_grads)


def solution(mesh):
    placed = (
        P("dp", "pipe", "expert", None),
        P("dp", "pipe", "expert", None),
        P("dp", "pipe", "expert", None),
        P("dp", "pipe", None, None, None, None),
        P("pipe", None, "expert", None),
    )
    return jax.shard_map(
        shards,
        mesh=mesh,
        in_specs=placed,
        out_specs=(P("dp", "pipe", "expert", None), P("pipe", None, "expert", "dp")),
        check_vma=False,
    )
```

time: 46.1 us -> 37.7 us (0.82)
  local copies, waits for them, and re-layouts: 8.65 us -> 0.01 us
  starting transfers between devices: 11.7 us -> 11 us
  waiting for transfers between devices: 12.6 us -> 13.2 us
  Pallas kernels: 12 us -> 12.5 us
    unnamed x12 -> x2, local copies, waits for them, and re-layouts: 8.57 us -> 0.01 us
    ppermute x0 -> x5, waiting for transfers between devices: none -> 8.09 us  [the longest x2 6.56 us: to_pair(): lax.ppermute(value, 'expert', [(j, i) for i, j in hops] if back else hops)]
    ppermute x8 -> x2, waiting for transfers between devices: 12.6 us -> 5.11 us  [exchange(): lax.ppermute(value, axis, [(i, partner(i, step, count)) for i in range(co...]
    ppermute x8 -> x2, starting transfers between devices: 6.1 us -> 3.05 us  [exchange(): lax.ppermute(value, axis, [(i, partner(i, step, count)) for i in range(co...]
    ppermute x0 -> x5, starting transfers between devices: none -> 2.38 us  [the longest x2 2.3 us: to_pair(): lax.ppermute(value, 'expert', [(j, i) for i, j in hops] if back else hops)]
    pallas_call x6 -> x8, Pallas kernels: 12 us -> 12.5 us  [run(): pl.pallas_call(body, name=name, out_shape=outs, in_specs=in_specs or [vme...]
  transfers between devices with their start and end apart: 10 -> 9, of which waited for: 3 -> 5; matrix products, arithmetic and copies ran while one was open for 0% -> 0% of each run, Pallas kernels for 23% -> 30%
where the time goes in v3:
time: 37.7 us; the launch traced here: 37.5 us
  waiting for transfers between devices  13.2 us (35%)
  Pallas kernels  12.5 us (33%)
  starting transfers between devices  11 us (29%)
  between operations  0.72 us (2%)
    pallas_call x8, Pallas kernels, run(): pl.pallas_call(body, name=name, out_shape=outs, in_specs=in_specs or [vme...  12.5 us
    ppermute x2, waiting for transfers between devices, to_pair(): lax.ppermute(value, 'expert', [(j, i) for i, j in hops] if back else hops)  6.56 us
    ppermute x2, starting transfers between devices, to_previous(): lax.ppermute(value, 'pipe', [(i, (i - 1) % count) for i in range(count)])  5.6 us
    ppermute x2, waiting for transfers between devices, exchange(): lax.ppermute(value, axis, [(i, partner(i, step, count)) for i in range(co...  5.11 us
    ppermute x2, starting transfers between devices, exchange(): lax.ppermute(value, axis, [(i, partner(i, step, count)) for i in range(co...  3.05 us
    ppermute x2, starting transfers between devices, to_pair(): lax.ppermute(value, 'expert', [(j, i) for i, j in hops] if back else hops)  2.3 us
    ppermute x3, waiting for transfers between devices, to_sibling(): lax.ppermute(value, 'expert', [(i, i ^ 1) for i in range(lax.axis_size('e...  1.53 us
  transfers between devices with their start and end apart: 9, of which 5 were waited for; matrix products, arithmetic and copies ran while one was open for 0% of the time, Pallas kernels for 30%

profile of v3, /device:TPU:0, one launch (start us, length us, event | category | flops | bytes accessed | tf_op | source)
XLA Modules:
  0.0 37.5 jit_solution(3546683421281446433)
XLA Ops:
  0.6 5.1 %collective-permute-start = (bf16[128,4096]{1,0:T(8,128)(2,1)}, bf16[128,4096]{1,0:T(8,128)(2,1)S(1)}, u32[]{:S(2)}, u32[]{:S(2)}) collective-permute-start(bf16[128,4096]{1,0:T(8,128)(2,1)} %bitcast.13), channel_id=1, source_target_pairs={{0,12},{4,0},{8,4},{12,8},{1,13},{5,1},{9,5},{13,9},{2,14},{6,2},{... | collective-permute-start | bytes 3145736 | tf_op jit(solution)/shard_map/ppermute | solution.py:61
  5.7 0.0 copy-start
  5.7 1.8 %route.1 = (bf16[16,4096]{1,0:T(8,128)(2,1)S(1)}, bf16[16,4096]{1,0:T(8,128)(2,1)S(1)}, bf16[16,128]{1,0:T(8,128)(2,1)S(1)}, bf16[64,2048]{1,0:T(8,128)(2,1)S(1)}) custom-call(s32[8,128]{1,0:T(8,128)} %bitcast.15, f32[8,128]{1,0:T(8,128)} %bitcast.16, bf16[128,4096]{1,0:T(8,128)(2,1)} %bitcast.14, bf16[4,16,4096]{2,1,0:T(8,128)(2,1)} %bitcast.11), custom_call_target="tpu_custom_call" | custom-call | flops 10000000000 | bytes 1581056 | tf_op jit(solution)/shard_map/route/pallas_call | solution.py:71
  7.6 1.6 %collective-permute-start.2 = (bf16[16,4096]{1,0:T(8,128)(2,1)S(1)}, bf16[16,4096]{1,0:T(8,128)(2,1)S(1)}, u32[]{:S(2)}, u32[]{:S(2)}) collective-permute-start(bf16[16,4096]{1,0:T(8,128)(2,1)S(1)} %get-tuple-element.17.refs_0_), channel_id=1, source_target_pairs={{0,2},{1,3},{2,0},{3,1},{4,6},{5,7},{6,4},{7,5},{8,10},{9,11},{10,... | collective-permute-start | bytes 393224 | tf_op jit(solution)/shard_map/ppermute | solution.py:56
  9.2 1.5 %collective-permute-start.4 = (bf16[64,2048]{1,0:T(8,128)(2,1)S(1)}, bf16[64,2048]{1,0:T(8,128)(2,1)S(1)}, u32[]{:S(2)}, u32[]{:S(2)}) collective-permute-start(bf16[64,2048]{1,0:T(8,128)(2,1)S(1)} %get-tuple-element.20), channel_id=1, source_target_pairs={{0,16},{16,0},{1,17},{17,1},{2,18},{18,2},{3,19},{19,3},{4,20},{20... | collective-permute-start | bytes 786440 | tf_op jit(solution)/shard_map/ppermute | solution.py:45
  10.6 0.0 collective-permute-start.1
  10.6 2.0 %collective-permute-done.2.refs_2_ = bf16[16,4096]{1,0:T(8,128)(2,1)S(1)} collective-permute-done((bf16[16,4096]{1,0:T(8,128)(2,1)S(1)}, bf16[16,4096]{1,0:T(8,128)(2,1)S(1)}, u32[]{:S(2)}, u32[]{:S(2)}) %collective-permute-start.2) | collective-permute-done | bytes 131104 | tf_op jit(solution)/shard_map/ppermute | solution.py:56
  12.6 0.0 collective-permute-start.3
  12.6 0.0 copy-done
  12.6 3.0 %forward.1 = (f32[384,64]{1,0:T(8,128)S(1)}, f32[384,64]{1,0:T(8,128)S(1)}, bf16[64,384]{1,0:T(8,128)(2,1)S(1)}, bf16[64,2048]{1,0:T(8,128)(2,1)S(1)}) custom-call(bf16[4,16,4096]{2,1,0:T(8,128)(2,1)} %bitcast.12, bf16[3,384,4096]{2,1,0:T(8,128)(2,1)S(1)} %bitcast.9), custom_call_target="tpu_custom_call" | custom-call | flops 402653184 | bytes 9961472 | tf_op jit(solution)/shard_map/forward/pallas_call | solution.py:71
  15.6 0.0 collective-permute-done.1.refs_1_
  15.6 0.0 collective-permute-done.3.refs_3_
  15.6 1.0 %collective-permute-done.4.refs_7_.refs_0_ = bf16[64,2048]{1,0:T(8,128)(2,1)S(1)} collective-permute-done((bf16[64,2048]{1,0:T(8,128)(2,1)S(1)}, bf16[64,2048]{1,0:T(8,128)(2,1)S(1)}, u32[]{:S(2)}, u32[]{:S(2)}) %collective-permute-start.4) | collective-permute-done | bytes 262176 | tf_op jit(solution)/shard_map/ppermute | solution.py:45
  16.6 3.6 %backward.1 = (bf16[32,4096]{1,0:T(8,128)(2,1)S(1)}, bf16[32,4096]{1,0:T(8,128)(2,1)S(1)}, bf16[64,768]{1,0:T(8,128)(2,1)S(1)}) custom-call(bf16[16,4096]{1,0:T(8,128)(2,1)S(1)} %get-tuple-element.17.refs_0_, bf16[16,4096]{1,0:T(8,128)(2,1)S(1)} %collective-permute-done.1.refs_1_, bf16[16,4096]{1,0:T(8,128)(2,1)S(1)} %collective-permute-done.2.refs_2_, ...), custom_call_target="tpu_custom_call" | custom-call | flops 603979776 | bytes 10420224 | tf_op jit(solution)/shard_map/backward/pallas_call | solution.py:71
  20.2 0.1 collective-permute-start.5
  20.3 1.5 %collective-permute-done.5.given_ref.refs_6_ = bf16[32,4096]{1,0:T(8,128)(2,1)S(1)} collective-permute-done((bf16[32,4096]{1,0:T(8,128)(2,1)S(1)}, bf16[32,4096]{1,0:T(8,128)(2,1)S(1)}, u32[]{:S(2)}, u32[]{:S(2)}) %collective-permute-start.5) | collective-permute-done | bytes 262176 | tf_op jit(solution)/shard_map/ppermute | solution.py:49
  21.9 1.6 %collective-permute-start.8 = (bf16[64,3200]{1,0:T(8,128)(2,1)S(1)}, bf16[64,3200]{1,0:T(8,128)(2,1)S(1)}, u32[]{:S(2)}, u32[]{:S(2)}) collective-permute-start(bf16[64,3200]{1,0:T(8,128)(2,1)S(1)} %get-tuple-element.27), channel_id=1, source_target_pairs={{0,16},{16,0},{1,17},{17,1},{2,18},{18,2},{3,19},{19,3},{4,20},{20... | collective-permute-start | bytes 1228808 | tf_op jit(solution)/shard_map/ppermute | solution.py:45
  23.5 0.7 %collective-permute-start.6 = (bf16[16,4096]{1,0:T(8,128)(2,1)S(1)}, bf16[16,4096]{1,0:T(8,128)(2,1)S(1)}, u32[]{:S(2)}, u32[]{:S(2)}) collective-permute-start(bf16[16,4096]{1,0:T(8,128)(2,1)S(1)} %pair_sums.1), channel_id=1, source_target_pairs={{2,0},{3,1},{0,2},{1,3},{6,4},{7,5},{4,6},{5,7},{10,8},{11,9},{8,1... | collective-permute-start | bytes 393224 | tf_op jit(solution)/shard_map/ppermute | solution.py:56
  24.2 4.6 %collective-permute-done.6.refs_0_ = bf16[16,4096]{1,0:T(8,128)(2,1)S(1)} collective-permute-done((bf16[16,4096]{1,0:T(8,128)(2,1)S(1)}, bf16[16,4096]{1,0:T(8,128)(2,1)S(1)}, u32[]{:S(2)}, u32[]{:S(2)}) %collective-permute-start.6) | collective-permute-done | bytes 131104 | tf_op jit(solution)/shard_map/ppermute | solution.py:56
  28.8 0.1 sum_returned.1
  28.9 0.5 %collective-permute-start.7 = (bf16[16,4224]{1,0:T(8,128)(2,1)S(1)}, bf16[16,4224]{1,0:T(8,128)(2,1)S(1)}, u32[]{:S(2)}, u32[]{:S(2)}) collective-permute-start(bf16[16,4224]{1,0:T(8,128)(2,1)S(1)} %sum_returned.1), channel_id=1, source_target_pairs={{0,12},{4,0},{8,4},{12,8},{1,13},{5,1},{9,5},{13,9},{2,14},{6,2},{... | collective-permute-start | bytes 405512 | tf_op jit(solution)/shard_map/ppermute | solution.py:61
  29.4 4.1 %collective-permute-done.8.refs_1_ = bf16[64,3200]{1,0:T(8,128)(2,1)S(1)} collective-permute-done((bf16[64,3200]{1,0:T(8,128)(2,1)S(1)}, bf16[64,3200]{1,0:T(8,128)(2,1)S(1)}, u32[]{:S(2)}, u32[]{:S(2)}) %collective-permute-start.8) | collective-permute-done | bytes 409632 | tf_op jit(solution)/shard_map/ppermute | solution.py:45
  33.5 2.6 %weight_grads.1 = bf16[1,3,384,2048]{3,2,1,0:T(8,128)(2,1)} custom-call(bf16[64,384]{1,0:T(8,128)(2,1)S(1)} %get-tuple-element.23.refs_4_.hidden_ref, bf16[64,768]{1,0:T(8,128)(2,1)S(1)} %get-tuple-element.24.refs_5_.grads_ref, bf16[64,2048]{1,0:T(8,128)(2,1)S(1)} %get-tuple-element.25.inputs_ref, bf16[64,2048]{1,0:T(8,128)(2,1)S(1)} %get-tuple-element.26.rows_ref, ...), custom_call_target="tpu_custom_call" | custom-call | flops 603979776 | bytes 1343488 | tf_op jit(solution)/shard_map/weight_grads/pallas_call | solution.py:71
  36.0 0.0 collective-permute-done.7.changed_ref
  36.0 0.0 collective-permute-done.shifted_ref
  36.0 1.5 %merge.1 = bf16[1,1,128,4096]{3,2,1,0:T(8,128)(2,1)} custom-call(bf16[128,4096]{1,0:T(8,128)(2,1)S(1)} %collective-permute-done.shifted_ref, bf16[16,4224]{1,0:T(8,128)(2,1)S(1)} %collective-permute-done.7.changed_ref), custom_call_target="tpu_custom_call" | custom-call | flops 16777216 | bytes 1183744 | tf_op jit(solution)/shard_map/merge/pallas_call | solution.py:71
  (2 shorter events, 0.1 us)
Async XLA Ops:
  0.6 35.4 %collective-permute-start = (bf16[128,4096]{1,0:T(8,128)(2,1)}, bf16[128,4096]{1,0:T(8,128)(2,1)S(1)}, u32[]{:S(2)}, u32[]{:S(2)}) collective-permute-start(bf16[128,4096]{1,0:T(8,128)(2,1)} %bitcast.13), channel_id=1, source_target_pairs={{0,12},{4,0},{8,4},{12,8},{1,13},{5,1},{9,5},{13,9},{2,14},{6,2},{... | collective-permute-start | bytes 3145736 | tf_op jit(solution)/shard_map/ppermute | solution.py:61
  5.7 6.9 %copy-start = (bf16[1,3,384,4096]{3,2,1,0:T(8,128)(2,1)S(1)}, bf16[1,3,384,4096]{3,2,1,0:T(8,128)(2,1)}, u32[]{:S(2)}) copy-start(bf16[1,3,384,4096]{3,2,1,0:T(8,128)(2,1)} %param.9) | copy-start | bytes 28311556
  7.6 5.0 %collective-permute-start.2 = (bf16[16,4096]{1,0:T(8,128)(2,1)S(1)}, bf16[16,4096]{1,0:T(8,128)(2,1)S(1)}, u32[]{:S(2)}, u32[]{:S(2)}) collective-permute-start(bf16[16,4096]{1,0:T(8,128)(2,1)S(1)} %get-tuple-element.17.refs_0_), channel_id=1, source_target_pairs={{0,2},{1,3},{2,0},{3,1},{4,6},{5,7},{6,4},{7,5},{8,10},{9,11},{10,... | collective-permute-start | bytes 393224 | tf_op jit(solution)/shard_map/ppermute | solution.py:56
  9.2 7.5 %collective-permute-start.4 = (bf16[64,2048]{1,0:T(8,128)(2,1)S(1)}, bf16[64,2048]{1,0:T(8,128)(2,1)S(1)}, u32[]{:S(2)}, u32[]{:S(2)}) collective-permute-start(bf16[64,2048]{1,0:T(8,128)(2,1)S(1)} %get-tuple-element.20), channel_id=1, source_target_pairs={{0,16},{16,0},{1,17},{17,1},{2,18},{18,2},{3,19},{19,3},{4,20},{20... | collective-permute-start | bytes 786440 | tf_op jit(solution)/shard_map/ppermute | solution.py:45
  10.6 4.9 %collective-permute-start.1 = (bf16[16,4096]{1,0:T(8,128)(2,1)S(1)}, bf16[16,4096]{1,0:T(8,128)(2,1)S(1)}, u32[]{:S(2)}, u32[]{:S(2)}) collective-permute-start(bf16[16,4096]{1,0:T(8,128)(2,1)S(1)} %get-tuple-element.17.refs_0_), channel_id=1, source_target_pairs={{0,1},{1,0},{2,3},{3,2},{4,5},{5,4},{6,7},{7,6},{8,9},{9,8},{10,11... | collective-permute-start | bytes 393224 | tf_op jit(solution)/shard_map/ppermute | solution.py:49
  12.6 3.0 %collective-permute-start.3 = (bf16[16,4096]{1,0:T(8,128)(2,1)S(1)}, bf16[16,4096]{1,0:T(8,128)(2,1)S(1)}, u32[]{:S(2)}, u32[]{:S(2)}) collective-permute-start(bf16[16,4096]{1,0:T(8,128)(2,1)S(1)} %collective-permute-done.2.refs_2_), channel_id=1, source_target_pairs={{0,1},{1,0},{2,3},{3,2},{4,5},{5,4},{6,7},{7,6},{8,9},{9,8},{10,11... | collective-permute-start | bytes 393224 | tf_op jit(solution)/shard_map/ppermute | solution.py:49
  20.2 1.6 %collective-permute-start.5 = (bf16[32,4096]{1,0:T(8,128)(2,1)S(1)}, bf16[32,4096]{1,0:T(8,128)(2,1)S(1)}, u32[]{:S(2)}, u32[]{:S(2)}) collective-permute-start(bf16[32,4096]{1,0:T(8,128)(2,1)S(1)} %get-tuple-element.22), channel_id=1, source_target_pairs={{0,1},{1,0},{2,3},{3,2},{4,5},{5,4},{6,7},{7,6},{8,9},{9,8},{10,11... | collective-permute-start | bytes 786440 | tf_op jit(solution)/shard_map/ppermute | solution.py:49
  21.9 11.6 %collective-permute-start.8 = (bf16[64,3200]{1,0:T(8,128)(2,1)S(1)}, bf16[64,3200]{1,0:T(8,128)(2,1)S(1)}, u32[]{:S(2)}, u32[]{:S(2)}) collective-permute-start(bf16[64,3200]{1,0:T(8,128)(2,1)S(1)} %get-tuple-element.27), channel_id=1, source_target_pairs={{0,16},{16,0},{1,17},{17,1},{2,18},{18,2},{3,19},{19,3},{4,20},{20... | collective-permute-start | bytes 1228808 | tf_op jit(solution)/shard_map/ppermute | solution.py:45
  23.5 5.3 %collective-permute-start.6 = (bf16[16,4096]{1,0:T(8,128)(2,1)S(1)}, bf16[16,4096]{1,0:T(8,128)(2,1)S(1)}, u32[]{:S(2)}, u32[]{:S(2)}) collective-permute-start(bf16[16,4096]{1,0:T(8,128)(2,1)S(1)} %pair_sums.1), channel_id=1, source_target_pairs={{2,0},{3,1},{0,2},{1,3},{6,4},{7,5},{4,6},{5,7},{10,8},{11,9},{8,1... | collective-permute-start | bytes 393224 | tf_op jit(solution)/shard_map/ppermute | solution.py:56
  28.9 7.2 %collective-permute-start.7 = (bf16[16,4224]{1,0:T(8,128)(2,1)S(1)}, bf16[16,4224]{1,0:T(8,128)(2,1)S(1)}, u32[]{:S(2)}, u32[]{:S(2)}) collective-permute-start(bf16[16,4224]{1,0:T(8,128)(2,1)S(1)} %sum_returned.1), channel_id=1, source_target_pairs={{0,12},{4,0},{8,4},{12,8},{1,13},{5,1},{9,5},{13,9},{2,14},{6,2},{... | collective-permute-start | bytes 405512 | tf_op jit(solution)/shard_map/ppermute | solution.py:61

commit v4 on v3

--- a/solution.py
+++ b/solution.py
@@ -87,9 +87,10 @@
 def route_body(routing_hbm, gates_hbm, incoming_hbm, saved_hbm, *refs):
     others = lax.axis_size("dp") - 1
     owners = lax.axis_size("expert")
-    routed_ref, picked_ref, ids_ref = refs[:3]
-    fars = refs[3 : 3 + others]
-    routing_ref, gates_ref, incoming_ref, sems, far_sem = refs[3 + others :]
+    inner, _ = pairs_of(owners)
+    routed_ref, picked_ref, ids_ref, rows_ref = refs[:4]
+    fars = refs[4 : 4 + others]
+    routing_ref, gates_ref, incoming_ref, sems, far_sem = refs[4 + others :]
     capacity = routed_ref.shape[0]
     tokens, width = incoming_ref.shape
     me = lax.axis_index("expert")
@@ -101,16 +102,21 @@
     ]
     for f in fetches:
         f.start()
-    copies = []
+    copies = [
+        pltpu.make_async_copy(
+            saved_hbm.at[source(me, k, owners)], rows_ref.at[pl.ds(k * capacity, capacity)], far_sem.at[others, k]
+        )
+        for k in range(owners)
+    ]
     for r in range(others):
         part = fars[r].shape[1]
         first = pl.multiple_of(partner(replica, r + 1, others + 1) * part, LANES)
-        for k in range(owners):
+        for j in range(owners // inner):
             copies.append(
                 pltpu.make_async_copy(
-                    saved_hbm.at[source(me, k, owners), :, pl.ds(first, part)],
-                    fars[r].at[pl.ds(k * capacity, capacity)],
-                    far_sem.at[r, k],
+                    saved_hbm.at[source(me, j * inner, owners), :, pl.ds(first, part)],
+                    fars[r].at[pl.ds(j * capacity, capacity)],
+                    far_sem.at[r, j],
                 )
             )
     for c in copies:
@@ -143,24 +149,7 @@
         c.wait()
 
 
-def forward_body(saved_hbm, weights_ref, slope_ref, active_ref, hidden_ref, own_ref, rows_ref, row_sem):
-    owners, capacity, width = saved_hbm.shape
-    part = own_ref.shape[1]
-    me = lax.axis_index("expert")
-    replica = lax.axis_index("dp")
-    fetches = []
-    for k in range(owners):
-        fetches.append(
-            pltpu.make_async_copy(
-                saved_hbm.at[source(me, k, owners)],
-                rows_ref.at[pl.ds(k * capacity, capacity)],
-                row_sem.at[k],
-            )
-        )
-    for f in fetches:
-        f.start()
-    for f in fetches:
-        f.wait()
+def forward_body(rows_ref, weights_ref, slope_ref, active_ref, hidden_ref):
     rows = rows_ref[...]
     gate_pre = mm(weights_ref[0], rows, LAST_LAST)
     up_pre = mm(weights_ref[1], rows, LAST_LAST)
@@ -169,12 +158,11 @@
     slope_ref[...] = up_pre * sigmoid_gate * (1.0 + gate_pre * (1.0 - sigmoid_gate))
     active_ref[...] = activated
     hidden_ref[...] = jnp.transpose(activated * up_pre).astype(BF16)
-    own_ref[...] = rows_ref[:, pl.ds(pl.multiple_of(replica * part, LANES), part)]
 
 
 def backward_body(order, *refs):
     blocks = refs[:order]
-    weights_ref, slope_ref, active_ref = refs[order : order + 3]
+    weights_ref, slope_ref, active_ref, hidden_ref = refs[order : order + 4]
     kept_ref, given_ref, grads_ref = refs[-3:]
     inner, outer = pairs_of(order)
     rows = jnp.concatenate([b[...] for b in blocks], axis=0)
@@ -192,10 +180,12 @@
             into[j * capacity : (j + 1) * capacity, at] = total[k * capacity : (k + 1) * capacity].astype(BF16)
     hid = weights_ref.shape[1]
     grads_ref[:, :hid] = gate_grad
-    grads_ref[:, hid:] = up_grad
-
-
-def pair_body(paired, kept_ref, given_ref, *outs):
+    grads_ref[:, hid : 2 * hid] = up_grad
+    grads_ref[:, 2 * hid :] = hidden_ref[...]
+
+
+def pair_body(paired, others, kept_ref, given_ref, *refs):
+    outs = refs[others:]
     capacity = outs[0].shape[0]
     for j, ref in enumerate(outs, 1):
         at = slice(j * capacity, (j + 1) * capacity)
@@ -203,22 +193,15 @@
         ref[...] = (total + given_ref[at].astype(F32) if paired else total).astype(BF16)
 
 
-def pack_body(order, *refs):
-    blocks = refs[:order]
-    hidden_ref, grads_ref, _ = refs[order : order + 3]
-    own_ref, fars = refs[order + 3], refs[order + 4 :]
+def pack_body(outer, *refs):
+    blocks, fars = refs[:outer], refs[outer:]
     capacity = blocks[0].shape[0]
-    part = own_ref.shape[1]
+    part = fars[0].shape[1]
     replica = lax.axis_index("dp")
-    for r in range(len(fars) + 1):
+    for r, into in enumerate(fars, 1):
         first = pl.multiple_of(partner(replica, r, len(fars) + 1) * part, LANES)
-        into = own_ref if r == 0 else fars[r - 1]
-        for k in range(order):
-            into[k * capacity : (k + 1) * capacity, :part] = blocks[k][:, pl.ds(first, part)]
-        if r:
-            hid = hidden_ref.shape[1]
-            into[:, part : part + 2 * hid] = grads_ref[...]
-            into[:, part + 2 * hid :] = hidden_ref[...]
+        for j in range(outer):
+            into[j * capacity : (j + 1) * capacity] = blocks[j][:, pl.ds(first, part)]
 
 
 def return_body(paired, picked_ref, ids_ref, kept_ref, given_ref, *refs):
@@ -233,25 +216,34 @@
     out_ref[:, width:] = ids_ref[...]
 
 
-def weight_body(others, hidden_ref, grads_ref, inputs_ref, rows_ref, *refs):
-    fars_in, fars_out = refs[:others], refs[others : 2 * others]
-    out_hbm, held, sems = refs[2 * others :]
-    part = inputs_ref.shape[1]
-    hid = hidden_ref.shape[1]
+def weight_body(others, owners, factors_ref, inputs_ref, *refs):
+    inner, outer = pairs_of(owners)
+    halves = others * inner
+    blocks, refs = refs[:owners], refs[owners:]
+    far_inputs, far_rows, far_factors = refs[:halves], refs[halves : 2 * halves], refs[2 * halves : 2 * halves + others]
+    out_hbm, held, sems = refs[2 * halves + others :]
+    capacity = blocks[0].shape[0]
+    hid, part = out_hbm.shape[2:]
     columns = held.shape[2]
+    replica = lax.axis_index("dp")
     left = [
-        jnp.concatenate(
-            [grads_ref[:, i * hid : (i + 1) * hid] if i < 2 else hidden_ref[...]]
-            + [f[:, part + i * hid : part + (i + 1) * hid] for f in fars_out],
-            axis=0,
-        )
-        for i in range(3)
+        jnp.concatenate([f[:, i * hid : (i + 1) * hid] for f in (factors_ref, *far_factors)], axis=0) for i in range(3)
     ]
+
+    def far(halves_of, at):
+        return [
+            halves_of[r * inner + i][j * capacity : (j + 1) * capacity, at]
+            for r in range(others)
+            for j in range(outer)
+            for i in range(inner)
+        ]
+
     copies = []
     for c in range(part // columns):
         at = slice(c * columns, (c + 1) * columns)
-        inputs = jnp.concatenate([inputs_ref[:, at]] + [f[:, at] for f in fars_in], axis=0)
-        rows = jnp.concatenate([rows_ref[:, at]] + [f[:, at] for f in fars_out], axis=0)
+        own = pl.ds(pl.multiple_of(replica * part + c * columns, LANES), columns)
+        inputs = jnp.concatenate([inputs_ref[:, own]] + far(far_inputs, at), axis=0)
+        rows = jnp.concatenate([b[:, own] for b in blocks] + far(far_rows, at), axis=0)
         for i in range(3):
             n = len(copies)
             held[n] = mm(left[i], rows if i == 2 else inputs, FIRST_FIRST).astype(BF16)
@@ -293,17 +285,20 @@
     hid = weights.shape[1]
     rows = owners * capacity
     top = routing.shape[3]
+    inner, outer = pairs_of(owners)
+    mine = outer * capacity
     out = jax.ShapeDtypeStruct
     hbm = pl.BlockSpec(memory_space=pltpu.HBM)
     saved = saved_inputs[0, 0, 0]
 
     shifted = to_previous(incoming)
 
-    routed, picked, ids, *fars = run(
+    routed, picked, ids, own_inputs, *fars = run(
         route_body,
         "route",
         [out((capacity, width), BF16), out((capacity, width), BF16), out((capacity, LANES), BF16)]
-        + [out((rows, part), BF16)] * others,
+        + [out((rows, width), BF16)]
+        + [out((mine, part), BF16)] * others,
         [in_hbm(v) for v in (jnp.transpose(routing[0, 0]), jnp.transpose(gate_values[0, 0]), incoming, saved)],
         ROUTE_COST,
         in_specs=[hbm] * 4,
@@ -312,62 +307,57 @@
             pltpu.VMEM((top, tokens), F32),
             pltpu.VMEM((tokens, width), BF16),
             pltpu.SemaphoreType.DMA((3,)),
-            pltpu.SemaphoreType.DMA((max(others, 1), owners)),
+            pltpu.SemaphoreType.DMA((replicas, owners)),
         ],
     )
-    inner, outer = pairs_of(owners)
     distant = [to_pair(routed, j) for j in range(1, outer)]
     arrived = [to_sibling(routed)] if inner == 2 else []
+    far_inputs = [exchange(f, "dp", k + 1) for k, f in enumerate(fars)]
+
+    def both_halves(values):
+        return [h for v in values for h in ((v, to_sibling(v)) if inner == 2 else (v,))]
+
+    slope, active, hidden = run(
+        forward_body,
+        "forward",
+        [out((hid, rows), F32), out((hid, rows), F32), out((rows, hid), BF16)],
+        [own_inputs, weights],
+        4 * rows * hid * width,
+    )
+    *distant, hidden = lax.optimization_barrier((*distant, hidden))
     for block in distant:
         arrived.append(block)
         if inner == 2:
             arrived.append(to_sibling(block))
-    far_inputs = [exchange(f, "dp", k + 1) for k, f in enumerate(fars)]
-
-    slope, active, hidden, own_inputs = run(
-        forward_body,
-        "forward",
-        [
-            out((hid, rows), F32),
-            out((hid, rows), F32),
-            out((rows, hid), BF16),
-            out((rows, part), BF16),
-        ],
-        [in_hbm(saved), weights],
-        4 * rows * hid * width,
-        in_specs=[hbm, pl.BlockSpec(memory_space=pltpu.VMEM)],
-        scratch=[
-            pltpu.VMEM((rows, width), BF16),
-            pltpu.SemaphoreType.DMA((owners,)),
-        ],
-    )
-
-    mine = outer * capacity
+
+    fars = run(
+        functools.partial(pack_body, outer),
+        "pack",
+        [out((mine, part), BF16)] * others,
+        [routed, *distant],
+        0,
+    )
+    far_rows = both_halves([exchange(f, "dp", k + 1) for k, f in enumerate(fars)])
+    far_inputs = both_halves(far_inputs)
+
     kept, given, grads = run(
         functools.partial(backward_body, owners),
         "backward",
-        [out((mine, width), BF16)] * 2 + [out((rows, 2 * hid), BF16)],
-        [routed, *arrived, weights, slope, active, *far_inputs],
+        [out((mine, width), BF16)] * 2 + [out((rows, 3 * hid), BF16)],
+        [routed, *arrived, weights, slope, active, hidden],
         6 * rows * hid * width,
     )
     if inner == 2:
         given = to_sibling(given)
     sums = run(
-        functools.partial(pair_body, inner == 2),
+        functools.partial(pair_body, inner == 2, len(far_inputs)),
         "pair_sums",
         [out((capacity, width), BF16)] * (outer - 1),
-        [kept, given],
+        [kept, given, *far_inputs],
         0,
     )
     returned = [to_pair(v, j, back=True) for j, v in enumerate(sums, 1)]
-    own_rows, *fars = run(
-        functools.partial(pack_body, owners),
-        "pack",
-        [out((rows, part), BF16)] + [out((rows, part + 3 * hid), BF16)] * others,
-        [routed, *arrived, hidden, grads, given],
-        0,
-    )
-    far_rows = [exchange(f, "dp", k + 1) for k, f in enumerate(fars)]
+    far_grads = [exchange(grads, "dp", k) for k in range(1, replicas)]
 
     changed = run(
         functools.partial(return_body, inner == 2),
@@ -381,10 +371,10 @@
     columns = min(part, 512)
     pieces = 3 * part // columns
     weight_grads = run(
-        functools.partial(weight_body, others),
+        functools.partial(weight_body, others, owners),
         "weight_grads",
         [out((1, 3, hid, part), BF16)],
-        [hidden, grads, own_inputs, own_rows, *far_inputs, *far_rows],
+        [grads, own_inputs, routed, *arrived, *far_inputs, *far_rows, *far_grads],
         6 * rows * replicas * hid * part,
         out_specs=[hbm],
         scratch=[pltpu.VMEM((pieces, hid, columns), BF16), pltpu.SemaphoreType.DMA((pieces,))],

time: 37.7 us -> 32.9 us (0.87)
  waiting for transfers between devices: 13.2 us -> 6.38 us
  starting transfers between devices: 11 us -> 13.4 us
  Pallas kernels: 12.5 us -> 11.6 us
  local copies, waits for them, and re-layouts: 0.01 us -> 0.68 us
    ppermute x2, waiting for transfers between devices: 6.56 us -> 2.07 us  [to_pair(): lax.ppermute(value, 'expert', [(j, i) for i, j in hops] if back else hops)]
    ppermute x2 -> x3, waiting for transfers between devices: 5.11 us -> 3.49 us  [exchange(): lax.ppermute(value, axis, [(i, partner(i, step, count)) for i in range(co...]
    ppermute x3 -> x5, waiting for transfers between devices: 1.53 us -> 0.01 us  [to_sibling(): lax.ppermute(value, 'expert', [(i, i ^ 1) for i in range(lax.axis_size('e...]
    ppermute x2 -> x3, starting transfers between devices: 3.05 us -> 4.31 us  [exchange(): lax.ppermute(value, axis, [(i, partner(i, step, count)) for i in range(co...]
    pallas_call x8, Pallas kernels: 12.5 us -> 11.6 us  [run(): pl.pallas_call(body, name=name, out_shape=outs, in_specs=in_specs or [vme...]
    ppermute x2, starting transfers between devices: 2.3 us -> 3.17 us  [to_pair(): lax.ppermute(value, 'expert', [(j, i) for i, j in hops] if back else hops)]
    ppermute x2, waiting for transfers between devices: 0.01 us -> 0.81 us  [to_previous(): lax.ppermute(value, 'pipe', [(i, (i - 1) % count) for i in range(count)])]
    unnamed x2, local copies, waits for them, and re-layouts: 0.01 us -> 0.68 us
  transfers between devices with their start and end apart: 9 -> 12, of which waited for: 5 -> 6; matrix products, arithmetic and copies ran while one was open for 0% -> 0% of each run, Pallas kernels for 30% -> 31%
where the time goes in v4:
time: 32.9 us; the launch traced here: 32.7 us
  starting transfers between devices  13.4 us (41%)
  Pallas kernels  11.6 us (35%)
  waiting for transfers between devices  6.38 us (19%)
  between operations  0.69 us (2%)
  local copies, waits for them, and re-layouts  0.68 us (2%)
    pallas_call x8, Pallas kernels, run(): pl.pallas_call(body, name=name, out_shape=outs, in_specs=in_specs or [vme...  11.6 us
    ppermute x2, starting transfers between devices, to_previous(): lax.ppermute(value, 'pipe', [(i, (i - 1) % count) for i in range(count)])  5.6 us
    ppermute x3, starting transfers between devices, exchange(): lax.ppermute(value, axis, [(i, partner(i, step, count)) for i in range(co...  4.31 us
    ppermute x3, waiting for transfers between devices, exchange(): lax.ppermute(value, axis, [(i, partner(i, step, count)) for i in range(co...  3.49 us
    ppermute x2, starting transfers between devices, to_pair(): lax.ppermute(value, 'expert', [(j, i) for i, j in hops] if back else hops)  3.17 us
    ppermute x2, waiting for transfers between devices, to_pair(): lax.ppermute(value, 'expert', [(j, i) for i, j in hops] if back else hops)  2.07 us
    ppermute x2, waiting for transfers between devices, to_previous(): lax.ppermute(value, 'pipe', [(i, (i - 1) % count) for i in range(count)])  0.81 us
    unnamed x2, local copies, waits for them, and re-layouts  0.68 us
  transfers between devices with their start and end apart: 12, of which 6 were waited for; matrix products, arithmetic and copies ran while one was open for 0% of the time, Pallas kernels for 31%

profile of v4, /device:TPU:0, one launch (start us, length us, event | category | flops | bytes accessed | tf_op | source)
XLA Modules:
  0.0 32.7 jit_solution(16398427234053232808)
XLA Ops:
  0.6 5.1 %collective-permute-start = (bf16[128,4096]{1,0:T(8,128)(2,1)}, bf16[128,4096]{1,0:T(8,128)(2,1)S(1)}, u32[]{:S(2)}, u32[]{:S(2)}) collective-permute-start(bf16[128,4096]{1,0:T(8,128)(2,1)} %bitcast.11), channel_id=1, source_target_pairs={{0,12},{4,0},{8,4},{12,8},{1,13},{5,1},{9,5},{13,9},{2,14},{6,2},{... | collective-permute-start | bytes 3145736 | tf_op jit(solution)/shard_map/ppermute | solution.py:61
  5.7 0.0 copy-start
  5.7 2.0 %route.1 = (bf16[16,4096]{1,0:T(8,128)(2,1)S(1)}, bf16[16,4096]{1,0:T(8,128)(2,1)S(1)}, bf16[16,128]{1,0:T(8,128)(2,1)S(1)}, bf16[64,4096]{1,0:T(8,128)(2,1)S(1)}, bf16[32,2048]{1,0:T(8,128)(2,1)S(1)}) custom-call(s32[8,128]{1,0:T(8,128)} %bitcast.14, f32[8,128]{1,0:T(8,128)} %bitcast.15, bf16[128,4096]{1,0:T(8,128)(2,1)} %bitcast.12, ...), custom_call_target="tpu_custom_call" | custom-call | flops 10000000000 | bytes 1581056 | tf_op jit(solution)/shard_map/route/pallas_call | solution.py:71
  7.8 1.6 %collective-permute-start.2 = (bf16[16,4096]{1,0:T(8,128)(2,1)S(1)}, bf16[16,4096]{1,0:T(8,128)(2,1)S(1)}, u32[]{:S(2)}, u32[]{:S(2)}) collective-permute-start(bf16[16,4096]{1,0:T(8,128)(2,1)S(1)} %get-tuple-element.17.refs_0_), channel_id=1, source_target_pairs={{0,2},{1,3},{2,0},{3,1},{4,6},{5,7},{6,4},{7,5},{8,10},{9,11},{10,... | collective-permute-start | bytes 393224 | tf_op jit(solution)/shard_map/ppermute | solution.py:56
  9.4 0.0 collective-permute-start.1
  9.4 0.7 %copy-done = bf16[1,3,384,4096]{3,2,1,0:T(8,128)(2,1)S(1)} copy-done((bf16[1,3,384,4096]{3,2,1,0:T(8,128)(2,1)S(1)}, bf16[1,3,384,4096]{3,2,1,0:T(8,128)(2,1)}, u32[]{:S(2)}) %copy-start) | copy-done | bytes 9437208
  10.1 1.8 %forward.1 = (f32[384,64]{1,0:T(8,128)S(1)}, f32[384,64]{1,0:T(8,128)S(1)}, bf16[64,384]{1,0:T(8,128)(2,1)S(1)}) custom-call(bf16[64,4096]{1,0:T(8,128)(2,1)S(1)} %get-tuple-element.18.rows_ref.inputs_ref, bf16[3,384,4096]{2,1,0:T(8,128)(2,1)S(1)} %bitcast.9), custom_call_target="tpu_custom_call" | custom-call | flops 402653184 | bytes 9961472 | tf_op jit(solution)/shard_map/forward/pallas_call | solution.py:71
  11.9 0.9 %collective-permute-done.2.refs_2_.refs_1_ = bf16[16,4096]{1,0:T(8,128)(2,1)S(1)} collective-permute-done((bf16[16,4096]{1,0:T(8,128)(2,1)S(1)}, bf16[16,4096]{1,0:T(8,128)(2,1)S(1)}, u32[]{:S(2)}, u32[]{:S(2)}) %collective-permute-start.2) | collective-permute-done | bytes 131104 | tf_op jit(solution)/shard_map/ppermute | solution.py:56
  12.8 0.0 collective-permute-start.3
  12.8 1.5 %collective-permute-start.5 = (bf16[32,2048]{1,0:T(8,128)(2,1)S(1)}, bf16[32,2048]{1,0:T(8,128)(2,1)S(1)}, u32[]{:S(2)}, u32[]{:S(2)}) collective-permute-start(bf16[32,2048]{1,0:T(8,128)(2,1)S(1)} %get-tuple-element.26), channel_id=1, source_target_pairs={{0,16},{16,0},{1,17},{17,1},{2,18},{18,2},{3,19},{19,3},{4,20},{20... | collective-permute-start | bytes 393224 | tf_op jit(solution)/shard_map/ppermute | solution.py:45
  14.3 0.0 collective-permute-done.1.refs_1_
  14.3 0.0 collective-permute-done.3.refs_3_
  14.3 3.6 %backward.1 = (bf16[32,4096]{1,0:T(8,128)(2,1)S(1)}, bf16[32,4096]{1,0:T(8,128)(2,1)S(1)}, bf16[64,1152]{1,0:T(8,128)(2,1)S(1)}) custom-call(bf16[16,4096]{1,0:T(8,128)(2,1)S(1)} %get-tuple-element.17.refs_0_, bf16[16,4096]{1,0:T(8,128)(2,1)S(1)} %collective-permute-done.1.refs_1_, bf16[16,4096]{1,0:T(8,128)(2,1)S(1)} %collective-permute-done.2.refs_2_.refs_1_, ...), custom_call_target="tpu_custom_call" | custom-call | flops 603979776 | bytes 10207232 | tf_op jit(solution)/shard_map/backward/pallas_call | solution.py:71
  17.9 0.3 collective-permute-start.4
  18.2 0.5 %collective-permute-done.5.refs_0_.refs_4_ = bf16[32,2048]{1,0:T(8,128)(2,1)S(1)} collective-permute-done((bf16[32,2048]{1,0:T(8,128)(2,1)S(1)}, bf16[32,2048]{1,0:T(8,128)(2,1)S(1)}, u32[]{:S(2)}, u32[]{:S(2)}) %collective-permute-start.5) | collective-permute-done | bytes 131104 | tf_op jit(solution)/shard_map/ppermute | solution.py:45
  18.7 0.0 collective-permute-start.6
  18.7 1.6 %collective-permute-start.9 = (bf16[32,2048]{1,0:T(8,128)(2,1)S(1)}, bf16[32,2048]{1,0:T(8,128)(2,1)S(1)}, u32[]{:S(2)}, u32[]{:S(2)}) collective-permute-start(bf16[32,2048]{1,0:T(8,128)(2,1)S(1)} %pack.1), channel_id=1, source_target_pairs={{0,16},{16,0},{1,17},{17,1},{2,18},{18,2},{3,19},{19,3},{4,20},{20... | collective-permute-start | bytes 393224 | tf_op jit(solution)/shard_map/ppermute | solution.py:45
  20.3 0.0 collective-permute-done.6.refs_1_.refs_5_
  20.3 0.0 collective-permute-done.4.given_ref
  20.3 1.6 %collective-permute-start.7 = (bf16[16,4096]{1,0:T(8,128)(2,1)S(1)}, bf16[16,4096]{1,0:T(8,128)(2,1)S(1)}, u32[]{:S(2)}, u32[]{:S(2)}) collective-permute-start(bf16[16,4096]{1,0:T(8,128)(2,1)S(1)} %pair_sums.1), channel_id=1, source_target_pairs={{2,0},{3,1},{0,2},{1,3},{6,4},{7,5},{4,6},{5,7},{10,8},{11,9},{8,1... | collective-permute-start | bytes 393224 | tf_op jit(solution)/shard_map/ppermute | solution.py:56
  21.9 1.3 %collective-permute-start.11 = (bf16[64,1152]{1,0:T(8,128)(2,1)S(1)}, bf16[64,1152]{1,0:T(8,128)(2,1)S(1)}, u32[]{:S(2)}, u32[]{:S(2)}) collective-permute-start(bf16[64,1152]{1,0:T(8,128)(2,1)S(1)} %get-tuple-element.27.factors_ref), channel_id=1, source_target_pairs={{0,16},{16,0},{1,17},{17,1},{2,18},{18,2},{3,19},{19,3},{4,20},{20... | collective-permute-start | bytes 442376 | tf_op jit(solution)/shard_map/ppermute | solution.py:45
  23.2 1.7 %collective-permute-done.9.refs_6_ = bf16[32,2048]{1,0:T(8,128)(2,1)S(1)} collective-permute-done((bf16[32,2048]{1,0:T(8,128)(2,1)S(1)}, bf16[32,2048]{1,0:T(8,128)(2,1)S(1)}, u32[]{:S(2)}, u32[]{:S(2)}) %collective-permute-start.9) | collective-permute-done | bytes 131104 | tf_op jit(solution)/shard_map/ppermute | solution.py:45
  24.9 0.0 collective-permute-start.10
  24.9 1.1 %collective-permute-done.7.refs_0_ = bf16[16,4096]{1,0:T(8,128)(2,1)S(1)} collective-permute-done((bf16[16,4096]{1,0:T(8,128)(2,1)S(1)}, bf16[16,4096]{1,0:T(8,128)(2,1)S(1)}, u32[]{:S(2)}, u32[]{:S(2)}) %collective-permute-start.7) | collective-permute-done | bytes 131104 | tf_op jit(solution)/shard_map/ppermute | solution.py:56
  26.0 0.1 sum_returned.1
  26.1 0.5 %collective-permute-start.8 = (bf16[16,4224]{1,0:T(8,128)(2,1)S(1)}, bf16[16,4224]{1,0:T(8,128)(2,1)S(1)}, u32[]{:S(2)}, u32[]{:S(2)}) collective-permute-start(bf16[16,4224]{1,0:T(8,128)(2,1)S(1)} %sum_returned.1), channel_id=1, source_target_pairs={{0,12},{4,0},{8,4},{12,8},{1,13},{5,1},{9,5},{13,9},{2,14},{6,2},{... | collective-permute-start | bytes 405512 | tf_op jit(solution)/shard_map/ppermute | solution.py:61
  26.6 0.0 collective-permute-done.10.refs_7_
  26.6 1.3 %collective-permute-done.11.refs_8_ = bf16[64,1152]{1,0:T(8,128)(2,1)S(1)} collective-permute-done((bf16[64,1152]{1,0:T(8,128)(2,1)S(1)}, bf16[64,1152]{1,0:T(8,128)(2,1)S(1)}, u32[]{:S(2)}, u32[]{:S(2)}) %collective-permute-start.11) | collective-permute-done | bytes 147488 | tf_op jit(solution)/shard_map/ppermute | solution.py:45
  27.9 2.6 %weight_grads.1 = bf16[1,3,384,2048]{3,2,1,0:T(8,128)(2,1)} custom-call(bf16[64,1152]{1,0:T(8,128)(2,1)S(1)} %get-tuple-element.27.factors_ref, bf16[64,4096]{1,0:T(8,128)(2,1)S(1)} %get-tuple-element.18.rows_ref.inputs_ref, bf16[16,4096]{1,0:T(8,128)(2,1)S(1)} %get-tuple-element.17.refs_0_, bf16[16,4096]{1,0:T(8,128)(2,1)S(1)} %collective-permute-done.1.refs_1_, ...), custom_call_target="tpu_custom_call" | custom-call | flops 603979776 | bytes 1867776 | tf_op jit(solution)/shard_map/weight_grads/pallas_call | solution.py:71
  30.4 0.8 %collective-permute-done.8.changed_ref = bf16[16,4224]{1,0:T(8,128)(2,1)S(1)} collective-permute-done((bf16[16,4224]{1,0:T(8,128)(2,1)S(1)}, bf16[16,4224]{1,0:T(8,128)(2,1)S(1)}, u32[]{:S(2)}, u32[]{:S(2)}) %collective-permute-start.8) | collective-permute-done | bytes 135200 | tf_op jit(solution)/shard_map/ppermute | solution.py:61
  31.3 0.0 collective-permute-done.shifted_ref
  31.3 1.5 %merge.1 = bf16[1,1,128,4096]{3,2,1,0:T(8,128)(2,1)} custom-call(bf16[128,4096]{1,0:T(8,128)(2,1)S(1)} %collective-permute-done.shifted_ref, bf16[16,4224]{1,0:T(8,128)(2,1)S(1)} %collective-permute-done.8.changed_ref), custom_call_target="tpu_custom_call" | custom-call | flops 16777216 | bytes 1183744 | tf_op jit(solution)/shard_map/merge/pallas_call | solution.py:71
  (2 shorter events, 0.0 us)
Async XLA Ops:
  0.6 30.6 %collective-permute-start = (bf16[128,4096]{1,0:T(8,128)(2,1)}, bf16[128,4096]{1,0:T(8,128)(2,1)S(1)}, u32[]{:S(2)}, u32[]{:S(2)}) collective-permute-start(bf16[128,4096]{1,0:T(8,128)(2,1)} %bitcast.11), channel_id=1, source_target_pairs={{0,12},{4,0},{8,4},{12,8},{1,13},{5,1},{9,5},{13,9},{2,14},{6,2},{... | collective-permute-start | bytes 3145736 | tf_op jit(solution)/shard_map/ppermute | solution.py:61
  5.7 4.3 %copy-start = (bf16[1,3,384,4096]{3,2,1,0:T(8,128)(2,1)S(1)}, bf16[1,3,384,4096]{3,2,1,0:T(8,128)(2,1)}, u32[]{:S(2)}) copy-start(bf16[1,3,384,4096]{3,2,1,0:T(8,128)(2,1)} %param.9) | copy-start | bytes 28311556
  7.8 5.0 %collective-permute-start.2 = (bf16[16,4096]{1,0:T(8,128)(2,1)S(1)}, bf16[16,4096]{1,0:T(8,128)(2,1)S(1)}, u32[]{:S(2)}, u32[]{:S(2)}) collective-permute-start(bf16[16,4096]{1,0:T(8,128)(2,1)S(1)} %get-tuple-element.17.refs_0_), channel_id=1, source_target_pairs={{0,2},{1,3},{2,0},{3,1},{4,6},{5,7},{6,4},{7,5},{8,10},{9,11},{10,... | collective-permute-start | bytes 393224 | tf_op jit(solution)/shard_map/ppermute | solution.py:56
  9.4 4.9 %collective-permute-start.1 = (bf16[16,4096]{1,0:T(8,128)(2,1)S(1)}, bf16[16,4096]{1,0:T(8,128)(2,1)S(1)}, u32[]{:S(2)}, u32[]{:S(2)}) collective-permute-start(bf16[16,4096]{1,0:T(8,128)(2,1)S(1)} %get-tuple-element.17.refs_0_), channel_id=1, source_target_pairs={{0,1},{1,0},{2,3},{3,2},{4,5},{5,4},{6,7},{7,6},{8,9},{9,8},{10,11... | collective-permute-start | bytes 393224 | tf_op jit(solution)/shard_map/ppermute | solution.py:49
  12.8 1.5 %collective-permute-start.3 = (bf16[16,4096]{1,0:T(8,128)(2,1)S(1)}, bf16[16,4096]{1,0:T(8,128)(2,1)S(1)}, u32[]{:S(2)}, u32[]{:S(2)}) collective-permute-start(bf16[16,4096]{1,0:T(8,128)(2,1)S(1)} %collective-permute-done.2.refs_2_.refs_1_), channel_id=1, source_target_pairs={{0,1},{1,0},{2,3},{3,2},{4,5},{5,4},{6,7},{7,6},{8,9},{9,8},{10,11... | collective-permute-start | bytes 393224 | tf_op jit(solution)/shard_map/ppermute | solution.py:49
  12.8 5.9 %collective-permute-start.5 = (bf16[32,2048]{1,0:T(8,128)(2,1)S(1)}, bf16[32,2048]{1,0:T(8,128)(2,1)S(1)}, u32[]{:S(2)}, u32[]{:S(2)}) collective-permute-start(bf16[32,2048]{1,0:T(8,128)(2,1)S(1)} %get-tuple-element.26), channel_id=1, source_target_pairs={{0,16},{16,0},{1,17},{17,1},{2,18},{18,2},{3,19},{19,3},{4,20},{20... | collective-permute-start | bytes 393224 | tf_op jit(solution)/shard_map/ppermute | solution.py:45
  17.9 2.4 %collective-permute-start.4 = (bf16[32,4096]{1,0:T(8,128)(2,1)S(1)}, bf16[32,4096]{1,0:T(8,128)(2,1)S(1)}, u32[]{:S(2)}, u32[]{:S(2)}) collective-permute-start(bf16[32,4096]{1,0:T(8,128)(2,1)S(1)} %get-tuple-element.25), channel_id=1, source_target_pairs={{0,1},{1,0},{2,3},{3,2},{4,5},{5,4},{6,7},{7,6},{8,9},{9,8},{10,11... | collective-permute-start | bytes 786440 | tf_op jit(solution)/shard_map/ppermute | solution.py:49
  18.7 1.6 %collective-permute-start.6 = (bf16[32,2048]{1,0:T(8,128)(2,1)S(1)}, bf16[32,2048]{1,0:T(8,128)(2,1)S(1)}, u32[]{:S(2)}, u32[]{:S(2)}) collective-permute-start(bf16[32,2048]{1,0:T(8,128)(2,1)S(1)} %collective-permute-done.5.refs_0_.refs_4_), channel_id=1, source_target_pairs={{0,1},{1,0},{2,3},{3,2},{4,5},{5,4},{6,7},{7,6},{8,9},{9,8},{10,11... | collective-permute-start | bytes 393224 | tf_op jit(solution)/shard_map/ppermute | solution.py:49
  18.7 6.2 %collective-permute-start.9 = (bf16[32,2048]{1,0:T(8,128)(2,1)S(1)}, bf16[32,2048]{1,0:T(8,128)(2,1)S(1)}, u32[]{:S(2)}, u32[]{:S(2)}) collective-permute-start(bf16[32,2048]{1,0:T(8,128)(2,1)S(1)} %pack.1), channel_id=1, source_target_pairs={{0,16},{16,0},{1,17},{17,1},{2,18},{18,2},{3,19},{19,3},{4,20},{20... | collective-permute-start | bytes 393224 | tf_op jit(solution)/shard_map/ppermute | solution.py:45
  20.3 5.7 %collective-permute-start.7 = (bf16[16,4096]{1,0:T(8,128)(2,1)S(1)}, bf16[16,4096]{1,0:T(8,128)(2,1)S(1)}, u32[]{:S(2)}, u32[]{:S(2)}) collective-permute-start(bf16[16,4096]{1,0:T(8,128)(2,1)S(1)} %pair_sums.1), channel_id=1, source_target_pairs={{2,0},{3,1},{0,2},{1,3},{6,4},{7,5},{4,6},{5,7},{10,8},{11,9},{8,1... | collective-permute-start | bytes 393224 | tf_op jit(solution)/shard_map/ppermute | solution.py:56
  21.9 5.9 %collective-permute-start.11 = (bf16[64,1152]{1,0:T(8,128)(2,1)S(1)}, bf16[64,1152]{1,0:T(8,128)(2,1)S(1)}, u32[]{:S(2)}, u32[]{:S(2)}) collective-permute-start(bf16[64,1152]{1,0:T(8,128)(2,1)S(1)} %get-tuple-element.27.factors_ref), channel_id=1, source_target_pairs={{0,16},{16,0},{1,17},{17,1},{2,18},{18,2},{3,19},{19,3},{4,20},{20... | collective-permute-start | bytes 442376 | tf_op jit(solution)/shard_map/ppermute | solution.py:45
  24.9 1.7 %collective-permute-start.10 = (bf16[32,2048]{1,0:T(8,128)(2,1)S(1)}, bf16[32,2048]{1,0:T(8,128)(2,1)S(1)}, u32[]{:S(2)}, u32[]{:S(2)}) collective-permute-start(bf16[32,2048]{1,0:T(8,128)(2,1)S(1)} %collective-permute-done.9.refs_6_), channel_id=1, source_target_pairs={{0,1},{1,0},{2,3},{3,2},{4,5},{5,4},{6,7},{7,6},{8,9},{9,8},{10,11... | collective-permute-start | bytes 393224 | tf_op jit(solution)/shard_map/ppermute | solution.py:49
  26.1 5.1 %collective-permute-start.8 = (bf16[16,4224]{1,0:T(8,128)(2,1)S(1)}, bf16[16,4224]{1,0:T(8,128)(2,1)S(1)}, u32[]{:S(2)}, u32[]{:S(2)}) collective-permute-start(bf16[16,4224]{1,0:T(8,128)(2,1)S(1)} %sum_returned.1), channel_id=1, source_target_pairs={{0,12},{4,0},{8,4},{12,8},{1,13},{5,1},{9,5},{13,9},{2,14},{6,2},{... | collective-permute-start | bytes 405512 | tf_op jit(solution)/shard_map/ppermute | solution.py:61

commit v5 on v4

--- a/solution.py
+++ b/solution.py
@@ -11,7 +11,6 @@
 F32 = jnp.float32
 LANES = 128
 VMEM_LIMIT = 20 * 2**20
-SUM_COST = 0
 ROUTE_COST = 10**10
 LAST_LAST = (((1,), (1,)), ((), ()))
 FIRST_FIRST = (((0,), (0,)), ((), ()))
@@ -65,7 +64,7 @@
     return lax.dot_general(left, right, dims, preferred_element_type=F32)
 
 
-def run(body, name, outs, inputs, flops, in_specs=None, out_specs=None, scratch=()):
+def run(body, name, outs, inputs, flops, in_specs=None, out_specs=None, scratch=(), aliases=None):
     vmem = pl.BlockSpec(memory_space=pltpu.VMEM)
     moved = sum(v.size * v.dtype.itemsize for v in inputs)
     return pl.pallas_call(
@@ -75,6 +74,7 @@
         in_specs=in_specs or [vmem] * len(inputs),
         out_specs=out_specs or [vmem] * len(outs),
         scratch_shapes=scratch,
+        input_output_aliases=aliases or {},
         compiler_params=pltpu.CompilerParams(vmem_limit_bytes=VMEM_LIMIT),
         cost_estimate=pl.CostEstimate(flops=flops, bytes_accessed=moved, transcendentals=0),
     )(*inputs)
@@ -84,17 +84,37 @@
     return pltpu.with_memory_space_constraint(value, pltpu.HBM)
 
 
-def route_body(routing_hbm, gates_hbm, incoming_hbm, saved_hbm, *refs):
-    others = lax.axis_size("dp") - 1
-    owners = lax.axis_size("expert")
-    inner, _ = pairs_of(owners)
-    routed_ref, picked_ref, ids_ref, rows_ref = refs[:4]
-    fars = refs[4 : 4 + others]
-    routing_ref, gates_ref, incoming_ref, sems, far_sem = refs[4 + others :]
-    capacity = routed_ref.shape[0]
-    tokens, width = incoming_ref.shape
-    me = lax.axis_index("expert")
-    replica = lax.axis_index("dp")
+def earlier_count(flags):
+    lanes = flags.shape[1]
+    before = lax.broadcasted_iota(jnp.int32, (lanes, lanes), 0) < lax.broadcasted_iota(jnp.int32, (lanes, lanes), 1)
+    return mm(flags.astype(BF16), jnp.where(before, F32(1.0), F32(0.0)).astype(BF16), ROWS_COLS)
+
+
+def one_hot(wanted, rows, valid):
+    number = lax.broadcasted_iota(jnp.int32, (rows, wanted.shape[1]), 0).astype(F32)
+    return jnp.where((number == wanted[:1]) & (valid[:1] > 0.5), F32(1.0), F32(0.0))
+
+
+def choose_late(routing, gates, capacity):
+    tokens = routing.shape[1]
+    matches = routing == 0
+    member = jnp.max(jnp.where(matches, F32(1.0), F32(0.0)), axis=0, keepdims=True)
+    share = jnp.sum(jnp.where(matches, gates, F32(0.0)), axis=0, keepdims=True)
+    spread = jnp.broadcast_to(member, (capacity, tokens))
+    slot = earlier_count(spread)
+    members = jnp.sum(spread, axis=1, keepdims=True)
+    rank = lax.broadcasted_iota(jnp.int32, (capacity, tokens), 1).astype(F32) - slot
+    left = rank - F32(tokens - capacity)
+    is_late = jnp.where((spread > 0.5) | (left >= 0.0), F32(1.0), F32(0.0))
+    chosen = one_hot(jnp.where(spread > 0.5, slot, members + left), capacity, is_late)
+    weighting = jnp.sum(chosen * share, axis=1, keepdims=True)
+    return chosen, weighting, one_hot(rank, tokens - capacity, 1.0 - is_late)
+
+
+def route_body(
+    routing_hbm, gates_hbm, incoming_hbm, early_ref, routed_ref, picked_ref, ids_ref, routing_ref, gates_ref, incoming_ref, sems
+):
+    capacity, width = routed_ref.shape
     fetches = [
         pltpu.make_async_copy(routing_hbm, routing_ref, sems.at[0]),
         pltpu.make_async_copy(gates_hbm, gates_ref, sems.at[1]),
@@ -102,54 +122,39 @@
     ]
     for f in fetches:
         f.start()
-    copies = [
-        pltpu.make_async_copy(
-            saved_hbm.at[source(me, k, owners)], rows_ref.at[pl.ds(k * capacity, capacity)], far_sem.at[others, k]
-        )
-        for k in range(owners)
-    ]
+    for f in fetches[:2]:
+        f.wait()
+    chosen, weighting, kept = choose_late(routing_ref[...], gates_ref[...], capacity)
+    both = jnp.concatenate([kept, chosen], axis=0).astype(BF16)
+    early = early_ref.shape[0]
+    fetches[2].wait()
+    step = min(width, 1024)
+    for c in range(width // step):
+        at = slice(c * step, (c + 1) * step)
+        sorted_rows = mm(both, incoming_ref[:, at], ROWS_COLS)
+        early_ref[:, at] = sorted_rows[:early].astype(BF16)
+        picked_ref[:, at] = sorted_rows[early:].astype(BF16)
+        routed_ref[:, at] = (sorted_rows[early:] * weighting).astype(BF16)
+    token = lax.broadcasted_iota(jnp.int32, chosen.shape, 1)
+    high = jnp.sum(chosen * (token // LANES).astype(F32), axis=1, keepdims=True)
+    low = jnp.sum(chosen * (token % LANES).astype(F32), axis=1, keepdims=True)
+    lane = lax.broadcasted_iota(jnp.int32, ids_ref.shape, 1)
+    ids_ref[...] = jnp.where(lane == 0, high, jnp.where(lane == 1, low, F32(0.0))).astype(BF16)
+
+
+def forward_body(saved_ref, weights_ref, slope_ref, active_ref, hidden_ref, rows_ref, *fars):
+    owners, capacity, _ = saved_ref.shape
+    others = len(fars)
+    inner, outer = pairs_of(owners)
+    me = lax.axis_index("expert")
+    replica = lax.axis_index("dp")
+    for k in range(owners):
+        rows_ref[k * capacity : (k + 1) * capacity] = saved_ref[source(me, k, owners)]
     for r in range(others):
         part = fars[r].shape[1]
         first = pl.multiple_of(partner(replica, r + 1, others + 1) * part, LANES)
-        for j in range(owners // inner):
-            copies.append(
-                pltpu.make_async_copy(
-                    saved_hbm.at[source(me, j * inner, owners), :, pl.ds(first, part)],
-                    fars[r].at[pl.ds(j * capacity, capacity)],
-                    far_sem.at[r, j],
-                )
-            )
-    for c in copies:
-        c.start()
-    fetches[0].wait()
-    fetches[1].wait()
-    matches = routing_ref[...] == 0
-    member = jnp.max(jnp.where(matches, F32(1.0), F32(0.0)), axis=0, keepdims=True)
-    share = jnp.sum(jnp.where(matches, gates_ref[...], F32(0.0)), axis=0, keepdims=True)
-    earlier = lax.broadcasted_iota(jnp.int32, (tokens, tokens), 0) < lax.broadcasted_iota(
-        jnp.int32, (tokens, tokens), 1
-    )
-    spread = jnp.broadcast_to(member, (capacity, tokens))
-    slot = mm(spread.astype(BF16), jnp.where(earlier, F32(1.0), F32(0.0)).astype(BF16), ROWS_COLS)
-    wanted = lax.broadcasted_iota(jnp.int32, (capacity, tokens), 0).astype(F32)
-    chosen = jnp.where((slot == wanted) & (spread > 0.5), F32(1.0), F32(0.0))
-    weighting = jnp.sum(chosen * share, axis=1, keepdims=True)
-    token = lax.broadcasted_iota(jnp.int32, (capacity, tokens), 1)
-    filled = jnp.sum(chosen, axis=1, keepdims=True)
-    high = jnp.sum(chosen * (token // LANES).astype(F32), axis=1, keepdims=True)
-    low = jnp.sum(chosen * (token % LANES).astype(F32), axis=1, keepdims=True)
-    high = jnp.where(filled > 0.5, high, F32(-1.0))
-    lane = lax.broadcasted_iota(jnp.int32, (capacity, LANES), 1)
-    ids_ref[...] = jnp.where(lane == 0, high, jnp.where(lane == 1, low, F32(0.0))).astype(BF16)
-    fetches[2].wait()
-    picked = mm(chosen.astype(BF16), incoming_ref[...], ROWS_COLS)
-    routed_ref[...] = (picked * weighting).astype(BF16)
-    picked_ref[...] = picked.astype(BF16)
-    for c in copies:
-        c.wait()
-
-
-def forward_body(rows_ref, weights_ref, slope_ref, active_ref, hidden_ref):
+        for j in range(outer):
+            fars[r][j * capacity : (j + 1) * capacity] = saved_ref[source(me, j * inner, owners), :, pl.ds(first, part)]
     rows = rows_ref[...]
     gate_pre = mm(weights_ref[0], rows, LAST_LAST)
     up_pre = mm(weights_ref[1], rows, LAST_LAST)
@@ -253,20 +258,23 @@
         c.wait()
 
 
-def merge_body(shifted_ref, changed_ref, out_hbm, held, sems):
-    tokens, width = shifted_ref.shape
+def merge_body(early_ref, changed_ref, out_hbm, held, sems):
+    early, width = early_ref.shape
     capacity = changed_ref.shape[0]
+    tokens = early + capacity
     high = changed_ref[:, width : width + 1].astype(F32)
     low = changed_ref[:, width + 1 : width + 2].astype(F32)
     token = lax.broadcasted_iota(jnp.int32, (capacity, tokens), 1).astype(F32)
-    chosen = jnp.where(token == high * F32(LANES) + low, F32(1.0), F32(0.0)).astype(BF16)
-    here = mm(chosen, jnp.ones((capacity, LANES), BF16), FIRST_FIRST)[:, :1] > 0.5
+    chosen = jnp.where(token == high * F32(LANES) + low, F32(1.0), F32(0.0))
+    is_late = jnp.broadcast_to(jnp.sum(chosen, axis=0, keepdims=True), (capacity, tokens))
+    kept = one_hot(token - earlier_count(is_late), early, 1.0 - is_late)
+    both = jnp.concatenate([kept, chosen], axis=0).astype(BF16)
     step = held.shape[2]
     copies = []
     for c in range(width // step):
         at = slice(c * step, (c + 1) * step)
-        placed = mm(chosen, changed_ref[:, at], FIRST_FIRST)
-        held[c] = jnp.where(here, placed, shifted_ref[:, at].astype(F32)).astype(BF16)
+        rows = jnp.concatenate([early_ref[:, at], changed_ref[:, at]], axis=0)
+        held[c] = mm(both, rows, FIRST_FIRST).astype(BF16)
         copies.append(pltpu.make_async_copy(held.at[c], out_hbm.at[0, 0, :, pl.ds(c * step, step)], sems.at[c]))
         copies[-1].start()
     for c in copies:
@@ -291,39 +299,42 @@
     hbm = pl.BlockSpec(memory_space=pltpu.HBM)
     saved = saved_inputs[0, 0, 0]
 
-    shifted = to_previous(incoming)
-
-    routed, picked, ids, own_inputs, *fars = run(
+    early = tokens - capacity
+    early_rows, routed, picked, ids = run(
         route_body,
         "route",
-        [out((capacity, width), BF16), out((capacity, width), BF16), out((capacity, LANES), BF16)]
-        + [out((rows, width), BF16)]
-        + [out((mine, part), BF16)] * others,
-        [in_hbm(v) for v in (jnp.transpose(routing[0, 0]), jnp.transpose(gate_values[0, 0]), incoming, saved)],
+        [
+            out((early, width), BF16),
+            out((capacity, width), BF16),
+            out((capacity, width), BF16),
+            out((capacity, LANES), BF16),
+        ],
+        [in_hbm(v) for v in (jnp.transpose(routing[0, 0]), jnp.transpose(gate_values[0, 0]), incoming)],
         ROUTE_COST,
-        in_specs=[hbm] * 4,
+        in_specs=[hbm] * 3,
         scratch=[
             pltpu.VMEM((top, tokens), jnp.int32),
             pltpu.VMEM((top, tokens), F32),
             pltpu.VMEM((tokens, width), BF16),
             pltpu.SemaphoreType.DMA((3,)),
-            pltpu.SemaphoreType.DMA((replicas, owners)),
         ],
     )
+    shifted = to_previous(early_rows)
     distant = [to_pair(routed, j) for j in range(1, outer)]
     arrived = [to_sibling(routed)] if inner == 2 else []
-    far_inputs = [exchange(f, "dp", k + 1) for k, f in enumerate(fars)]
 
     def both_halves(values):
         return [h for v in values for h in ((v, to_sibling(v)) if inner == 2 else (v,))]
 
-    slope, active, hidden = run(
+    slope, active, hidden, own_inputs, *fars = run(
         forward_body,
         "forward",
-        [out((hid, rows), F32), out((hid, rows), F32), out((rows, hid), BF16)],
-        [own_inputs, weights],
+        [out((hid, rows), F32), out((hid, rows), F32), out((rows, hid), BF16), out((rows, width), BF16)]
+        + [out((mine, part), BF16)] * others,
+        [saved, weights],
         4 * rows * hid * width,
     )
+    far_inputs = [exchange(f, "dp", k + 1) for k, f in enumerate(fars)]
     *distant, hidden = lax.optimization_barrier((*distant, hidden))
     for block in distant:
         arrived.append(block)
@@ -364,7 +375,7 @@
         "sum_returned",
         [out((capacity, width + LANES), BF16)],
         [picked, ids, kept, given, *returned],
-        SUM_COST,
+        0,
     )[0]
     next_changed = to_previous(changed)
 

time: 32.9 us -> 32.6 us (level)
  local copies, waits for them, and re-layouts: 0.68 us -> 0.01 us
  waiting for transfers between devices: 6.38 us -> 6.96 us
    unnamed x2 -> x4, local copies, waits for them, and re-layouts: 0.68 us -> 0.01 us
    ppermute x2, waiting for transfers between devices: 2.07 us -> 2.73 us  [to_pair(): lax.ppermute(value, 'expert', [(j, i) for i, j in hops] if back else hops)]
  transfers between devices with their start and end apart: 12 -> 12, of which waited for: 6 -> 6; matrix products, arithmetic and copies ran while one was open for 0% -> 0% of each run, Pallas kernels for 31% -> 25%
where the time goes in v5:
time: 32.6 us; the launch traced here: 32.5 us
  starting transfers between devices  13.3 us (41%)
  Pallas kernels  11.5 us (35%)
  waiting for transfers between devices  6.96 us (21%)
  between operations  0.7 us (2%)
    pallas_call x8, Pallas kernels, run(): pl.pallas_call(body, name=name, out_shape=outs, in_specs=in_specs or [vme...  11.5 us
    ppermute x2, starting transfers between devices, to_previous(): lax.ppermute(value, 'pipe', [(i, (i - 1) % count) for i in range(count)])  5.6 us
    ppermute x3, starting transfers between devices, exchange(): lax.ppermute(value, axis, [(i, partner(i, step, count)) for i in range(co...  4.31 us
    ppermute x3, waiting for transfers between devices, exchange(): lax.ppermute(value, axis, [(i, partner(i, step, count)) for i in range(co...  3.49 us
    ppermute x2, starting transfers between devices, to_pair(): lax.ppermute(value, 'expert', [(j, i) for i, j in hops] if back else hops)  3.1 us
    ppermute x2, waiting for transfers between devices, to_pair(): lax.ppermute(value, 'expert', [(j, i) for i, j in hops] if back else hops)  2.73 us
    ppermute x2, waiting for transfers between devices, to_previous(): lax.ppermute(value, 'pipe', [(i, (i - 1) % count) for i in range(count)])  0.73 us
  transfers between devices with their start and end apart: 12, of which 6 were waited for; matrix products, arithmetic and copies ran while one was open for 0% of the time, Pallas kernels for 25%

profile of v5, /device:TPU:0, one launch (start us, length us, event | category | flops | bytes accessed | tf_op | source)
XLA Modules:
  0.0 32.5 jit_solution(3830141521701663044)
XLA Ops:
  0.6 0.0 copy-start
  0.6 0.0 copy-start.1
  0.7 1.9 %route.1 = (bf16[112,4096]{1,0:T(8,128)(2,1)S(1)}, bf16[16,4096]{1,0:T(8,128)(2,1)S(1)}, bf16[16,4096]{1,0:T(8,128)(2,1)S(1)}, bf16[16,128]{1,0:T(8,128)(2,1)S(1)}) custom-call(s32[8,128]{1,0:T(8,128)} %bitcast.13, f32[8,128]{1,0:T(8,128)} %bitcast.14, bf16[128,4096]{1,0:T(8,128)(2,1)} %bitcast.12), custom_call_target="tpu_custom_call" | custom-call | flops 10000000000 | bytes 1056768 | tf_op jit(solution)/shard_map/route/pallas_call | solution.py:70
  2.5 5.1 %collective-permute-start = (bf16[112,4096]{1,0:T(8,128)(2,1)S(1)}, bf16[112,4096]{1,0:T(8,128)(2,1)S(1)}, u32[]{:S(2)}, u32[]{:S(2)}) collective-permute-start(bf16[112,4096]{1,0:T(8,128)(2,1)S(1)} %get-tuple-element.16), channel_id=1, source_target_pairs={{0,12},{4,0},{8,4},{12,8},{1,13},{5,1},{9,5},{13,9},{2,14},{6,2},{... | collective-permute-start | bytes 2752520 | tf_op jit(solution)/shard_map/ppermute | solution.py:60
  7.6 1.5 %collective-permute-start.2 = (bf16[16,4096]{1,0:T(8,128)(2,1)S(1)}, bf16[16,4096]{1,0:T(8,128)(2,1)S(1)}, u32[]{:S(2)}, u32[]{:S(2)}) collective-permute-start(bf16[16,4096]{1,0:T(8,128)(2,1)S(1)} %get-tuple-element.19.refs_0_), channel_id=1, source_target_pairs={{0,2},{1,3},{2,0},{3,1},{4,6},{5,7},{6,4},{7,5},{8,10},{9,11},{10,... | collective-permute-start | bytes 393224 | tf_op jit(solution)/shard_map/ppermute | solution.py:55
  9.1 0.0 collective-permute-start.1
  9.2 0.0 copy-done
  9.2 0.0 copy-done.1
  9.2 1.8 %forward.1 = (f32[384,64]{1,0:T(8,128)S(1)}, f32[384,64]{1,0:T(8,128)S(1)}, bf16[64,384]{1,0:T(8,128)(2,1)S(1)}, bf16[64,4096]{1,0:T(8,128)(2,1)S(1)}, bf16[32,2048]{1,0:T(8,128)(2,1)S(1)}) custom-call(bf16[4,16,4096]{2,1,0:T(8,128)(2,1)S(1)} %bitcast.11, bf16[3,384,4096]{2,1,0:T(8,128)(2,1)S(1)} %bitcast.9), custom_call_target="tpu_custom_call" | custom-call | flops 402653184 | bytes 9961472 | tf_op jit(solution)/shard_map/forward/pallas_call | solution.py:70
  11.0 1.6 %collective-permute-done.2.refs_2_.refs_1_ = bf16[16,4096]{1,0:T(8,128)(2,1)S(1)} collective-permute-done((bf16[16,4096]{1,0:T(8,128)(2,1)S(1)}, bf16[16,4096]{1,0:T(8,128)(2,1)S(1)}, u32[]{:S(2)}, u32[]{:S(2)}) %collective-permute-start.2) | collective-permute-done | bytes 131104 | tf_op jit(solution)/shard_map/ppermute | solution.py:55
  12.6 0.0 collective-permute-start.3
  12.6 1.5 %collective-permute-start.5 = (bf16[32,2048]{1,0:T(8,128)(2,1)S(1)}, bf16[32,2048]{1,0:T(8,128)(2,1)S(1)}, u32[]{:S(2)}, u32[]{:S(2)}) collective-permute-start(bf16[32,2048]{1,0:T(8,128)(2,1)S(1)} %get-tuple-element.27), channel_id=1, source_target_pairs={{0,16},{16,0},{1,17},{17,1},{2,18},{18,2},{3,19},{19,3},{4,20},{20... | collective-permute-start | bytes 393224 | tf_op jit(solution)/shard_map/ppermute | solution.py:44
  14.1 0.0 collective-permute-done.1.refs_1_
  14.1 0.0 collective-permute-done.3.refs_3_
  14.1 3.6 %backward.1 = (bf16[32,4096]{1,0:T(8,128)(2,1)S(1)}, bf16[32,4096]{1,0:T(8,128)(2,1)S(1)}, bf16[64,1152]{1,0:T(8,128)(2,1)S(1)}) custom-call(bf16[16,4096]{1,0:T(8,128)(2,1)S(1)} %get-tuple-element.19.refs_0_, bf16[16,4096]{1,0:T(8,128)(2,1)S(1)} %collective-permute-done.1.refs_1_, bf16[16,4096]{1,0:T(8,128)(2,1)S(1)} %collective-permute-done.2.refs_2_.refs_1_, ...), custom_call_target="tpu_custom_call" | custom-call | flops 603979776 | bytes 10207232 | tf_op jit(solution)/shard_map/backward/pallas_call | solution.py:70
  17.7 0.3 collective-permute-start.4
  18.0 0.5 %collective-permute-done.5.refs_0_.refs_4_ = bf16[32,2048]{1,0:T(8,128)(2,1)S(1)} collective-permute-done((bf16[32,2048]{1,0:T(8,128)(2,1)S(1)}, bf16[32,2048]{1,0:T(8,128)(2,1)S(1)}, u32[]{:S(2)}, u32[]{:S(2)}) %collective-permute-start.5) | collective-permute-done | bytes 131104 | tf_op jit(solution)/shard_map/ppermute | solution.py:44
  18.5 0.0 collective-permute-start.6
  18.5 1.6 %collective-permute-start.9 = (bf16[32,2048]{1,0:T(8,128)(2,1)S(1)}, bf16[32,2048]{1,0:T(8,128)(2,1)S(1)}, u32[]{:S(2)}, u32[]{:S(2)}) collective-permute-start(bf16[32,2048]{1,0:T(8,128)(2,1)S(1)} %pack.1), channel_id=1, source_target_pairs={{0,16},{16,0},{1,17},{17,1},{2,18},{18,2},{3,19},{19,3},{4,20},{20... | collective-permute-start | bytes 393224 | tf_op jit(solution)/shard_map/ppermute | solution.py:44
  20.1 0.0 collective-permute-done.6.refs_1_.refs_5_
  20.1 0.0 collective-permute-done.4.given_ref
  20.1 1.6 %collective-permute-start.7 = (bf16[16,4096]{1,0:T(8,128)(2,1)S(1)}, bf16[16,4096]{1,0:T(8,128)(2,1)S(1)}, u32[]{:S(2)}, u32[]{:S(2)}) collective-permute-start(bf16[16,4096]{1,0:T(8,128)(2,1)S(1)} %pair_sums.1), channel_id=1, source_target_pairs={{2,0},{3,1},{0,2},{1,3},{6,4},{7,5},{4,6},{5,7},{10,8},{11,9},{8,1... | collective-permute-start | bytes 393224 | tf_op jit(solution)/shard_map/ppermute | solution.py:55
  21.7 1.3 %collective-permute-start.11 = (bf16[64,1152]{1,0:T(8,128)(2,1)S(1)}, bf16[64,1152]{1,0:T(8,128)(2,1)S(1)}, u32[]{:S(2)}, u32[]{:S(2)}) collective-permute-start(bf16[64,1152]{1,0:T(8,128)(2,1)S(1)} %get-tuple-element.28.factors_ref), channel_id=1, source_target_pairs={{0,16},{16,0},{1,17},{17,1},{2,18},{18,2},{3,19},{19,3},{4,20},{20... | collective-permute-start | bytes 442376 | tf_op jit(solution)/shard_map/ppermute | solution.py:44
  23.0 1.7 %collective-permute-done.9.refs_6_ = bf16[32,2048]{1,0:T(8,128)(2,1)S(1)} collective-permute-done((bf16[32,2048]{1,0:T(8,128)(2,1)S(1)}, bf16[32,2048]{1,0:T(8,128)(2,1)S(1)}, u32[]{:S(2)}, u32[]{:S(2)}) %collective-permute-start.9) | collective-permute-done | bytes 131104 | tf_op jit(solution)/shard_map/ppermute | solution.py:44
  24.7 0.0 collective-permute-start.10
  24.7 1.1 %collective-permute-done.7.refs_0_ = bf16[16,4096]{1,0:T(8,128)(2,1)S(1)} collective-permute-done((bf16[16,4096]{1,0:T(8,128)(2,1)S(1)}, bf16[16,4096]{1,0:T(8,128)(2,1)S(1)}, u32[]{:S(2)}, u32[]{:S(2)}) %collective-permute-start.7) | collective-permute-done | bytes 131104 | tf_op jit(solution)/shard_map/ppermute | solution.py:55
  25.8 0.1 sum_returned.1
  25.9 0.5 %collective-permute-start.8 = (bf16[16,4224]{1,0:T(8,128)(2,1)S(1)}, bf16[16,4224]{1,0:T(8,128)(2,1)S(1)}, u32[]{:S(2)}, u32[]{:S(2)}) collective-permute-start(bf16[16,4224]{1,0:T(8,128)(2,1)S(1)} %sum_returned.1), channel_id=1, source_target_pairs={{0,12},{4,0},{8,4},{12,8},{1,13},{5,1},{9,5},{13,9},{2,14},{6,2},{... | collective-permute-start | bytes 405512 | tf_op jit(solution)/shard_map/ppermute | solution.py:60
  26.4 0.0 collective-permute-done.10.refs_7_
  26.4 1.3 %collective-permute-done.11.refs_8_ = bf16[64,1152]{1,0:T(8,128)(2,1)S(1)} collective-permute-done((bf16[64,1152]{1,0:T(8,128)(2,1)S(1)}, bf16[64,1152]{1,0:T(8,128)(2,1)S(1)}, u32[]{:S(2)}, u32[]{:S(2)}) %collective-permute-start.11) | collective-permute-done | bytes 147488 | tf_op jit(solution)/shard_map/ppermute | solution.py:44
  27.7 2.6 %weight_grads.1 = bf16[1,3,384,2048]{3,2,1,0:T(8,128)(2,1)} custom-call(bf16[64,1152]{1,0:T(8,128)(2,1)S(1)} %get-tuple-element.28.factors_ref, bf16[64,4096]{1,0:T(8,128)(2,1)S(1)} %get-tuple-element.29.inputs_ref, bf16[16,4096]{1,0:T(8,128)(2,1)S(1)} %get-tuple-element.19.refs_0_, bf16[16,4096]{1,0:T(8,128)(2,1)S(1)} %collective-permute-done.1.refs_1_, ...), custom_call_target="tpu_custom_call" | custom-call | flops 603979776 | bytes 1867776 | tf_op jit(solution)/shard_map/weight_grads/pallas_call | solution.py:70
  30.2 0.7 %collective-permute-done.8.changed_ref = bf16[16,4224]{1,0:T(8,128)(2,1)S(1)} collective-permute-done((bf16[16,4224]{1,0:T(8,128)(2,1)S(1)}, bf16[16,4224]{1,0:T(8,128)(2,1)S(1)}, u32[]{:S(2)}, u32[]{:S(2)}) %collective-permute-start.8) | collective-permute-done | bytes 135200 | tf_op jit(solution)/shard_map/ppermute | solution.py:60
  31.0 0.0 collective-permute-done.early_ref
  31.0 1.5 %merge.1 = bf16[1,1,128,4096]{3,2,1,0:T(8,128)(2,1)} custom-call(bf16[112,4096]{1,0:T(8,128)(2,1)S(1)} %collective-permute-done.early_ref, bf16[16,4224]{1,0:T(8,128)(2,1)S(1)} %collective-permute-done.8.changed_ref), custom_call_target="tpu_custom_call" | custom-call | flops 16777216 | bytes 1052672 | tf_op jit(solution)/shard_map/merge/pallas_call | solution.py:70
  (2 shorter events, 0.0 us)
Async XLA Ops:
  0.6 8.5 %copy-start = (bf16[1,3,384,4096]{3,2,1,0:T(8,128)(2,1)S(1)}, bf16[1,3,384,4096]{3,2,1,0:T(8,128)(2,1)}, u32[]{:S(2)}) copy-start(bf16[1,3,384,4096]{3,2,1,0:T(8,128)(2,1)} %param.9) | copy-start | bytes 28311556
  0.6 8.5 %copy-start.1 = (bf16[1,1,1,4,16,4096]{5,4,3,2,1,0:T(8,128)(2,1)S(1)}, bf16[1,1,1,4,16,4096]{5,4,3,2,1,0:T(8,128)(2,1)}, u32[]{:S(2)}) copy-start(bf16[1,1,1,4,16,4096]{5,4,3,2,1,0:T(8,128)(2,1)} %param.8) | copy-start | bytes 1572868
  2.5 28.4 %collective-permute-start = (bf16[112,4096]{1,0:T(8,128)(2,1)S(1)}, bf16[112,4096]{1,0:T(8,128)(2,1)S(1)}, u32[]{:S(2)}, u32[]{:S(2)}) collective-permute-start(bf16[112,4096]{1,0:T(8,128)(2,1)S(1)} %get-tuple-element.16), channel_id=1, source_target_pairs={{0,12},{4,0},{8,4},{12,8},{1,13},{5,1},{9,5},{13,9},{2,14},{6,2},{... | collective-permute-start | bytes 2752520 | tf_op jit(solution)/shard_map/ppermute | solution.py:60
  7.6 5.0 %collective-permute-start.2 = (bf16[16,4096]{1,0:T(8,128)(2,1)S(1)}, bf16[16,4096]{1,0:T(8,128)(2,1)S(1)}, u32[]{:S(2)}, u32[]{:S(2)}) collective-permute-start(bf16[16,4096]{1,0:T(8,128)(2,1)S(1)} %get-tuple-element.19.refs_0_), channel_id=1, source_target_pairs={{0,2},{1,3},{2,0},{3,1},{4,6},{5,7},{6,4},{7,5},{8,10},{9,11},{10,... | collective-permute-start | bytes 393224 | tf_op jit(solution)/shard_map/ppermute | solution.py:55
  9.1 4.9 %collective-permute-start.1 = (bf16[16,4096]{1,0:T(8,128)(2,1)S(1)}, bf16[16,4096]{1,0:T(8,128)(2,1)S(1)}, u32[]{:S(2)}, u32[]{:S(2)}) collective-permute-start(bf16[16,4096]{1,0:T(8,128)(2,1)S(1)} %get-tuple-element.19.refs_0_), channel_id=1, source_target_pairs={{0,1},{1,0},{2,3},{3,2},{4,5},{5,4},{6,7},{7,6},{8,9},{9,8},{10,11... | collective-permute-start | bytes 393224 | tf_op jit(solution)/shard_map/ppermute | solution.py:48
  12.6 1.5 %collective-permute-start.3 = (bf16[16,4096]{1,0:T(8,128)(2,1)S(1)}, bf16[16,4096]{1,0:T(8,128)(2,1)S(1)}, u32[]{:S(2)}, u32[]{:S(2)}) collective-permute-start(bf16[16,4096]{1,0:T(8,128)(2,1)S(1)} %collective-permute-done.2.refs_2_.refs_1_), channel_id=1, source_target_pairs={{0,1},{1,0},{2,3},{3,2},{4,5},{5,4},{6,7},{7,6},{8,9},{9,8},{10,11... | collective-permute-start | bytes 393224 | tf_op jit(solution)/shard_map/ppermute | solution.py:48
  12.6 5.9 %collective-permute-start.5 = (bf16[32,2048]{1,0:T(8,128)(2,1)S(1)}, bf16[32,2048]{1,0:T(8,128)(2,1)S(1)}, u32[]{:S(2)}, u32[]{:S(2)}) collective-permute-start(bf16[32,2048]{1,0:T(8,128)(2,1)S(1)} %get-tuple-element.27), channel_id=1, source_target_pairs={{0,16},{16,0},{1,17},{17,1},{2,18},{18,2},{3,19},{19,3},{4,20},{20... | collective-permute-start | bytes 393224 | tf_op jit(solution)/shard_map/ppermute | solution.py:44
  17.7 2.4 %collective-permute-start.4 = (bf16[32,4096]{1,0:T(8,128)(2,1)S(1)}, bf16[32,4096]{1,0:T(8,128)(2,1)S(1)}, u32[]{:S(2)}, u32[]{:S(2)}) collective-permute-start(bf16[32,4096]{1,0:T(8,128)(2,1)S(1)} %get-tuple-element.26), channel_id=1, source_target_pairs={{0,1},{1,0},{2,3},{3,2},{4,5},{5,4},{6,7},{7,6},{8,9},{9,8},{10,11... | collective-permute-start | bytes 786440 | tf_op jit(solution)/shard_map/ppermute | solution.py:48
  18.5 1.6 %collective-permute-start.6 = (bf16[32,2048]{1,0:T(8,128)(2,1)S(1)}, bf16[32,2048]{1,0:T(8,128)(2,1)S(1)}, u32[]{:S(2)}, u32[]{:S(2)}) collective-permute-start(bf16[32,2048]{1,0:T(8,128)(2,1)S(1)} %collective-permute-done.5.refs_0_.refs_4_), channel_id=1, source_target_pairs={{0,1},{1,0},{2,3},{3,2},{4,5},{5,4},{6,7},{7,6},{8,9},{9,8},{10,11... | collective-permute-start | bytes 393224 | tf_op jit(solution)/shard_map/ppermute | solution.py:48
  18.5 6.2 %collective-permute-start.9 = (bf16[32,2048]{1,0:T(8,128)(2,1)S(1)}, bf16[32,2048]{1,0:T(8,128)(2,1)S(1)}, u32[]{:S(2)}, u32[]{:S(2)}) collective-permute-start(bf16[32,2048]{1,0:T(8,128)(2,1)S(1)} %pack.1), channel_id=1, source_target_pairs={{0,16},{16,0},{1,17},{17,1},{2,18},{18,2},{3,19},{19,3},{4,20},{20... | collective-permute-start | bytes 393224 | tf_op jit(solution)/shard_map/ppermute | solution.py:44
  20.1 5.7 %collective-permute-start.7 = (bf16[16,4096]{1,0:T(8,128)(2,1)S(1)}, bf16[16,4096]{1,0:T(8,128)(2,1)S(1)}, u32[]{:S(2)}, u32[]{:S(2)}) collective-permute-start(bf16[16,4096]{1,0:T(8,128)(2,1)S(1)} %pair_sums.1), channel_id=1, source_target_pairs={{2,0},{3,1},{0,2},{1,3},{6,4},{7,5},{4,6},{5,7},{10,8},{11,9},{8,1... | collective-permute-start | bytes 393224 | tf_op jit(solution)/shard_map/ppermute | solution.py:55
  21.7 5.9 %collective-permute-start.11 = (bf16[64,1152]{1,0:T(8,128)(2,1)S(1)}, bf16[64,1152]{1,0:T(8,128)(2,1)S(1)}, u32[]{:S(2)}, u32[]{:S(2)}) collective-permute-start(bf16[64,1152]{1,0:T(8,128)(2,1)S(1)} %get-tuple-element.28.factors_ref), channel_id=1, source_target_pairs={{0,16},{16,0},{1,17},{17,1},{2,18},{18,2},{3,19},{19,3},{4,20},{20... | collective-permute-start | bytes 442376 | tf_op jit(solution)/shard_map/ppermute | solution.py:44
  24.7 1.7 %collective-permute-start.10 = (bf16[32,2048]{1,0:T(8,128)(2,1)S(1)}, bf16[32,2048]{1,0:T(8,128)(2,1)S(1)}, u32[]{:S(2)}, u32[]{:S(2)}) collective-permute-start(bf16[32,2048]{1,0:T(8,128)(2,1)S(1)} %collective-permute-done.9.refs_6_), channel_id=1, source_target_pairs={{0,1},{1,0},{2,3},{3,2},{4,5},{5,4},{6,7},{7,6},{8,9},{9,8},{10,11... | collective-permute-start | bytes 393224 | tf_op jit(solution)/shard_map/ppermute | solution.py:48
  25.9 5.1 %collective-permute-start.8 = (bf16[16,4224]{1,0:T(8,128)(2,1)S(1)}, bf16[16,4224]{1,0:T(8,128)(2,1)S(1)}, u32[]{:S(2)}, u32[]{:S(2)}) collective-permute-start(bf16[16,4224]{1,0:T(8,128)(2,1)S(1)} %sum_returned.1), channel_id=1, source_target_pairs={{0,12},{4,0},{8,4},{12,8},{1,13},{5,1},{9,5},{13,9},{2,14},{6,2},{... | collective-permute-start | bytes 405512 | tf_op jit(solution)/shard_map/ppermute | solution.py:60

commit v6 on v5

--- a/solution.py
+++ b/solution.py
@@ -90,9 +90,14 @@
     return mm(flags.astype(BF16), jnp.where(before, F32(1.0), F32(0.0)).astype(BF16), ROWS_COLS)
 
 
-def one_hot(wanted, rows, valid):
+def one_hot(wanted, rows):
     number = lax.broadcasted_iota(jnp.int32, (rows, wanted.shape[1]), 0).astype(F32)
-    return jnp.where((number == wanted[:1]) & (valid[:1] > 0.5), F32(1.0), F32(0.0))
+    return jnp.where(number == wanted[:1], F32(1.0), F32(0.0))
+
+
+def sorting(early_row, late_row, tokens, capacity):
+    early = one_hot(early_row, tokens - capacity)
+    return jnp.concatenate([early, one_hot(late_row, capacity)], axis=0).astype(BF16)
 
 
 def choose_late(routing, gates, capacity):
@@ -106,9 +111,9 @@
     rank = lax.broadcasted_iota(jnp.int32, (capacity, tokens), 1).astype(F32) - slot
     left = rank - F32(tokens - capacity)
     is_late = jnp.where((spread > 0.5) | (left >= 0.0), F32(1.0), F32(0.0))
-    chosen = one_hot(jnp.where(spread > 0.5, slot, members + left), capacity, is_late)
-    weighting = jnp.sum(chosen * share, axis=1, keepdims=True)
-    return chosen, weighting, one_hot(rank, tokens - capacity, 1.0 - is_late)
+    late_row = jnp.where(is_late > 0.5, jnp.where(spread > 0.5, slot, members + left), F32(-1.0))
+    weighting = jnp.sum(one_hot(late_row, capacity) * share, axis=1, keepdims=True)
+    return jnp.where(is_late > 0.5, F32(-1.0), rank), late_row, weighting
 
 
 def route_body(
@@ -124,9 +129,15 @@
         f.start()
     for f in fetches[:2]:
         f.wait()
-    chosen, weighting, kept = choose_late(routing_ref[...], gates_ref[...], capacity)
-    both = jnp.concatenate([kept, chosen], axis=0).astype(BF16)
     early = early_ref.shape[0]
+    early_row, late_row, weighting = choose_late(routing_ref[...], gates_ref[...], capacity)
+    both = sorting(early_row, late_row, early + capacity, capacity)
+    digits = [d for row in (early_row, late_row) for d in (row.astype(jnp.int32) >> 7, row.astype(jnp.int32) & 127)]
+    number = lax.broadcasted_iota(jnp.int32, ids_ref.shape, 0)
+    ids = digits[3]
+    for i in range(3):
+        ids = jnp.where(number == i, digits[i], ids)
+    ids_ref[...] = ids.astype(F32).astype(BF16)
     fetches[2].wait()
     step = min(width, 1024)
     for c in range(width // step):
@@ -135,11 +146,6 @@
         early_ref[:, at] = sorted_rows[:early].astype(BF16)
         picked_ref[:, at] = sorted_rows[early:].astype(BF16)
         routed_ref[:, at] = (sorted_rows[early:] * weighting).astype(BF16)
-    token = lax.broadcasted_iota(jnp.int32, chosen.shape, 1)
-    high = jnp.sum(chosen * (token // LANES).astype(F32), axis=1, keepdims=True)
-    low = jnp.sum(chosen * (token % LANES).astype(F32), axis=1, keepdims=True)
-    lane = lax.broadcasted_iota(jnp.int32, ids_ref.shape, 1)
-    ids_ref[...] = jnp.where(lane == 0, high, jnp.where(lane == 1, low, F32(0.0))).astype(BF16)
 
 
 def forward_body(saved_ref, weights_ref, slope_ref, active_ref, hidden_ref, rows_ref, *fars):
@@ -168,7 +174,7 @@
 def backward_body(order, *refs):
     blocks = refs[:order]
     weights_ref, slope_ref, active_ref, hidden_ref = refs[order : order + 4]
-    kept_ref, given_ref, grads_ref = refs[-3:]
+    kept_ref, grads_ref, *given = refs[order + 4 :]
     inner, outer = pairs_of(order)
     rows = jnp.concatenate([b[...] for b in blocks], axis=0)
     hidden_grad = mm(weights_ref[2], rows, LAST_LAST)
@@ -180,22 +186,26 @@
         at = slice(c * step, (c + 1) * step)
         total = mm(gate_grad, weights_ref[0, :, at], ROWS_COLS) + mm(up_grad, weights_ref[1, :, at], ROWS_COLS)
         for k in range(order):
-            into = kept_ref if k % inner == 0 else given_ref
             j = k // inner
-            into[j * capacity : (j + 1) * capacity, at] = total[k * capacity : (k + 1) * capacity].astype(BF16)
+            block = total[k * capacity : (k + 1) * capacity].astype(BF16)
+            if k % inner:
+                given[j][:, at] = block
+            else:
+                kept_ref[j * capacity : (j + 1) * capacity, at] = block
     hid = weights_ref.shape[1]
     grads_ref[:, :hid] = gate_grad
     grads_ref[:, hid : 2 * hid] = up_grad
     grads_ref[:, 2 * hid :] = hidden_ref[...]
 
 
-def pair_body(paired, others, kept_ref, given_ref, *refs):
-    outs = refs[others:]
+def pair_body(outer, paired, kept_ref, *refs):
+    given, outs = refs[: outer - 1] if paired else (), refs[1 - outer :]
     capacity = outs[0].shape[0]
     for j, ref in enumerate(outs, 1):
-        at = slice(j * capacity, (j + 1) * capacity)
-        total = kept_ref[at].astype(F32)
-        ref[...] = (total + given_ref[at].astype(F32) if paired else total).astype(BF16)
+        total = kept_ref[j * capacity : (j + 1) * capacity].astype(F32)
+        if paired:
+            total = total + given[j - 1][...].astype(F32)
+        ref[...] = total.astype(BF16)
 
 
 def pack_body(outer, *refs):
@@ -209,12 +219,10 @@
             into[j * capacity : (j + 1) * capacity] = blocks[j][:, pl.ds(first, part)]
 
 
-def return_body(paired, picked_ref, ids_ref, kept_ref, given_ref, *refs):
+def return_body(picked_ref, ids_ref, kept_ref, *refs):
     returned, out_ref = refs[:-1], refs[-1]
     capacity, width = picked_ref.shape
     back = kept_ref[:capacity].astype(F32)
-    if paired:
-        back = back + given_ref[:capacity].astype(F32)
     for ref in returned:
         back = back + ref[...].astype(F32)
     out_ref[:, :width] = (picked_ref[...].astype(F32) + back).astype(BF16)
@@ -262,13 +270,8 @@
     early, width = early_ref.shape
     capacity = changed_ref.shape[0]
     tokens = early + capacity
-    high = changed_ref[:, width : width + 1].astype(F32)
-    low = changed_ref[:, width + 1 : width + 2].astype(F32)
-    token = lax.broadcasted_iota(jnp.int32, (capacity, tokens), 1).astype(F32)
-    chosen = jnp.where(token == high * F32(LANES) + low, F32(1.0), F32(0.0))
-    is_late = jnp.broadcast_to(jnp.sum(chosen, axis=0, keepdims=True), (capacity, tokens))
-    kept = one_hot(token - earlier_count(is_late), early, 1.0 - is_late)
-    both = jnp.concatenate([kept, chosen], axis=0).astype(BF16)
+    digits = [changed_ref[:, width:][i : i + 1].astype(F32) for i in range(4)]
+    both = sorting(digits[0] * 128.0 + digits[1], digits[2] * 128.0 + digits[3], tokens, capacity)
     step = held.shape[2]
     copies = []
     for c in range(width // step):
@@ -307,7 +310,7 @@
             out((early, width), BF16),
             out((capacity, width), BF16),
             out((capacity, width), BF16),
-            out((capacity, LANES), BF16),
+            out((capacity, tokens), BF16),
         ],
         [in_hbm(v) for v in (jnp.transpose(routing[0, 0]), jnp.transpose(gate_values[0, 0]), incoming)],
         ROUTE_COST,
@@ -351,30 +354,29 @@
     far_rows = both_halves([exchange(f, "dp", k + 1) for k, f in enumerate(fars)])
     far_inputs = both_halves(far_inputs)
 
-    kept, given, grads = run(
+    kept, grads, *given = run(
         functools.partial(backward_body, owners),
         "backward",
-        [out((mine, width), BF16)] * 2 + [out((rows, 3 * hid), BF16)],
+        [out((mine, width), BF16), out((rows, 3 * hid), BF16)] + [out((capacity, width), BF16)] * ((inner - 1) * outer),
         [routed, *arrived, weights, slope, active, hidden],
         6 * rows * hid * width,
     )
-    if inner == 2:
-        given = to_sibling(given)
+    given = [to_sibling(v) for v in given]
     sums = run(
-        functools.partial(pair_body, inner == 2, len(far_inputs)),
+        functools.partial(pair_body, outer, inner == 2),
         "pair_sums",
         [out((capacity, width), BF16)] * (outer - 1),
-        [kept, given, *far_inputs],
+        [kept, *given[1:], *far_inputs[::inner]],
         0,
     )
     returned = [to_pair(v, j, back=True) for j, v in enumerate(sums, 1)]
     far_grads = [exchange(grads, "dp", k) for k in range(1, replicas)]
 
     changed = run(
-        functools.partial(return_body, inner == 2),
+        return_body,
         "sum_returned",
-        [out((capacity, width + LANES), BF16)],
-        [picked, ids, kept, given, *returned],
+        [out((capacity, width + tokens), BF16)],
+        [picked, ids, kept, *given[:1], *returned],
         0,
     )[0]
     next_changed = to_previous(changed)

time: 32.6 us -> 32 us (0.982)
  waiting for transfers between devices: 6.96 us -> 6.5 us
    ppermute x3, waiting for transfers between devices: 3.49 us -> 2.69 us  [exchange(): lax.ppermute(value, axis, [(i, partner(i, step, count)) for i in range(co...]
    ppermute x5 -> x6, starting transfers between devices: 0.3 us -> 0.88 us  [to_sibling(): lax.ppermute(value, 'expert', [(i, i ^ 1) for i in range(lax.axis_size('e...]
    ppermute x3, starting transfers between devices: 4.31 us -> 3.86 us  [exchange(): lax.ppermute(value, axis, [(i, partner(i, step, count)) for i in range(co...]
    ppermute x2, waiting for transfers between devices: 0.73 us -> 1.11 us  [to_previous(): lax.ppermute(value, 'pipe', [(i, (i - 1) % count) for i in range(count)])]
  transfers between devices with their start and end apart: 12 -> 13, of which waited for: 6 -> 5; matrix products, arithmetic and copies ran while one was open for 0% -> 0% of each run, Pallas kernels for 25% -> 25%
where the time goes in v6:
time: 32 us; the launch traced here: 31.9 us
  starting transfers between devices  13.4 us (42%)
  Pallas kernels  11.2 us (35%)
  waiting for transfers between devices  6.5 us (20%)
  between operations  0.7 us (2%)
    pallas_call x8, Pallas kernels, run(): pl.pallas_call(body, name=name, out_shape=outs, in_specs=in_specs or [vme...  11.2 us
    ppermute x2, starting transfers between devices, to_previous(): lax.ppermute(value, 'pipe', [(i, (i - 1) % count) for i in range(count)])  5.6 us
    ppermute x3, starting transfers between devices, exchange(): lax.ppermute(value, axis, [(i, partner(i, step, count)) for i in range(co...  3.86 us
    ppermute x2, starting transfers between devices, to_pair(): lax.ppermute(value, 'expert', [(j, i) for i, j in hops] if back else hops)  3.1 us
    ppermute x3, waiting for transfers between devices, exchange(): lax.ppermute(value, axis, [(i, partner(i, step, count)) for i in range(co...  2.69 us
    ppermute x2, waiting for transfers between devices, to_pair(): lax.ppermute(value, 'expert', [(j, i) for i, j in hops] if back else hops)  2.69 us
    ppermute x2, waiting for transfers between devices, to_previous(): lax.ppermute(value, 'pipe', [(i, (i - 1) % count) for i in range(count)])  1.11 us
    ppermute x6, starting transfers between devices, to_sibling(): lax.ppermute(value, 'expert', [(i, i ^ 1) for i in range(lax.axis_size('e...  0.88 us
  transfers between devices with their start and end apart: 13, of which 5 were waited for; matrix products, arithmetic and copies ran while one was open for 0% of the time, Pallas kernels for 25%

profile of v6, /device:TPU:0, one launch (start us, length us, event | category | flops | bytes accessed | tf_op | source)
XLA Modules:
  0.0 31.9 jit_solution(11713367272203329229)
XLA Ops:
  0.6 0.0 copy-start
  0.6 0.0 copy-start.1
  0.7 1.9 %route.1 = (bf16[112,4096]{1,0:T(8,128)(2,1)S(1)}, bf16[16,4096]{1,0:T(8,128)(2,1)S(1)}, bf16[16,4096]{1,0:T(8,128)(2,1)S(1)}, bf16[16,128]{1,0:T(8,128)(2,1)S(1)}) custom-call(s32[8,128]{1,0:T(8,128)} %bitcast.13, f32[8,128]{1,0:T(8,128)} %bitcast.14, bf16[128,4096]{1,0:T(8,128)(2,1)} %bitcast.12), custom_call_target="tpu_custom_call" | custom-call | flops 10000000000 | bytes 1056768 | tf_op jit(solution)/shard_map/route/pallas_call | solution.py:70
  2.5 5.1 %collective-permute-start = (bf16[112,4096]{1,0:T(8,128)(2,1)S(1)}, bf16[112,4096]{1,0:T(8,128)(2,1)S(1)}, u32[]{:S(2)}, u32[]{:S(2)}) collective-permute-start(bf16[112,4096]{1,0:T(8,128)(2,1)S(1)} %get-tuple-element.17), channel_id=1, source_target_pairs={{0,12},{4,0},{8,4},{12,8},{1,13},{5,1},{9,5},{13,9},{2,14},{6,2},{... | collective-permute-start | bytes 2752520 | tf_op jit(solution)/shard_map/ppermute | solution.py:60
  7.6 1.5 %collective-permute-start.2 = (bf16[16,4096]{1,0:T(8,128)(2,1)S(1)}, bf16[16,4096]{1,0:T(8,128)(2,1)S(1)}, u32[]{:S(2)}, u32[]{:S(2)}) collective-permute-start(bf16[16,4096]{1,0:T(8,128)(2,1)S(1)} %get-tuple-element.20.refs_0_), channel_id=1, source_target_pairs={{0,2},{1,3},{2,0},{3,1},{4,6},{5,7},{6,4},{7,5},{8,10},{9,11},{10,... | collective-permute-start | bytes 393224 | tf_op jit(solution)/shard_map/ppermute | solution.py:55
  9.1 0.0 collective-permute-start.1
  9.2 0.0 copy-done
  9.2 0.0 copy-done.1
  9.2 1.8 %forward.1 = (f32[384,64]{1,0:T(8,128)S(1)}, f32[384,64]{1,0:T(8,128)S(1)}, bf16[64,384]{1,0:T(8,128)(2,1)S(1)}, bf16[64,4096]{1,0:T(8,128)(2,1)S(1)}, bf16[32,2048]{1,0:T(8,128)(2,1)S(1)}) custom-call(bf16[4,16,4096]{2,1,0:T(8,128)(2,1)S(1)} %bitcast.11, bf16[3,384,4096]{2,1,0:T(8,128)(2,1)S(1)} %bitcast.9), custom_call_target="tpu_custom_call" | custom-call | flops 402653184 | bytes 9961472 | tf_op jit(solution)/shard_map/forward/pallas_call | solution.py:70
  11.0 1.6 %collective-permute-done.2.refs_2_.refs_1_ = bf16[16,4096]{1,0:T(8,128)(2,1)S(1)} collective-permute-done((bf16[16,4096]{1,0:T(8,128)(2,1)S(1)}, bf16[16,4096]{1,0:T(8,128)(2,1)S(1)}, u32[]{:S(2)}, u32[]{:S(2)}) %collective-permute-start.2) | collective-permute-done | bytes 131104 | tf_op jit(solution)/shard_map/ppermute | solution.py:55
  12.6 0.0 collective-permute-start.3
  12.6 1.5 %collective-permute-start.6 = (bf16[32,2048]{1,0:T(8,128)(2,1)S(1)}, bf16[32,2048]{1,0:T(8,128)(2,1)S(1)}, u32[]{:S(2)}, u32[]{:S(2)}) collective-permute-start(bf16[32,2048]{1,0:T(8,128)(2,1)S(1)} %get-tuple-element.29), channel_id=1, source_target_pairs={{0,16},{16,0},{1,17},{17,1},{2,18},{18,2},{3,19},{19,3},{4,20},{20... | collective-permute-start | bytes 393224 | tf_op jit(solution)/shard_map/ppermute | solution.py:44
  14.1 0.0 collective-permute-done.1.refs_1_
  14.1 0.0 collective-permute-done.3.refs_3_
  14.1 3.6 %backward.1 = (bf16[32,4096]{1,0:T(8,128)(2,1)S(1)}, bf16[64,1152]{1,0:T(8,128)(2,1)S(1)}, bf16[16,4096]{1,0:T(8,128)(2,1)S(1)}, bf16[16,4096]{1,0:T(8,128)(2,1)S(1)}) custom-call(bf16[16,4096]{1,0:T(8,128)(2,1)S(1)} %get-tuple-element.20.refs_0_, bf16[16,4096]{1,0:T(8,128)(2,1)S(1)} %collective-permute-done.1.refs_1_, ...), custom_call_target="tpu_custom_call" | custom-call | flops 603979776 | bytes 10207232 | tf_op jit(solution)/shard_map/backward/pallas_call | solution.py:70
  17.7 0.3 collective-permute-start.5
  18.0 1.3 %collective-permute-start.10 = (bf16[32,2048]{1,0:T(8,128)(2,1)S(1)}, bf16[32,2048]{1,0:T(8,128)(2,1)S(1)}, u32[]{:S(2)}, u32[]{:S(2)}) collective-permute-start(bf16[32,2048]{1,0:T(8,128)(2,1)S(1)} %pack.1), channel_id=1, source_target_pairs={{0,16},{16,0},{1,17},{17,1},{2,18},{18,2},{3,19},{19,3},{4,20},{20... | collective-permute-start | bytes 393224 | tf_op jit(solution)/shard_map/ppermute | solution.py:44
  19.3 0.1 collective-permute-start.4
  19.4 0.0 collective-permute-done.6.refs_1_.refs_4_
  19.4 0.0 collective-permute-done.5.refs_0_
  19.5 1.6 %collective-permute-start.7 = (bf16[16,4096]{1,0:T(8,128)(2,1)S(1)}, bf16[16,4096]{1,0:T(8,128)(2,1)S(1)}, u32[]{:S(2)}, u32[]{:S(2)}) collective-permute-start(bf16[16,4096]{1,0:T(8,128)(2,1)S(1)} %pair_sums.1), channel_id=1, source_target_pairs={{2,0},{3,1},{0,2},{1,3},{6,4},{7,5},{4,6},{5,7},{10,8},{11,9},{8,1... | collective-permute-start | bytes 393224 | tf_op jit(solution)/shard_map/ppermute | solution.py:55
  21.0 1.0 %collective-permute-start.12 = (bf16[64,1152]{1,0:T(8,128)(2,1)S(1)}, bf16[64,1152]{1,0:T(8,128)(2,1)S(1)}, u32[]{:S(2)}, u32[]{:S(2)}) collective-permute-start(bf16[64,1152]{1,0:T(8,128)(2,1)S(1)} %get-tuple-element.30.factors_ref), channel_id=1, source_target_pairs={{0,16},{16,0},{1,17},{17,1},{2,18},{18,2},{3,19},{19,3},{4,20},{20... | collective-permute-start | bytes 442376 | tf_op jit(solution)/shard_map/ppermute | solution.py:44
  22.1 1.7 %collective-permute-done.10.refs_6_ = bf16[32,2048]{1,0:T(8,128)(2,1)S(1)} collective-permute-done((bf16[32,2048]{1,0:T(8,128)(2,1)S(1)}, bf16[32,2048]{1,0:T(8,128)(2,1)S(1)}, u32[]{:S(2)}, u32[]{:S(2)}) %collective-permute-start.10) | collective-permute-done | bytes 131104 | tf_op jit(solution)/shard_map/ppermute | solution.py:44
  23.8 0.0 collective-permute-start.9
  23.8 0.0 collective-permute-done.4.refs_0_
  23.8 0.5 %collective-permute-start.11 = (bf16[32,2048]{1,0:T(8,128)(2,1)S(1)}, bf16[32,2048]{1,0:T(8,128)(2,1)S(1)}, u32[]{:S(2)}, u32[]{:S(2)}) collective-permute-start(bf16[32,2048]{1,0:T(8,128)(2,1)S(1)} %collective-permute-done.10.refs_6_), channel_id=1, source_target_pairs={{0,1},{1,0},{2,3},{3,2},{4,5},{5,4},{6,7},{7,6},{8,9},{9,8},{10,11... | collective-permute-start | bytes 393224 | tf_op jit(solution)/shard_map/ppermute | solution.py:48
  24.3 1.1 %collective-permute-done.7.refs_1_ = bf16[16,4096]{1,0:T(8,128)(2,1)S(1)} collective-permute-done((bf16[16,4096]{1,0:T(8,128)(2,1)S(1)}, bf16[16,4096]{1,0:T(8,128)(2,1)S(1)}, u32[]{:S(2)}, u32[]{:S(2)}) %collective-permute-start.7) | collective-permute-done | bytes 131104 | tf_op jit(solution)/shard_map/ppermute | solution.py:55
  25.4 0.1 sum_returned.1
  25.4 0.5 %collective-permute-start.8 = (bf16[16,4224]{1,0:T(8,128)(2,1)S(1)}, bf16[16,4224]{1,0:T(8,128)(2,1)S(1)}, u32[]{:S(2)}, u32[]{:S(2)}) collective-permute-start(bf16[16,4224]{1,0:T(8,128)(2,1)S(1)} %sum_returned.1), channel_id=1, source_target_pairs={{0,12},{4,0},{8,4},{12,8},{1,13},{5,1},{9,5},{13,9},{2,14},{6,2},{... | collective-permute-start | bytes 405512 | tf_op jit(solution)/shard_map/ppermute | solution.py:60
  25.9 0.0 collective-permute-done.9.refs_5_
  25.9 0.0 collective-permute-done.11.refs_7_
  25.9 1.0 %collective-permute-done.12.refs_8_ = bf16[64,1152]{1,0:T(8,128)(2,1)S(1)} collective-permute-done((bf16[64,1152]{1,0:T(8,128)(2,1)S(1)}, bf16[64,1152]{1,0:T(8,128)(2,1)S(1)}, u32[]{:S(2)}, u32[]{:S(2)}) %collective-permute-start.12) | collective-permute-done | bytes 147488 | tf_op jit(solution)/shard_map/ppermute | solution.py:44
  27.0 2.6 %weight_grads.1 = bf16[1,3,384,2048]{3,2,1,0:T(8,128)(2,1)} custom-call(bf16[64,1152]{1,0:T(8,128)(2,1)S(1)} %get-tuple-element.30.factors_ref, bf16[64,4096]{1,0:T(8,128)(2,1)S(1)} %get-tuple-element.31.inputs_ref, bf16[16,4096]{1,0:T(8,128)(2,1)S(1)} %get-tuple-element.20.refs_0_, bf16[16,4096]{1,0:T(8,128)(2,1)S(1)} %collective-permute-done.1.refs_1_, ...), custom_call_target="tpu_custom_call" | custom-call | flops 603979776 | bytes 1867776 | tf_op jit(solution)/shard_map/weight_grads/pallas_call | solution.py:70
  29.5 1.1 %collective-permute-done.8.changed_ref = bf16[16,4224]{1,0:T(8,128)(2,1)S(1)} collective-permute-done((bf16[16,4224]{1,0:T(8,128)(2,1)S(1)}, bf16[16,4224]{1,0:T(8,128)(2,1)S(1)}, u32[]{:S(2)}, u32[]{:S(2)}) %collective-permute-start.8) | collective-permute-done | bytes 135200 | tf_op jit(solution)/shard_map/ppermute | solution.py:60
  30.6 0.0 collective-permute-done.early_ref
  30.6 1.3 %merge.1 = bf16[1,1,128,4096]{3,2,1,0:T(8,128)(2,1)} custom-call(bf16[112,4096]{1,0:T(8,128)(2,1)S(1)} %collective-permute-done.early_ref, bf16[16,4224]{1,0:T(8,128)(2,1)S(1)} %collective-permute-done.8.changed_ref), custom_call_target="tpu_custom_call" | custom-call | flops 16777216 | bytes 1052672 | tf_op jit(solution)/shard_map/merge/pallas_call | solution.py:70
  (2 shorter events, 0.0 us)
Async XLA Ops:
  0.6 8.5 %copy-start = (bf16[1,3,384,4096]{3,2,1,0:T(8,128)(2,1)S(1)}, bf16[1,3,384,4096]{3,2,1,0:T(8,128)(2,1)}, u32[]{:S(2)}) copy-start(bf16[1,3,384,4096]{3,2,1,0:T(8,128)(2,1)} %param.9) | copy-start | bytes 28311556
  0.6 8.5 %copy-start.1 = (bf16[1,1,1,4,16,4096]{5,4,3,2,1,0:T(8,128)(2,1)S(1)}, bf16[1,1,1,4,16,4096]{5,4,3,2,1,0:T(8,128)(2,1)}, u32[]{:S(2)}) copy-start(bf16[1,1,1,4,16,4096]{5,4,3,2,1,0:T(8,128)(2,1)} %param.8) | copy-start | bytes 1572868
  2.5 28.1 %collective-permute-start = (bf16[112,4096]{1,0:T(8,128)(2,1)S(1)}, bf16[112,4096]{1,0:T(8,128)(2,1)S(1)}, u32[]{:S(2)}, u32[]{:S(2)}) collective-permute-start(bf16[112,4096]{1,0:T(8,128)(2,1)S(1)} %get-tuple-element.17), channel_id=1, source_target_pairs={{0,12},{4,0},{8,4},{12,8},{1,13},{5,1},{9,5},{13,9},{2,14},{6,2},{... | collective-permute-start | bytes 2752520 | tf_op jit(solution)/shard_map/ppermute | solution.py:60
  7.6 5.0 %collective-permute-start.2 = (bf16[16,4096]{1,0:T(8,128)(2,1)S(1)}, bf16[16,4096]{1,0:T(8,128)(2,1)S(1)}, u32[]{:S(2)}, u32[]{:S(2)}) collective-permute-start(bf16[16,4096]{1,0:T(8,128)(2,1)S(1)} %get-tuple-element.20.refs_0_), channel_id=1, source_target_pairs={{0,2},{1,3},{2,0},{3,1},{4,6},{5,7},{6,4},{7,5},{8,10},{9,11},{10,... | collective-permute-start | bytes 393224 | tf_op jit(solution)/shard_map/ppermute | solution.py:55
  9.1 4.9 %collective-permute-start.1 = (bf16[16,4096]{1,0:T(8,128)(2,1)S(1)}, bf16[16,4096]{1,0:T(8,128)(2,1)S(1)}, u32[]{:S(2)}, u32[]{:S(2)}) collective-permute-start(bf16[16,4096]{1,0:T(8,128)(2,1)S(1)} %get-tuple-element.20.refs_0_), channel_id=1, source_target_pairs={{0,1},{1,0},{2,3},{3,2},{4,5},{5,4},{6,7},{7,6},{8,9},{9,8},{10,11... | collective-permute-start | bytes 393224 | tf_op jit(solution)/shard_map/ppermute | solution.py:48
  12.6 1.5 %collective-permute-start.3 = (bf16[16,4096]{1,0:T(8,128)(2,1)S(1)}, bf16[16,4096]{1,0:T(8,128)(2,1)S(1)}, u32[]{:S(2)}, u32[]{:S(2)}) collective-permute-start(bf16[16,4096]{1,0:T(8,128)(2,1)S(1)} %collective-permute-done.2.refs_2_.refs_1_), channel_id=1, source_target_pairs={{0,1},{1,0},{2,3},{3,2},{4,5},{5,4},{6,7},{7,6},{8,9},{9,8},{10,11... | collective-permute-start | bytes 393224 | tf_op jit(solution)/shard_map/ppermute | solution.py:48
  12.6 6.8 %collective-permute-start.6 = (bf16[32,2048]{1,0:T(8,128)(2,1)S(1)}, bf16[32,2048]{1,0:T(8,128)(2,1)S(1)}, u32[]{:S(2)}, u32[]{:S(2)}) collective-permute-start(bf16[32,2048]{1,0:T(8,128)(2,1)S(1)} %get-tuple-element.29), channel_id=1, source_target_pairs={{0,16},{16,0},{1,17},{17,1},{2,18},{18,2},{3,19},{19,3},{4,20},{20... | collective-permute-start | bytes 393224 | tf_op jit(solution)/shard_map/ppermute | solution.py:44
  17.7 1.7 %collective-permute-start.5 = (bf16[16,4096]{1,0:T(8,128)(2,1)S(1)}, bf16[16,4096]{1,0:T(8,128)(2,1)S(1)}, u32[]{:S(2)}, u32[]{:S(2)}) collective-permute-start(bf16[16,4096]{1,0:T(8,128)(2,1)S(1)} %get-tuple-element.28), channel_id=1, source_target_pairs={{0,1},{1,0},{2,3},{3,2},{4,5},{5,4},{6,7},{7,6},{8,9},{9,8},{10,11... | collective-permute-start | bytes 393224 | tf_op jit(solution)/shard_map/ppermute | solution.py:48
  18.0 5.7 %collective-permute-start.10 = (bf16[32,2048]{1,0:T(8,128)(2,1)S(1)}, bf16[32,2048]{1,0:T(8,128)(2,1)S(1)}, u32[]{:S(2)}, u32[]{:S(2)}) collective-permute-start(bf16[32,2048]{1,0:T(8,128)(2,1)S(1)} %pack.1), channel_id=1, source_target_pairs={{0,16},{16,0},{1,17},{17,1},{2,18},{18,2},{3,19},{19,3},{4,20},{20... | collective-permute-start | bytes 393224 | tf_op jit(solution)/shard_map/ppermute | solution.py:44
  19.3 4.4 %collective-permute-start.4 = (bf16[16,4096]{1,0:T(8,128)(2,1)S(1)}, bf16[16,4096]{1,0:T(8,128)(2,1)S(1)}, u32[]{:S(2)}, u32[]{:S(2)}) collective-permute-start(bf16[16,4096]{1,0:T(8,128)(2,1)S(1)} %get-tuple-element.27), channel_id=1, source_target_pairs={{0,1},{1,0},{2,3},{3,2},{4,5},{5,4},{6,7},{7,6},{8,9},{9,8},{10,11... | collective-permute-start | bytes 393224 | tf_op jit(solution)/shard_map/ppermute | solution.py:48
  19.5 5.9 %collective-permute-start.7 = (bf16[16,4096]{1,0:T(8,128)(2,1)S(1)}, bf16[16,4096]{1,0:T(8,128)(2,1)S(1)}, u32[]{:S(2)}, u32[]{:S(2)}) collective-permute-start(bf16[16,4096]{1,0:T(8,128)(2,1)S(1)} %pair_sums.1), channel_id=1, source_target_pairs={{2,0},{3,1},{0,2},{1,3},{6,4},{7,5},{4,6},{5,7},{10,8},{11,9},{8,1... | collective-permute-start | bytes 393224 | tf_op jit(solution)/shard_map/ppermute | solution.py:55
  21.0 5.9 %collective-permute-start.12 = (bf16[64,1152]{1,0:T(8,128)(2,1)S(1)}, bf16[64,1152]{1,0:T(8,128)(2,1)S(1)}, u32[]{:S(2)}, u32[]{:S(2)}) collective-permute-start(bf16[64,1152]{1,0:T(8,128)(2,1)S(1)} %get-tuple-element.30.factors_ref), channel_id=1, source_target_pairs={{0,16},{16,0},{1,17},{17,1},{2,18},{18,2},{3,19},{19,3},{4,20},{20... | collective-permute-start | bytes 442376 | tf_op jit(solution)/shard_map/ppermute | solution.py:44
  23.8 2.2 %collective-permute-start.9 = (bf16[32,2048]{1,0:T(8,128)(2,1)S(1)}, bf16[32,2048]{1,0:T(8,128)(2,1)S(1)}, u32[]{:S(2)}, u32[]{:S(2)}) collective-permute-start(bf16[32,2048]{1,0:T(8,128)(2,1)S(1)} %collective-permute-done.6.refs_1_.refs_4_), channel_id=1, source_target_pairs={{0,1},{1,0},{2,3},{3,2},{4,5},{5,4},{6,7},{7,6},{8,9},{9,8},{10,11... | collective-permute-start | bytes 393224 | tf_op jit(solution)/shard_map/ppermute | solution.py:48
  23.8 2.2 %collective-permute-start.11 = (bf16[32,2048]{1,0:T(8,128)(2,1)S(1)}, bf16[32,2048]{1,0:T(8,128)(2,1)S(1)}, u32[]{:S(2)}, u32[]{:S(2)}) collective-permute-start(bf16[32,2048]{1,0:T(8,128)(2,1)S(1)} %collective-permute-done.10.refs_6_), channel_id=1, source_target_pairs={{0,1},{1,0},{2,3},{3,2},{4,5},{5,4},{6,7},{7,6},{8,9},{9,8},{10,11... | collective-permute-start | bytes 393224 | tf_op jit(solution)/shard_map/ppermute | solution.py:48
  25.4 5.2 %collective-permute-start.8 = (bf16[16,4224]{1,0:T(8,128)(2,1)S(1)}, bf16[16,4224]{1,0:T(8,128)(2,1)S(1)}, u32[]{:S(2)}, u32[]{:S(2)}) collective-permute-start(bf16[16,4224]{1,0:T(8,128)(2,1)S(1)} %sum_returned.1), channel_id=1, source_target_pairs={{0,12},{4,0},{8,4},{12,8},{1,13},{5,1},{9,5},{13,9},{2,14},{6,2},{... | collective-permute-start | bytes 405512 | tf_op jit(solution)/shard_map/ppermute | solution.py:60

commit v7 on v6

--- a/solution.py
+++ b/solution.py
@@ -64,9 +64,10 @@
     return lax.dot_general(left, right, dims, preferred_element_type=F32)
 
 
-def run(body, name, outs, inputs, flops, in_specs=None, out_specs=None, scratch=(), aliases=None):
+def run(body, name, outs, inputs, flops, moved=None, in_specs=None, out_specs=None, scratch=(), aliases=None):
     vmem = pl.BlockSpec(memory_space=pltpu.VMEM)
-    moved = sum(v.size * v.dtype.itemsize for v in inputs)
+    if moved is None:
+        moved = sum(v.size * v.dtype.itemsize for v in inputs)
     return pl.pallas_call(
         body,
         name=name,
@@ -116,8 +117,26 @@
     return jnp.where(is_late > 0.5, F32(-1.0), rank), late_row, weighting
 
 
+def store_late(both, weighting, incoming, picked_ref, routed_ref):
+    picked = mm(both[-picked_ref.shape[0] :], incoming, ROWS_COLS)
+    picked_ref[...] = picked.astype(BF16)
+    routed_ref[...] = (picked * weighting).astype(BF16)
+
+
 def route_body(
-    routing_hbm, gates_hbm, incoming_hbm, early_ref, routed_ref, picked_ref, ids_ref, routing_ref, gates_ref, incoming_ref, sems
+    routing_hbm,
+    gates_hbm,
+    incoming_hbm,
+    early_ref,
+    picked_ref,
+    routed_ref,
+    both_ref,
+    weighting_ref,
+    ids_ref,
+    incoming_ref,
+    routing_ref,
+    gates_ref,
+    sems,
 ):
     capacity, width = routed_ref.shape
     fetches = [
@@ -132,6 +151,8 @@
     early = early_ref.shape[0]
     early_row, late_row, weighting = choose_late(routing_ref[...], gates_ref[...], capacity)
     both = sorting(early_row, late_row, early + capacity, capacity)
+    both_ref[...] = both
+    weighting_ref[...] = jnp.broadcast_to(weighting, weighting_ref.shape)
     digits = [d for row in (early_row, late_row) for d in (row.astype(jnp.int32) >> 7, row.astype(jnp.int32) & 127)]
     number = lax.broadcasted_iota(jnp.int32, ids_ref.shape, 0)
     ids = digits[3]
@@ -142,10 +163,17 @@
     step = min(width, 1024)
     for c in range(width // step):
         at = slice(c * step, (c + 1) * step)
-        sorted_rows = mm(both, incoming_ref[:, at], ROWS_COLS)
-        early_ref[:, at] = sorted_rows[:early].astype(BF16)
-        picked_ref[:, at] = sorted_rows[early:].astype(BF16)
-        routed_ref[:, at] = (sorted_rows[early:] * weighting).astype(BF16)
+        early_ref[:, at] = mm(both[:early], incoming_ref[:, at], ROWS_COLS).astype(BF16)
+
+    @pl.when(lax.axis_index("pipe") == 0)
+    def _():
+        store_late(both, weighting, incoming_ref[...], picked_ref, routed_ref)
+
+
+def route_late_body(incoming_ref, both_ref, weighting_ref, _, __, picked_ref, routed_ref):
+    @pl.when(lax.axis_index("pipe") > 0)
+    def _():
+        store_late(both_ref[...], weighting_ref[:, :1], incoming_ref[...], picked_ref, routed_ref)
 
 
 def forward_body(saved_ref, weights_ref, slope_ref, active_ref, hidden_ref, rows_ref, *fars):
@@ -303,26 +331,33 @@
     saved = saved_inputs[0, 0, 0]
 
     early = tokens - capacity
-    early_rows, routed, picked, ids = run(
+    late_outs = [out((capacity, width), BF16)] * 2
+    early_rows, picked, routed, both, weighting, ids, incoming = run(
         route_body,
         "route",
         [
             out((early, width), BF16),
-            out((capacity, width), BF16),
-            out((capacity, width), BF16),
+            *late_outs,
+            out((tokens, tokens), BF16),
+            out((capacity, LANES), F32),
             out((capacity, tokens), BF16),
+            out((tokens, width), BF16),
         ],
         [in_hbm(v) for v in (jnp.transpose(routing[0, 0]), jnp.transpose(gate_values[0, 0]), incoming)],
+        0,
+        moved=0,
+        in_specs=[hbm] * 3,
+        scratch=[pltpu.VMEM((top, tokens), jnp.int32), pltpu.VMEM((top, tokens), F32), pltpu.SemaphoreType.DMA((3,))],
+    )
+    shifted = to_previous(early_rows)
+    picked, routed = run(
+        route_late_body,
+        "route_late",
+        late_outs,
+        [incoming, both, weighting, picked, routed],
         ROUTE_COST,
-        in_specs=[hbm] * 3,
-        scratch=[
-            pltpu.VMEM((top, tokens), jnp.int32),
-            pltpu.VMEM((top, tokens), F32),
-            pltpu.VMEM((tokens, width), BF16),
-            pltpu.SemaphoreType.DMA((3,)),
-        ],
-    )
-    shifted = to_previous(early_rows)
+        aliases={3: 0, 4: 1},
+    )
     distant = [to_pair(routed, j) for j in range(1, outer)]
     arrived = [to_sibling(routed)] if inner == 2 else []
 

time: 32 us -> 32 us (level)
  waiting for transfers between devices: 6.5 us -> 5.12 us
  local copies, waits for them, and re-layouts: 0.01 us -> 1.09 us
    unnamed x4 -> x8, local copies, waits for them, and re-layouts: 0.01 us -> 1.09 us
    ppermute x2, waiting for transfers between devices: 2.69 us -> 1.61 us  [to_pair(): lax.ppermute(value, 'expert', [(j, i) for i, j in hops] if back else hops)]
    pallas_call x8 -> x9, Pallas kernels: 11.2 us -> 11.4 us  [run(): pl.pallas_call(body, name=name, out_shape=outs, in_specs=in_specs or [vme...]
where the time goes in v7:
time: 32 us; the launch traced here: 31.9 us
  starting transfers between devices  13.5 us (42%)
  Pallas kernels  11.4 us (36%)
  waiting for transfers between devices  5.12 us (16%)
  local copies, waits for them, and re-layouts  1.09 us (3%)
  between operations  0.7 us (2%)
    pallas_call x9, Pallas kernels, run(): pl.pallas_call(body, name=name, out_shape=outs, in_specs=in_specs or [vme...  11.4 us
    ppermute x2, starting transfers between devices, to_previous(): lax.ppermute(value, 'pipe', [(i, (i - 1) % count) for i in range(count)])  5.67 us
    ppermute x3, starting transfers between devices, exchange(): lax.ppermute(value, axis, [(i, partner(i, step, count)) for i in range(co...  3.86 us
    ppermute x2, starting transfers between devices, to_pair(): lax.ppermute(value, 'expert', [(j, i) for i, j in hops] if back else hops)  3.1 us
    ppermute x3, waiting for transfers between devices, exchange(): lax.ppermute(value, axis, [(i, partner(i, step, count)) for i in range(co...  2.39 us
    ppermute x2, waiting for transfers between devices, to_pair(): lax.ppermute(value, 'expert', [(j, i) for i, j in hops] if back else hops)  1.61 us
    ppermute x2, waiting for transfers between devices, to_previous(): lax.ppermute(value, 'pipe', [(i, (i - 1) % count) for i in range(count)])  1.11 us
    unnamed x8, local copies, waits for them, and re-layouts  1.09 us
  transfers between devices with their start and end apart: 13, of which 5 were waited for; matrix products, arithmetic and copies ran while one was open for 0% of the time, Pallas kernels for 25%

profile of v7, /device:TPU:0, one launch (start us, length us, event | category | flops | bytes accessed | tf_op | source)
XLA Modules:
  0.0 31.9 jit_solution(8631876868713892908)
XLA Ops:
  0.6 0.0 slice-start
  0.6 2.1 %route.1 = (bf16[112,4096]{1,0:T(8,128)(2,1)S(1)}, bf16[16,4096]{1,0:T(8,128)(2,1)S(1)}, bf16[16,4096]{1,0:T(8,128)(2,1)S(1)}, bf16[128,128]{1,0:T(8,128)(2,1)S(...) custom-call(s32[8,128]{1,0:T(8,128)} %bitcast.15, f32[8,128]{1,0:T(8,128)} %bitcast.16, ...), custom_call_target="tpu_custom_call" | custom-call | tf_op jit(solution)/shard_map/route/pallas_call | solution.py:71
  2.7 4.9 %collective-permute-start = (bf16[112,4096]{1,0:T(8,128)(2,1)S(1)}, bf16[112,4096]{1,0:T(8,128)(2,1)S(1)}, u32[]{:S(2)}, u32[]{:S(2)}) collective-permute-start(bf16[112,4096]{1,0:T(8,128)(2,1)S(1)} %get-tuple-element.22), channel_id=1, source_target_pairs={{0,12},{4,0},{8,4},{12,8},{1,13},{5,1},{9,5},{13,9},{2,14},{6,2},{... | collective-permute-start | bytes 2752520 | tf_op jit(solution)/shard_map/ppermute | solution.py:60
  7.6 0.0 slice-start.1
  7.6 0.0 slice-start.2
  7.6 0.0 copy-start
  7.6 1.5 %collective-permute-start.2 = (bf16[16,4096]{1,0:T(8,128)(2,1)S(1)}, bf16[16,4096]{1,0:T(8,128)(2,1)S(1)}, u32[]{:S(2)}, u32[]{:S(2)}) collective-permute-start(bf16[16,4096]{1,0:T(8,128)(2,1)S(1)} %get-tuple-element.30.refs_0_), channel_id=1, source_target_pairs={{0,2},{1,3},{2,0},{3,1},{4,6},{5,7},{6,4},{7,5},{8,10},{9,11},{10,... | collective-permute-start | bytes 393224 | tf_op jit(solution)/shard_map/ppermute | solution.py:55
  9.1 0.0 collective-permute-start.1
  9.1 0.0 slice-done
  9.1 0.7 %slice-done.1 = s8[4194304]{0:T(1024)(128)(4,1)S(1)} async-done(((s8[9437184]{0:T(1024)(128)(4,1)}), s8[4194304]{0:T(1024)(128)(4,1)S(1)}, s32[]{:S(2)}) %slice-start.1) | async-done | bytes 4194328
  9.8 0.3 slice-done.2
  10.1 0.1 copy-done
  10.2 1.8 %forward.1 = (f32[384,64]{1,0:T(8,128)S(1)}, f32[384,64]{1,0:T(8,128)S(1)}, bf16[64,384]{1,0:T(8,128)(2,1)S(1)}, bf16[64,4096]{1,0:T(8,128)(2,1)S(1)}, bf16[32,2048]{1,0:T(8,128)(2,1)S(1)}) custom-call(bf16[4,16,4096]{2,1,0:T(8,128)(2,1)S(1)} %bitcast.13, bf16[3,384,4096]{2,1,0:T(8,128)(2,1)S(1)} %bitcast.11), custom_call_target="tpu_custom_call" | custom-call | flops 402653184 | bytes 9961472 | tf_op jit(solution)/shard_map/forward/pallas_call | solution.py:71
  12.0 0.5 %collective-permute-done.2.refs_2_.refs_1_ = bf16[16,4096]{1,0:T(8,128)(2,1)S(1)} collective-permute-done((bf16[16,4096]{1,0:T(8,128)(2,1)S(1)}, bf16[16,4096]{1,0:T(8,128)(2,1)S(1)}, u32[]{:S(2)}, u32[]{:S(2)}) %collective-permute-start.2) | collective-permute-done | bytes 131104 | tf_op jit(solution)/shard_map/ppermute | solution.py:55
  12.6 0.0 collective-permute-start.3
  12.6 1.5 %collective-permute-start.6 = (bf16[32,2048]{1,0:T(8,128)(2,1)S(1)}, bf16[32,2048]{1,0:T(8,128)(2,1)S(1)}, u32[]{:S(2)}, u32[]{:S(2)}) collective-permute-start(bf16[32,2048]{1,0:T(8,128)(2,1)S(1)} %get-tuple-element.39), channel_id=1, source_target_pairs={{0,16},{16,0},{1,17},{17,1},{2,18},{18,2},{3,19},{19,3},{4,20},{20... | collective-permute-start | bytes 393224 | tf_op jit(solution)/shard_map/ppermute | solution.py:44
  14.1 0.0 collective-permute-done.1.refs_1_
  14.1 0.0 collective-permute-done.3.refs_3_
  14.1 3.6 %backward.1 = (bf16[32,4096]{1,0:T(8,128)(2,1)S(1)}, bf16[64,1152]{1,0:T(8,128)(2,1)S(1)}, bf16[16,4096]{1,0:T(8,128)(2,1)S(1)}, bf16[16,4096]{1,0:T(8,128)(2,1)S(1)}) custom-call(bf16[16,4096]{1,0:T(8,128)(2,1)S(1)} %get-tuple-element.30.refs_0_, bf16[16,4096]{1,0:T(8,128)(2,1)S(1)} %collective-permute-done.1.refs_1_, ...), custom_call_target="tpu_custom_call" | custom-call | flops 603979776 | bytes 10207232 | tf_op jit(solution)/shard_map/backward/pallas_call | solution.py:71
  17.7 0.3 collective-permute-start.5
  18.0 1.3 %collective-permute-start.10 = (bf16[32,2048]{1,0:T(8,128)(2,1)S(1)}, bf16[32,2048]{1,0:T(8,128)(2,1)S(1)}, u32[]{:S(2)}, u32[]{:S(2)}) collective-permute-start(bf16[32,2048]{1,0:T(8,128)(2,1)S(1)} %pack.1), channel_id=1, source_target_pairs={{0,16},{16,0},{1,17},{17,1},{2,18},{18,2},{3,19},{19,3},{4,20},{20... | collective-permute-start | bytes 393224 | tf_op jit(solution)/shard_map/ppermute | solution.py:44
  19.3 0.1 collective-permute-start.4
  19.4 0.0 collective-permute-done.6.refs_1_.refs_4_
  19.4 0.0 collective-permute-done.5.refs_0_
  19.4 1.6 %collective-permute-start.7 = (bf16[16,4096]{1,0:T(8,128)(2,1)S(1)}, bf16[16,4096]{1,0:T(8,128)(2,1)S(1)}, u32[]{:S(2)}, u32[]{:S(2)}) collective-permute-start(bf16[16,4096]{1,0:T(8,128)(2,1)S(1)} %pair_sums.1), channel_id=1, source_target_pairs={{2,0},{3,1},{0,2},{1,3},{6,4},{7,5},{4,6},{5,7},{10,8},{11,9},{8,1... | collective-permute-start | bytes 393224 | tf_op jit(solution)/shard_map/ppermute | solution.py:55
  21.0 1.0 %collective-permute-start.12 = (bf16[64,1152]{1,0:T(8,128)(2,1)S(1)}, bf16[64,1152]{1,0:T(8,128)(2,1)S(1)}, u32[]{:S(2)}, u32[]{:S(2)}) collective-permute-start(bf16[64,1152]{1,0:T(8,128)(2,1)S(1)} %get-tuple-element.40.factors_ref), channel_id=1, source_target_pairs={{0,16},{16,0},{1,17},{17,1},{2,18},{18,2},{3,19},{19,3},{4,20},{20... | collective-permute-start | bytes 442376 | tf_op jit(solution)/shard_map/ppermute | solution.py:44
  22.0 1.7 %collective-permute-done.10.refs_6_ = bf16[32,2048]{1,0:T(8,128)(2,1)S(1)} collective-permute-done((bf16[32,2048]{1,0:T(8,128)(2,1)S(1)}, bf16[32,2048]{1,0:T(8,128)(2,1)S(1)}, u32[]{:S(2)}, u32[]{:S(2)}) %collective-permute-start.10) | collective-permute-done | bytes 131104 | tf_op jit(solution)/shard_map/ppermute | solution.py:44
  23.7 0.0 collective-permute-start.9
  23.7 0.0 collective-permute-done.4.refs_0_
  23.7 0.5 %collective-permute-start.11 = (bf16[32,2048]{1,0:T(8,128)(2,1)S(1)}, bf16[32,2048]{1,0:T(8,128)(2,1)S(1)}, u32[]{:S(2)}, u32[]{:S(2)}) collective-permute-start(bf16[32,2048]{1,0:T(8,128)(2,1)S(1)} %collective-permute-done.10.refs_6_), channel_id=1, source_target_pairs={{0,1},{1,0},{2,3},{3,2},{4,5},{5,4},{6,7},{7,6},{8,9},{9,8},{10,11... | collective-permute-start | bytes 393224 | tf_op jit(solution)/shard_map/ppermute | solution.py:48
  24.2 1.1 %collective-permute-done.7.refs_1_ = bf16[16,4096]{1,0:T(8,128)(2,1)S(1)} collective-permute-done((bf16[16,4096]{1,0:T(8,128)(2,1)S(1)}, bf16[16,4096]{1,0:T(8,128)(2,1)S(1)}, u32[]{:S(2)}, u32[]{:S(2)}) %collective-permute-start.7) | collective-permute-done | bytes 131104 | tf_op jit(solution)/shard_map/ppermute | solution.py:55
  25.3 0.1 sum_returned.1
  25.4 0.8 %collective-permute-start.8 = (bf16[16,4224]{1,0:T(8,128)(2,1)S(1)}, bf16[16,4224]{1,0:T(8,128)(2,1)S(1)}, u32[]{:S(2)}, u32[]{:S(2)}) collective-permute-start(bf16[16,4224]{1,0:T(8,128)(2,1)S(1)} %sum_returned.1), channel_id=1, source_target_pairs={{0,12},{4,0},{8,4},{12,8},{1,13},{5,1},{9,5},{13,9},{2,14},{6,2},{... | collective-permute-start | bytes 405512 | tf_op jit(solution)/shard_map/ppermute | solution.py:60
  26.2 0.0 collective-permute-done.9.refs_5_
  26.2 0.0 collective-permute-done.11.refs_7_
  26.2 0.7 %collective-permute-done.12.refs_8_ = bf16[64,1152]{1,0:T(8,128)(2,1)S(1)} collective-permute-done((bf16[64,1152]{1,0:T(8,128)(2,1)S(1)}, bf16[64,1152]{1,0:T(8,128)(2,1)S(1)}, u32[]{:S(2)}, u32[]{:S(2)}) %collective-permute-start.12) | collective-permute-done | bytes 147488 | tf_op jit(solution)/shard_map/ppermute | solution.py:44
  26.9 2.6 %weight_grads.1 = bf16[1,3,384,2048]{3,2,1,0:T(8,128)(2,1)} custom-call(bf16[64,1152]{1,0:T(8,128)(2,1)S(1)} %get-tuple-element.40.factors_ref, bf16[64,4096]{1,0:T(8,128)(2,1)S(1)} %get-tuple-element.41.inputs_ref, bf16[16,4096]{1,0:T(8,128)(2,1)S(1)} %get-tuple-element.30.refs_0_, bf16[16,4096]{1,0:T(8,128)(2,1)S(1)} %collective-permute-done.1.refs_1_, ...), custom_call_target="tpu_custom_call" | custom-call | flops 603979776 | bytes 1867776 | tf_op jit(solution)/shard_map/weight_grads/pallas_call | solution.py:71
  29.5 1.1 %collective-permute-done.8.changed_ref = bf16[16,4224]{1,0:T(8,128)(2,1)S(1)} collective-permute-done((bf16[16,4224]{1,0:T(8,128)(2,1)S(1)}, bf16[16,4224]{1,0:T(8,128)(2,1)S(1)}, u32[]{:S(2)}, u32[]{:S(2)}) %collective-permute-start.8) | collective-permute-done | bytes 135200 | tf_op jit(solution)/shard_map/ppermute | solution.py:60
  30.6 0.0 collective-permute-done.early_ref
  30.6 1.3 %merge.1 = bf16[1,1,128,4096]{3,2,1,0:T(8,128)(2,1)} custom-call(bf16[112,4096]{1,0:T(8,128)(2,1)S(1)} %collective-permute-done.early_ref, bf16[16,4224]{1,0:T(8,128)(2,1)S(1)} %collective-permute-done.8.changed_ref), custom_call_target="tpu_custom_call" | custom-call | flops 16777216 | bytes 1052672 | tf_op jit(solution)/shard_map/merge/pallas_call | solution.py:71
  (4 shorter events, 0.0 us)
Async XLA Ops:
  0.6 8.5 %slice-start = ((s8[9437184]{0:T(1024)(128)(4,1)}), s8[4194304]{0:T(1024)(128)(4,1)S(1)}, s32[]{:S(2)}) async-start(s8[9437184]{0:T(1024)(128)(4,1)} %bitcast.9), calls=%async_computation | async-start | bytes 8388608
  2.7 27.9 %collective-permute-start = (bf16[112,4096]{1,0:T(8,128)(2,1)S(1)}, bf16[112,4096]{1,0:T(8,128)(2,1)S(1)}, u32[]{:S(2)}, u32[]{:S(2)}) collective-permute-start(bf16[112,4096]{1,0:T(8,128)(2,1)S(1)} %get-tuple-element.22), channel_id=1, source_target_pairs={{0,12},{4,0},{8,4},{12,8},{1,13},{5,1},{9,5},{13,9},{2,14},{6,2},{... | collective-permute-start | bytes 2752520 | tf_op jit(solution)/shard_map/ppermute | solution.py:60
  7.6 2.2 %slice-start.1 = ((s8[9437184]{0:T(1024)(128)(4,1)}), s8[4194304]{0:T(1024)(128)(4,1)S(1)}, s32[]{:S(2)}) async-start(s8[9437184]{0:T(1024)(128)(4,1)} %bitcast.9), calls=%async_computation.1 | async-start | bytes 8388608
  7.6 2.5 %slice-start.2 = ((s8[9437184]{0:T(1024)(128)(4,1)}), s8[1048576]{0:T(1024)(128)(4,1)S(1)}, s32[]{:S(2)}) async-start(s8[9437184]{0:T(1024)(128)(4,1)} %bitcast.9), calls=%async_computation.2 | async-start | bytes 2097152
  7.6 2.6 %copy-start = (bf16[1,1,1,4,16,4096]{5,4,3,2,1,0:T(8,128)(2,1)S(1)}, bf16[1,1,1,4,16,4096]{5,4,3,2,1,0:T(8,128)(2,1)}, u32[]{:S(2)}) copy-start(bf16[1,1,1,4,16,4096]{5,4,3,2,1,0:T(8,128)(2,1)} %param.8) | copy-start | bytes 1572868
  7.6 5.0 %collective-permute-start.2 = (bf16[16,4096]{1,0:T(8,128)(2,1)S(1)}, bf16[16,4096]{1,0:T(8,128)(2,1)S(1)}, u32[]{:S(2)}, u32[]{:S(2)}) collective-permute-start(bf16[16,4096]{1,0:T(8,128)(2,1)S(1)} %get-tuple-element.30.refs_0_), channel_id=1, source_target_pairs={{0,2},{1,3},{2,0},{3,1},{4,6},{5,7},{6,4},{7,5},{8,10},{9,11},{10,... | collective-permute-start | bytes 393224 | tf_op jit(solution)/shard_map/ppermute | solution.py:55
  9.1 4.9 %collective-permute-start.1 = (bf16[16,4096]{1,0:T(8,128)(2,1)S(1)}, bf16[16,4096]{1,0:T(8,128)(2,1)S(1)}, u32[]{:S(2)}, u32[]{:S(2)}) collective-permute-start(bf16[16,4096]{1,0:T(8,128)(2,1)S(1)} %get-tuple-element.30.refs_0_), channel_id=1, source_target_pairs={{0,1},{1,0},{2,3},{3,2},{4,5},{5,4},{6,7},{7,6},{8,9},{9,8},{10,11... | collective-permute-start | bytes 393224 | tf_op jit(solution)/shard_map/ppermute | solution.py:48
  12.6 1.5 %collective-permute-start.3 = (bf16[16,4096]{1,0:T(8,128)(2,1)S(1)}, bf16[16,4096]{1,0:T(8,128)(2,1)S(1)}, u32[]{:S(2)}, u32[]{:S(2)}) collective-permute-start(bf16[16,4096]{1,0:T(8,128)(2,1)S(1)} %collective-permute-done.2.refs_2_.refs_1_), channel_id=1, source_target_pairs={{0,1},{1,0},{2,3},{3,2},{4,5},{5,4},{6,7},{7,6},{8,9},{9,8},{10,11... | collective-permute-start | bytes 393224 | tf_op jit(solution)/shard_map/ppermute | solution.py:48
  12.6 6.8 %collective-permute-start.6 = (bf16[32,2048]{1,0:T(8,128)(2,1)S(1)}, bf16[32,2048]{1,0:T(8,128)(2,1)S(1)}, u32[]{:S(2)}, u32[]{:S(2)}) collective-permute-start(bf16[32,2048]{1,0:T(8,128)(2,1)S(1)} %get-tuple-element.39), channel_id=1, source_target_pairs={{0,16},{16,0},{1,17},{17,1},{2,18},{18,2},{3,19},{19,3},{4,20},{20... | collective-permute-start | bytes 393224 | tf_op jit(solution)/shard_map/ppermute | solution.py:44
  17.7 1.7 %collective-permute-start.5 = (bf16[16,4096]{1,0:T(8,128)(2,1)S(1)}, bf16[16,4096]{1,0:T(8,128)(2,1)S(1)}, u32[]{:S(2)}, u32[]{:S(2)}) collective-permute-start(bf16[16,4096]{1,0:T(8,128)(2,1)S(1)} %get-tuple-element.38), channel_id=1, source_target_pairs={{0,1},{1,0},{2,3},{3,2},{4,5},{5,4},{6,7},{7,6},{8,9},{9,8},{10,11... | collective-permute-start | bytes 393224 | tf_op jit(solution)/shard_map/ppermute | solution.py:48
  18.0 5.8 %collective-permute-start.10 = (bf16[32,2048]{1,0:T(8,128)(2,1)S(1)}, bf16[32,2048]{1,0:T(8,128)(2,1)S(1)}, u32[]{:S(2)}, u32[]{:S(2)}) collective-permute-start(bf16[32,2048]{1,0:T(8,128)(2,1)S(1)} %pack.1), channel_id=1, source_target_pairs={{0,16},{16,0},{1,17},{17,1},{2,18},{18,2},{3,19},{19,3},{4,20},{20... | collective-permute-start | bytes 393224 | tf_op jit(solution)/shard_map/ppermute | solution.py:44
  19.3 4.4 %collective-permute-start.4 = (bf16[16,4096]{1,0:T(8,128)(2,1)S(1)}, bf16[16,4096]{1,0:T(8,128)(2,1)S(1)}, u32[]{:S(2)}, u32[]{:S(2)}) collective-permute-start(bf16[16,4096]{1,0:T(8,128)(2,1)S(1)} %get-tuple-element.37), channel_id=1, source_target_pairs={{0,1},{1,0},{2,3},{3,2},{4,5},{5,4},{6,7},{7,6},{8,9},{9,8},{10,11... | collective-permute-start | bytes 393224 | tf_op jit(solution)/shard_map/ppermute | solution.py:48
  19.4 5.9 %collective-permute-start.7 = (bf16[16,4096]{1,0:T(8,128)(2,1)S(1)}, bf16[16,4096]{1,0:T(8,128)(2,1)S(1)}, u32[]{:S(2)}, u32[]{:S(2)}) collective-permute-start(bf16[16,4096]{1,0:T(8,128)(2,1)S(1)} %pair_sums.1), channel_id=1, source_target_pairs={{2,0},{3,1},{0,2},{1,3},{6,4},{7,5},{4,6},{5,7},{10,8},{11,9},{8,1... | collective-permute-start | bytes 393224 | tf_op jit(solution)/shard_map/ppermute | solution.py:55
  21.0 5.9 %collective-permute-start.12 = (bf16[64,1152]{1,0:T(8,128)(2,1)S(1)}, bf16[64,1152]{1,0:T(8,128)(2,1)S(1)}, u32[]{:S(2)}, u32[]{:S(2)}) collective-permute-start(bf16[64,1152]{1,0:T(8,128)(2,1)S(1)} %get-tuple-element.40.factors_ref), channel_id=1, source_target_pairs={{0,16},{16,0},{1,17},{17,1},{2,18},{18,2},{3,19},{19,3},{4,20},{20... | collective-permute-start | bytes 442376 | tf_op jit(solution)/shard_map/ppermute | solution.py:44
  23.7 2.5 %collective-permute-start.9 = (bf16[32,2048]{1,0:T(8,128)(2,1)S(1)}, bf16[32,2048]{1,0:T(8,128)(2,1)S(1)}, u32[]{:S(2)}, u32[]{:S(2)}) collective-permute-start(bf16[32,2048]{1,0:T(8,128)(2,1)S(1)} %collective-permute-done.6.refs_1_.refs_4_), channel_id=1, source_target_pairs={{0,1},{1,0},{2,3},{3,2},{4,5},{5,4},{6,7},{7,6},{8,9},{9,8},{10,11... | collective-permute-start | bytes 393224 | tf_op jit(solution)/shard_map/ppermute | solution.py:48
  23.7 2.5 %collective-permute-start.11 = (bf16[32,2048]{1,0:T(8,128)(2,1)S(1)}, bf16[32,2048]{1,0:T(8,128)(2,1)S(1)}, u32[]{:S(2)}, u32[]{:S(2)}) collective-permute-start(bf16[32,2048]{1,0:T(8,128)(2,1)S(1)} %collective-permute-done.10.refs_6_), channel_id=1, source_target_pairs={{0,1},{1,0},{2,3},{3,2},{4,5},{5,4},{6,7},{7,6},{8,9},{9,8},{10,11... | collective-permute-start | bytes 393224 | tf_op jit(solution)/shard_map/ppermute | solution.py:48
  25.4 5.2 %collective-permute-start.8 = (bf16[16,4224]{1,0:T(8,128)(2,1)S(1)}, bf16[16,4224]{1,0:T(8,128)(2,1)S(1)}, u32[]{:S(2)}, u32[]{:S(2)}) collective-permute-start(bf16[16,4224]{1,0:T(8,128)(2,1)S(1)} %sum_returned.1), channel_id=1, source_target_pairs={{0,12},{4,0},{8,4},{12,8},{1,13},{5,1},{9,5},{13,9},{2,14},{6,2},{... | collective-permute-start | bytes 405512 | tf_op jit(solution)/shard_map/ppermute | solution.py:60

commit v8 on v7

--- a/solution.py
+++ b/solution.py
@@ -144,7 +144,7 @@
         pltpu.make_async_copy(gates_hbm, gates_ref, sems.at[1]),
         pltpu.make_async_copy(incoming_hbm, incoming_ref, sems.at[2]),
     ]
-    for f in fetches:
+    for f in reversed(fetches):
         f.start()
     for f in fetches[:2]:
         f.wait()

time: 32 us -> 32 us (level)
  no operation moved by 1% of the time
where the time goes in v8:
time: 32 us; the launch traced here: 31.8 us
  starting transfers between devices  13.5 us (42%)
  Pallas kernels  11.4 us (36%)
  waiting for transfers between devices  5.13 us (16%)
  local copies, waits for them, and re-layouts  1.09 us (3%)
  between operations  0.7 us (2%)
    pallas_call x9, Pallas kernels, run(): pl.pallas_call(body, name=name, out_shape=outs, in_specs=in_specs or [vme...  11.4 us
    ppermute x2, starting transfers between devices, to_previous(): lax.ppermute(value, 'pipe', [(i, (i - 1) % count) for i in range(count)])  5.67 us
    ppermute x3, starting transfers between devices, exchange(): lax.ppermute(value, axis, [(i, partner(i, step, count)) for i in range(co...  3.86 us
    ppermute x2, starting transfers between devices, to_pair(): lax.ppermute(value, 'expert', [(j, i) for i, j in hops] if back else hops)  3.1 us
    ppermute x3, waiting for transfers between devices, exchange(): lax.ppermute(value, axis, [(i, partner(i, step, count)) for i in range(co...  2.38 us
    ppermute x2, waiting for transfers between devices, to_pair(): lax.ppermute(value, 'expert', [(j, i) for i, j in hops] if back else hops)  1.62 us
    ppermute x2, waiting for transfers between devices, to_previous(): lax.ppermute(value, 'pipe', [(i, (i - 1) % count) for i in range(count)])  1.11 us
    unnamed x8, local copies, waits for them, and re-layouts  1.09 us
  transfers between devices with their start and end apart: 13, of which 5 were waited for; matrix products, arithmetic and copies ran while one was open for 0% of the time, Pallas kernels for 25%

profile of v8, /device:TPU:0, one launch (start us, length us, event | category | flops | bytes accessed | tf_op | source)
XLA Modules:
  0.0 31.8 jit_solution(16693837753092378663)
XLA Ops:
  0.6 0.0 slice-start
  0.6 2.1 %route.1 = (bf16[112,4096]{1,0:T(8,128)(2,1)S(1)}, bf16[16,4096]{1,0:T(8,128)(2,1)S(1)}, bf16[16,4096]{1,0:T(8,128)(2,1)S(1)}, bf16[128,128]{1,0:T(8,128)(2,1)S(...) custom-call(s32[8,128]{1,0:T(8,128)} %bitcast.15, f32[8,128]{1,0:T(8,128)} %bitcast.16, ...), custom_call_target="tpu_custom_call" | custom-call | tf_op jit(solution)/shard_map/route/pallas_call | solution.py:71
  2.7 4.9 %collective-permute-start = (bf16[112,4096]{1,0:T(8,128)(2,1)S(1)}, bf16[112,4096]{1,0:T(8,128)(2,1)S(1)}, u32[]{:S(2)}, u32[]{:S(2)}) collective-permute-start(bf16[112,4096]{1,0:T(8,128)(2,1)S(1)} %get-tuple-element.22), channel_id=1, source_target_pairs={{0,12},{4,0},{8,4},{12,8},{1,13},{5,1},{9,5},{13,9},{2,14},{6,2},{... | collective-permute-start | bytes 2752520 | tf_op jit(solution)/shard_map/ppermute | solution.py:60
  7.6 0.0 slice-start.1
  7.6 0.0 slice-start.2
  7.6 0.0 copy-start
  7.6 1.5 %collective-permute-start.2 = (bf16[16,4096]{1,0:T(8,128)(2,1)S(1)}, bf16[16,4096]{1,0:T(8,128)(2,1)S(1)}, u32[]{:S(2)}, u32[]{:S(2)}) collective-permute-start(bf16[16,4096]{1,0:T(8,128)(2,1)S(1)} %get-tuple-element.30.refs_0_), channel_id=1, source_target_pairs={{0,2},{1,3},{2,0},{3,1},{4,6},{5,7},{6,4},{7,5},{8,10},{9,11},{10,... | collective-permute-start | bytes 393224 | tf_op jit(solution)/shard_map/ppermute | solution.py:55
  9.1 0.0 collective-permute-start.1
  9.1 0.0 slice-done
  9.1 0.7 %slice-done.1 = s8[4194304]{0:T(1024)(128)(4,1)S(1)} async-done(((s8[9437184]{0:T(1024)(128)(4,1)}), s8[4194304]{0:T(1024)(128)(4,1)S(1)}, s32[]{:S(2)}) %slice-start.1) | async-done | bytes 4194328
  9.8 0.3 slice-done.2
  10.1 0.1 copy-done
  10.2 1.8 %forward.1 = (f32[384,64]{1,0:T(8,128)S(1)}, f32[384,64]{1,0:T(8,128)S(1)}, bf16[64,384]{1,0:T(8,128)(2,1)S(1)}, bf16[64,4096]{1,0:T(8,128)(2,1)S(1)}, bf16[32,2048]{1,0:T(8,128)(2,1)S(1)}) custom-call(bf16[4,16,4096]{2,1,0:T(8,128)(2,1)S(1)} %bitcast.13, bf16[3,384,4096]{2,1,0:T(8,128)(2,1)S(1)} %bitcast.11), custom_call_target="tpu_custom_call" | custom-call | flops 402653184 | bytes 9961472 | tf_op jit(solution)/shard_map/forward/pallas_call | solution.py:71
  12.0 0.5 %collective-permute-done.2.refs_2_.refs_1_ = bf16[16,4096]{1,0:T(8,128)(2,1)S(1)} collective-permute-done((bf16[16,4096]{1,0:T(8,128)(2,1)S(1)}, bf16[16,4096]{1,0:T(8,128)(2,1)S(1)}, u32[]{:S(2)}, u32[]{:S(2)}) %collective-permute-start.2) | collective-permute-done | bytes 131104 | tf_op jit(solution)/shard_map/ppermute | solution.py:55
  12.6 0.0 collective-permute-start.3
  12.6 1.5 %collective-permute-start.6 = (bf16[32,2048]{1,0:T(8,128)(2,1)S(1)}, bf16[32,2048]{1,0:T(8,128)(2,1)S(1)}, u32[]{:S(2)}, u32[]{:S(2)}) collective-permute-start(bf16[32,2048]{1,0:T(8,128)(2,1)S(1)} %get-tuple-element.39), channel_id=1, source_target_pairs={{0,16},{16,0},{1,17},{17,1},{2,18},{18,2},{3,19},{19,3},{4,20},{20... | collective-permute-start | bytes 393224 | tf_op jit(solution)/shard_map/ppermute | solution.py:44
  14.0 0.0 collective-permute-done.1.refs_1_
  14.1 0.0 collective-permute-done.3.refs_3_
  14.1 3.6 %backward.1 = (bf16[32,4096]{1,0:T(8,128)(2,1)S(1)}, bf16[64,1152]{1,0:T(8,128)(2,1)S(1)}, bf16[16,4096]{1,0:T(8,128)(2,1)S(1)}, bf16[16,4096]{1,0:T(8,128)(2,1)S(1)}) custom-call(bf16[16,4096]{1,0:T(8,128)(2,1)S(1)} %get-tuple-element.30.refs_0_, bf16[16,4096]{1,0:T(8,128)(2,1)S(1)} %collective-permute-done.1.refs_1_, ...), custom_call_target="tpu_custom_call" | custom-call | flops 603979776 | bytes 10207232 | tf_op jit(solution)/shard_map/backward/pallas_call | solution.py:71
  17.7 0.3 collective-permute-start.5
  18.0 1.3 %collective-permute-start.10 = (bf16[32,2048]{1,0:T(8,128)(2,1)S(1)}, bf16[32,2048]{1,0:T(8,128)(2,1)S(1)}, u32[]{:S(2)}, u32[]{:S(2)}) collective-permute-start(bf16[32,2048]{1,0:T(8,128)(2,1)S(1)} %pack.1), channel_id=1, source_target_pairs={{0,16},{16,0},{1,17},{17,1},{2,18},{18,2},{3,19},{19,3},{4,20},{20... | collective-permute-start | bytes 393224 | tf_op jit(solution)/shard_map/ppermute | solution.py:44
  19.3 0.1 collective-permute-start.4
  19.4 0.0 collective-permute-done.6.refs_1_.refs_4_
  19.4 0.0 collective-permute-done.5.refs_0_
  19.4 1.6 %collective-permute-start.7 = (bf16[16,4096]{1,0:T(8,128)(2,1)S(1)}, bf16[16,4096]{1,0:T(8,128)(2,1)S(1)}, u32[]{:S(2)}, u32[]{:S(2)}) collective-permute-start(bf16[16,4096]{1,0:T(8,128)(2,1)S(1)} %pair_sums.1), channel_id=1, source_target_pairs={{2,0},{3,1},{0,2},{1,3},{6,4},{7,5},{4,6},{5,7},{10,8},{11,9},{8,1... | collective-permute-start | bytes 393224 | tf_op jit(solution)/shard_map/ppermute | solution.py:55
  21.0 1.0 %collective-permute-start.12 = (bf16[64,1152]{1,0:T(8,128)(2,1)S(1)}, bf16[64,1152]{1,0:T(8,128)(2,1)S(1)}, u32[]{:S(2)}, u32[]{:S(2)}) collective-permute-start(bf16[64,1152]{1,0:T(8,128)(2,1)S(1)} %get-tuple-element.40.factors_ref), channel_id=1, source_target_pairs={{0,16},{16,0},{1,17},{17,1},{2,18},{18,2},{3,19},{19,3},{4,20},{20... | collective-permute-start | bytes 442376 | tf_op jit(solution)/shard_map/ppermute | solution.py:44
  22.0 1.7 %collective-permute-done.10.refs_6_ = bf16[32,2048]{1,0:T(8,128)(2,1)S(1)} collective-permute-done((bf16[32,2048]{1,0:T(8,128)(2,1)S(1)}, bf16[32,2048]{1,0:T(8,128)(2,1)S(1)}, u32[]{:S(2)}, u32[]{:S(2)}) %collective-permute-start.10) | collective-permute-done | bytes 131104 | tf_op jit(solution)/shard_map/ppermute | solution.py:44
  23.7 0.0 collective-permute-start.9
  23.7 0.0 collective-permute-done.4.refs_0_
  23.7 0.5 %collective-permute-start.11 = (bf16[32,2048]{1,0:T(8,128)(2,1)S(1)}, bf16[32,2048]{1,0:T(8,128)(2,1)S(1)}, u32[]{:S(2)}, u32[]{:S(2)}) collective-permute-start(bf16[32,2048]{1,0:T(8,128)(2,1)S(1)} %collective-permute-done.10.refs_6_), channel_id=1, source_target_pairs={{0,1},{1,0},{2,3},{3,2},{4,5},{5,4},{6,7},{7,6},{8,9},{9,8},{10,11... | collective-permute-start | bytes 393224 | tf_op jit(solution)/shard_map/ppermute | solution.py:48
  24.2 1.1 %collective-permute-done.7.refs_1_ = bf16[16,4096]{1,0:T(8,128)(2,1)S(1)} collective-permute-done((bf16[16,4096]{1,0:T(8,128)(2,1)S(1)}, bf16[16,4096]{1,0:T(8,128)(2,1)S(1)}, u32[]{:S(2)}, u32[]{:S(2)}) %collective-permute-start.7) | collective-permute-done | bytes 131104 | tf_op jit(solution)/shard_map/ppermute | solution.py:55
  25.3 0.1 sum_returned.1
  25.4 0.8 %collective-permute-start.8 = (bf16[16,4224]{1,0:T(8,128)(2,1)S(1)}, bf16[16,4224]{1,0:T(8,128)(2,1)S(1)}, u32[]{:S(2)}, u32[]{:S(2)}) collective-permute-start(bf16[16,4224]{1,0:T(8,128)(2,1)S(1)} %sum_returned.1), channel_id=1, source_target_pairs={{0,12},{4,0},{8,4},{12,8},{1,13},{5,1},{9,5},{13,9},{2,14},{6,2},{... | collective-permute-start | bytes 405512 | tf_op jit(solution)/shard_map/ppermute | solution.py:60
  26.2 0.0 collective-permute-done.9.refs_5_
  26.2 0.0 collective-permute-done.11.refs_7_
  26.2 0.7 %collective-permute-done.12.refs_8_ = bf16[64,1152]{1,0:T(8,128)(2,1)S(1)} collective-permute-done((bf16[64,1152]{1,0:T(8,128)(2,1)S(1)}, bf16[64,1152]{1,0:T(8,128)(2,1)S(1)}, u32[]{:S(2)}, u32[]{:S(2)}) %collective-permute-start.12) | collective-permute-done | bytes 147488 | tf_op jit(solution)/shard_map/ppermute | solution.py:44
  26.9 2.6 %weight_grads.1 = bf16[1,3,384,2048]{3,2,1,0:T(8,128)(2,1)} custom-call(bf16[64,1152]{1,0:T(8,128)(2,1)S(1)} %get-tuple-element.40.factors_ref, bf16[64,4096]{1,0:T(8,128)(2,1)S(1)} %get-tuple-element.41.inputs_ref, bf16[16,4096]{1,0:T(8,128)(2,1)S(1)} %get-tuple-element.30.refs_0_, bf16[16,4096]{1,0:T(8,128)(2,1)S(1)} %collective-permute-done.1.refs_1_, ...), custom_call_target="tpu_custom_call" | custom-call | flops 603979776 | bytes 1867776 | tf_op jit(solution)/shard_map/weight_grads/pallas_call | solution.py:71
  29.5 1.1 %collective-permute-done.8.changed_ref = bf16[16,4224]{1,0:T(8,128)(2,1)S(1)} collective-permute-done((bf16[16,4224]{1,0:T(8,128)(2,1)S(1)}, bf16[16,4224]{1,0:T(8,128)(2,1)S(1)}, u32[]{:S(2)}, u32[]{:S(2)}) %collective-permute-start.8) | collective-permute-done | bytes 135200 | tf_op jit(solution)/shard_map/ppermute | solution.py:60
  30.6 0.0 collective-permute-done.early_ref
  30.6 1.3 %merge.1 = bf16[1,1,128,4096]{3,2,1,0:T(8,128)(2,1)} custom-call(bf16[112,4096]{1,0:T(8,128)(2,1)S(1)} %collective-permute-done.early_ref, bf16[16,4224]{1,0:T(8,128)(2,1)S(1)} %collective-permute-done.8.changed_ref), custom_call_target="tpu_custom_call" | custom-call | flops 16777216 | bytes 1052672 | tf_op jit(solution)/shard_map/merge/pallas_call | solution.py:71
  (4 shorter events, 0.0 us)
Async XLA Ops:
  0.6 8.5 %slice-start = ((s8[9437184]{0:T(1024)(128)(4,1)}), s8[4194304]{0:T(1024)(128)(4,1)S(1)}, s32[]{:S(2)}) async-start(s8[9437184]{0:T(1024)(128)(4,1)} %bitcast.9), calls=%async_computation | async-start | bytes 8388608
  2.7 27.9 %collective-permute-start = (bf16[112,4096]{1,0:T(8,128)(2,1)S(1)}, bf16[112,4096]{1,0:T(8,128)(2,1)S(1)}, u32[]{:S(2)}, u32[]{:S(2)}) collective-permute-start(bf16[112,4096]{1,0:T(8,128)(2,1)S(1)} %get-tuple-element.22), channel_id=1, source_target_pairs={{0,12},{4,0},{8,4},{12,8},{1,13},{5,1},{9,5},{13,9},{2,14},{6,2},{... | collective-permute-start | bytes 2752520 | tf_op jit(solution)/shard_map/ppermute | solution.py:60
  7.6 2.2 %slice-start.1 = ((s8[9437184]{0:T(1024)(128)(4,1)}), s8[4194304]{0:T(1024)(128)(4,1)S(1)}, s32[]{:S(2)}) async-start(s8[9437184]{0:T(1024)(128)(4,1)} %bitcast.9), calls=%async_computation.1 | async-start | bytes 8388608
  7.6 2.5 %slice-start.2 = ((s8[9437184]{0:T(1024)(128)(4,1)}), s8[1048576]{0:T(1024)(128)(4,1)S(1)}, s32[]{:S(2)}) async-start(s8[9437184]{0:T(1024)(128)(4,1)} %bitcast.9), calls=%async_computation.2 | async-start | bytes 2097152
  7.6 2.6 %copy-start = (bf16[1,1,1,4,16,4096]{5,4,3,2,1,0:T(8,128)(2,1)S(1)}, bf16[1,1,1,4,16,4096]{5,4,3,2,1,0:T(8,128)(2,1)}, u32[]{:S(2)}) copy-start(bf16[1,1,1,4,16,4096]{5,4,3,2,1,0:T(8,128)(2,1)} %param.8) | copy-start | bytes 1572868
  7.6 5.0 %collective-permute-start.2 = (bf16[16,4096]{1,0:T(8,128)(2,1)S(1)}, bf16[16,4096]{1,0:T(8,128)(2,1)S(1)}, u32[]{:S(2)}, u32[]{:S(2)}) collective-permute-start(bf16[16,4096]{1,0:T(8,128)(2,1)S(1)} %get-tuple-element.30.refs_0_), channel_id=1, source_target_pairs={{0,2},{1,3},{2,0},{3,1},{4,6},{5,7},{6,4},{7,5},{8,10},{9,11},{10,... | collective-permute-start | bytes 393224 | tf_op jit(solution)/shard_map/ppermute | solution.py:55
  9.1 5.0 %collective-permute-start.1 = (bf16[16,4096]{1,0:T(8,128)(2,1)S(1)}, bf16[16,4096]{1,0:T(8,128)(2,1)S(1)}, u32[]{:S(2)}, u32[]{:S(2)}) collective-permute-start(bf16[16,4096]{1,0:T(8,128)(2,1)S(1)} %get-tuple-element.30.refs_0_), channel_id=1, source_target_pairs={{0,1},{1,0},{2,3},{3,2},{4,5},{5,4},{6,7},{7,6},{8,9},{9,8},{10,11... | collective-permute-start | bytes 393224 | tf_op jit(solution)/shard_map/ppermute | solution.py:48
  12.6 1.5 %collective-permute-start.3 = (bf16[16,4096]{1,0:T(8,128)(2,1)S(1)}, bf16[16,4096]{1,0:T(8,128)(2,1)S(1)}, u32[]{:S(2)}, u32[]{:S(2)}) collective-permute-start(bf16[16,4096]{1,0:T(8,128)(2,1)S(1)} %collective-permute-done.2.refs_2_.refs_1_), channel_id=1, source_target_pairs={{0,1},{1,0},{2,3},{3,2},{4,5},{5,4},{6,7},{7,6},{8,9},{9,8},{10,11... | collective-permute-start | bytes 393224 | tf_op jit(solution)/shard_map/ppermute | solution.py:48
  12.6 6.8 %collective-permute-start.6 = (bf16[32,2048]{1,0:T(8,128)(2,1)S(1)}, bf16[32,2048]{1,0:T(8,128)(2,1)S(1)}, u32[]{:S(2)}, u32[]{:S(2)}) collective-permute-start(bf16[32,2048]{1,0:T(8,128)(2,1)S(1)} %get-tuple-element.39), channel_id=1, source_target_pairs={{0,16},{16,0},{1,17},{17,1},{2,18},{18,2},{3,19},{19,3},{4,20},{20... | collective-permute-start | bytes 393224 | tf_op jit(solution)/shard_map/ppermute | solution.py:44
  17.7 1.7 %collective-permute-start.5 = (bf16[16,4096]{1,0:T(8,128)(2,1)S(1)}, bf16[16,4096]{1,0:T(8,128)(2,1)S(1)}, u32[]{:S(2)}, u32[]{:S(2)}) collective-permute-start(bf16[16,4096]{1,0:T(8,128)(2,1)S(1)} %get-tuple-element.38), channel_id=1, source_target_pairs={{0,1},{1,0},{2,3},{3,2},{4,5},{5,4},{6,7},{7,6},{8,9},{9,8},{10,11... | collective-permute-start | bytes 393224 | tf_op jit(solution)/shard_map/ppermute | solution.py:48
  18.0 5.8 %collective-permute-start.10 = (bf16[32,2048]{1,0:T(8,128)(2,1)S(1)}, bf16[32,2048]{1,0:T(8,128)(2,1)S(1)}, u32[]{:S(2)}, u32[]{:S(2)}) collective-permute-start(bf16[32,2048]{1,0:T(8,128)(2,1)S(1)} %pack.1), channel_id=1, source_target_pairs={{0,16},{16,0},{1,17},{17,1},{2,18},{18,2},{3,19},{19,3},{4,20},{20... | collective-permute-start | bytes 393224 | tf_op jit(solution)/shard_map/ppermute | solution.py:44
  19.3 4.4 %collective-permute-start.4 = (bf16[16,4096]{1,0:T(8,128)(2,1)S(1)}, bf16[16,4096]{1,0:T(8,128)(2,1)S(1)}, u32[]{:S(2)}, u32[]{:S(2)}) collective-permute-start(bf16[16,4096]{1,0:T(8,128)(2,1)S(1)} %get-tuple-element.37), channel_id=1, source_target_pairs={{0,1},{1,0},{2,3},{3,2},{4,5},{5,4},{6,7},{7,6},{8,9},{9,8},{10,11... | collective-permute-start | bytes 393224 | tf_op jit(solution)/shard_map/ppermute | solution.py:48
  19.4 5.9 %collective-permute-start.7 = (bf16[16,4096]{1,0:T(8,128)(2,1)S(1)}, bf16[16,4096]{1,0:T(8,128)(2,1)S(1)}, u32[]{:S(2)}, u32[]{:S(2)}) collective-permute-start(bf16[16,4096]{1,0:T(8,128)(2,1)S(1)} %pair_sums.1), channel_id=1, source_target_pairs={{2,0},{3,1},{0,2},{1,3},{6,4},{7,5},{4,6},{5,7},{10,8},{11,9},{8,1... | collective-permute-start | bytes 393224 | tf_op jit(solution)/shard_map/ppermute | solution.py:55
  21.0 5.9 %collective-permute-start.12 = (bf16[64,1152]{1,0:T(8,128)(2,1)S(1)}, bf16[64,1152]{1,0:T(8,128)(2,1)S(1)}, u32[]{:S(2)}, u32[]{:S(2)}) collective-permute-start(bf16[64,1152]{1,0:T(8,128)(2,1)S(1)} %get-tuple-element.40.factors_ref), channel_id=1, source_target_pairs={{0,16},{16,0},{1,17},{17,1},{2,18},{18,2},{3,19},{19,3},{4,20},{20... | collective-permute-start | bytes 442376 | tf_op jit(solution)/shard_map/ppermute | solution.py:44
  23.7 2.5 %collective-permute-start.9 = (bf16[32,2048]{1,0:T(8,128)(2,1)S(1)}, bf16[32,2048]{1,0:T(8,128)(2,1)S(1)}, u32[]{:S(2)}, u32[]{:S(2)}) collective-permute-start(bf16[32,2048]{1,0:T(8,128)(2,1)S(1)} %collective-permute-done.6.refs_1_.refs_4_), channel_id=1, source_target_pairs={{0,1},{1,0},{2,3},{3,2},{4,5},{5,4},{6,7},{7,6},{8,9},{9,8},{10,11... | collective-permute-start | bytes 393224 | tf_op jit(solution)/shard_map/ppermute | solution.py:48
  23.7 2.5 %collective-permute-start.11 = (bf16[32,2048]{1,0:T(8,128)(2,1)S(1)}, bf16[32,2048]{1,0:T(8,128)(2,1)S(1)}, u32[]{:S(2)}, u32[]{:S(2)}) collective-permute-start(bf16[32,2048]{1,0:T(8,128)(2,1)S(1)} %collective-permute-done.10.refs_6_), channel_id=1, source_target_pairs={{0,1},{1,0},{2,3},{3,2},{4,5},{5,4},{6,7},{7,6},{8,9},{9,8},{10,11... | collective-permute-start | bytes 393224 | tf_op jit(solution)/shard_map/ppermute | solution.py:48
  25.4 5.2 %collective-permute-start.8 = (bf16[16,4224]{1,0:T(8,128)(2,1)S(1)}, bf16[16,4224]{1,0:T(8,128)(2,1)S(1)}, u32[]{:S(2)}, u32[]{:S(2)}) collective-permute-start(bf16[16,4224]{1,0:T(8,128)(2,1)S(1)} %sum_returned.1), channel_id=1, source_target_pairs={{0,12},{4,0},{8,4},{12,8},{1,13},{5,1},{9,5},{13,9},{2,14},{6,2},{... | collective-permute-start | bytes 405512 | tf_op jit(solution)/shard_map/ppermute | solution.py:60

commit v9 on v8

--- a/solution.py
+++ b/solution.py
@@ -10,7 +10,7 @@
 BF16 = jnp.bfloat16
 F32 = jnp.float32
 LANES = 128
-VMEM_LIMIT = 20 * 2**20
+VMEM_LIMIT = 12 * 2**20
 ROUTE_COST = 10**10
 LAST_LAST = (((1,), (1,)), ((), ()))
 FIRST_FIRST = (((0,), (0,)), ((), ()))

time: 32 us -> 32 us (level)
  no operation moved by 1% of the time
where the time goes in v9:
time: 32 us; the launch traced here: 31.8 us
  starting transfers between devices  13.5 us (42%)
  Pallas kernels  11.4 us (36%)
  waiting for transfers between devices  5.13 us (16%)
  local copies, waits for them, and re-layouts  1.09 us (3%)
  between operations  0.7 us (2%)
    pallas_call x9, Pallas kernels, run(): pl.pallas_call(body, name=name, out_shape=outs, in_specs=in_specs or [vme...  11.4 us
    ppermute x2, starting transfers between devices, to_previous(): lax.ppermute(value, 'pipe', [(i, (i - 1) % count) for i in range(count)])  5.67 us
    ppermute x3, starting transfers between devices, exchange(): lax.ppermute(value, axis, [(i, partner(i, step, count)) for i in range(co...  3.86 us
    ppermute x2, starting transfers between devices, to_pair(): lax.ppermute(value, 'expert', [(j, i) for i, j in hops] if back else hops)  3.1 us
    ppermute x3, waiting for transfers between devices, exchange(): lax.ppermute(value, axis, [(i, partner(i, step, count)) for i in range(co...  2.38 us
    ppermute x2, waiting for transfers between devices, to_pair(): lax.ppermute(value, 'expert', [(j, i) for i, j in hops] if back else hops)  1.62 us
    ppermute x2, waiting for transfers between devices, to_previous(): lax.ppermute(value, 'pipe', [(i, (i - 1) % count) for i in range(count)])  1.11 us
    unnamed x8, local copies, waits for them, and re-layouts  1.09 us
  transfers between devices with their start and end apart: 13, of which 5 were waited for; matrix products, arithmetic and copies ran while one was open for 0% of the time, Pallas kernels for 25%

profile of v9, /device:TPU:0, one launch (start us, length us, event | category | flops | bytes accessed | tf_op | source)
XLA Modules:
  0.0 31.8 jit_solution(11366052611547606226)
XLA Ops:
  0.6 0.0 slice-start
  0.6 2.1 %route.1 = (bf16[112,4096]{1,0:T(8,128)(2,1)S(1)}, bf16[16,4096]{1,0:T(8,128)(2,1)S(1)}, bf16[16,4096]{1,0:T(8,128)(2,1)S(1)}, bf16[128,128]{1,0:T(8,128)(2,1)S(...) custom-call(s32[8,128]{1,0:T(8,128)} %bitcast.15, f32[8,128]{1,0:T(8,128)} %bitcast.16, ...), custom_call_target="tpu_custom_call" | custom-call | tf_op jit(solution)/shard_map/route/pallas_call | solution.py:71
  2.7 4.9 %collective-permute-start = (bf16[112,4096]{1,0:T(8,128)(2,1)S(1)}, bf16[112,4096]{1,0:T(8,128)(2,1)S(1)}, u32[]{:S(2)}, u32[]{:S(2)}) collective-permute-start(bf16[112,4096]{1,0:T(8,128)(2,1)S(1)} %get-tuple-element.22), channel_id=1, source_target_pairs={{0,12},{4,0},{8,4},{12,8},{1,13},{5,1},{9,5},{13,9},{2,14},{6,2},{... | collective-permute-start | bytes 2752520 | tf_op jit(solution)/shard_map/ppermute | solution.py:60
  7.6 0.0 slice-start.1
  7.6 0.0 slice-start.2
  7.6 0.0 copy-start
  7.6 1.5 %collective-permute-start.2 = (bf16[16,4096]{1,0:T(8,128)(2,1)S(1)}, bf16[16,4096]{1,0:T(8,128)(2,1)S(1)}, u32[]{:S(2)}, u32[]{:S(2)}) collective-permute-start(bf16[16,4096]{1,0:T(8,128)(2,1)S(1)} %get-tuple-element.30.refs_0_), channel_id=1, source_target_pairs={{0,2},{1,3},{2,0},{3,1},{4,6},{5,7},{6,4},{7,5},{8,10},{9,11},{10,... | collective-permute-start | bytes 393224 | tf_op jit(solution)/shard_map/ppermute | solution.py:55
  9.1 0.0 collective-permute-start.1
  9.1 0.0 slice-done
  9.1 0.7 %slice-done.1 = s8[4194304]{0:T(1024)(128)(4,1)S(1)} async-done(((s8[9437184]{0:T(1024)(128)(4,1)}), s8[4194304]{0:T(1024)(128)(4,1)S(1)}, s32[]{:S(2)}) %slice-start.1) | async-done | bytes 4194328
  9.8 0.3 slice-done.2
  10.1 0.1 copy-done
  10.2 1.8 %forward.1 = (f32[384,64]{1,0:T(8,128)S(1)}, f32[384,64]{1,0:T(8,128)S(1)}, bf16[64,384]{1,0:T(8,128)(2,1)S(1)}, bf16[64,4096]{1,0:T(8,128)(2,1)S(1)}, bf16[32,2048]{1,0:T(8,128)(2,1)S(1)}) custom-call(bf16[4,16,4096]{2,1,0:T(8,128)(2,1)S(1)} %bitcast.13, bf16[3,384,4096]{2,1,0:T(8,128)(2,1)S(1)} %bitcast.11), custom_call_target="tpu_custom_call" | custom-call | flops 402653184 | bytes 9961472 | tf_op jit(solution)/shard_map/forward/pallas_call | solution.py:71
  12.0 0.5 %collective-permute-done.2.refs_2_.refs_1_ = bf16[16,4096]{1,0:T(8,128)(2,1)S(1)} collective-permute-done((bf16[16,4096]{1,0:T(8,128)(2,1)S(1)}, bf16[16,4096]{1,0:T(8,128)(2,1)S(1)}, u32[]{:S(2)}, u32[]{:S(2)}) %collective-permute-start.2) | collective-permute-done | bytes 131104 | tf_op jit(solution)/shard_map/ppermute | solution.py:55
  12.6 0.0 collective-permute-start.3
  12.6 1.5 %collective-permute-start.6 = (bf16[32,2048]{1,0:T(8,128)(2,1)S(1)}, bf16[32,2048]{1,0:T(8,128)(2,1)S(1)}, u32[]{:S(2)}, u32[]{:S(2)}) collective-permute-start(bf16[32,2048]{1,0:T(8,128)(2,1)S(1)} %get-tuple-element.39), channel_id=1, source_target_pairs={{0,16},{16,0},{1,17},{17,1},{2,18},{18,2},{3,19},{19,3},{4,20},{20... | collective-permute-start | bytes 393224 | tf_op jit(solution)/shard_map/ppermute | solution.py:44
  14.0 0.0 collective-permute-done.1.refs_1_
  14.1 0.0 collective-permute-done.3.refs_3_
  14.1 3.6 %backward.1 = (bf16[32,4096]{1,0:T(8,128)(2,1)S(1)}, bf16[64,1152]{1,0:T(8,128)(2,1)S(1)}, bf16[16,4096]{1,0:T(8,128)(2,1)S(1)}, bf16[16,4096]{1,0:T(8,128)(2,1)S(1)}) custom-call(bf16[16,4096]{1,0:T(8,128)(2,1)S(1)} %get-tuple-element.30.refs_0_, bf16[16,4096]{1,0:T(8,128)(2,1)S(1)} %collective-permute-done.1.refs_1_, ...), custom_call_target="tpu_custom_call" | custom-call | flops 603979776 | bytes 10207232 | tf_op jit(solution)/shard_map/backward/pallas_call | solution.py:71
  17.7 0.3 collective-permute-start.5
  18.0 1.3 %collective-permute-start.10 = (bf16[32,2048]{1,0:T(8,128)(2,1)S(1)}, bf16[32,2048]{1,0:T(8,128)(2,1)S(1)}, u32[]{:S(2)}, u32[]{:S(2)}) collective-permute-start(bf16[32,2048]{1,0:T(8,128)(2,1)S(1)} %pack.1), channel_id=1, source_target_pairs={{0,16},{16,0},{1,17},{17,1},{2,18},{18,2},{3,19},{19,3},{4,20},{20... | collective-permute-start | bytes 393224 | tf_op jit(solution)/shard_map/ppermute | solution.py:44
  19.3 0.1 collective-permute-start.4
  19.4 0.0 collective-permute-done.6.refs_1_.refs_4_
  19.4 0.0 collective-permute-done.5.refs_0_
  19.4 1.6 %collective-permute-start.7 = (bf16[16,4096]{1,0:T(8,128)(2,1)S(1)}, bf16[16,4096]{1,0:T(8,128)(2,1)S(1)}, u32[]{:S(2)}, u32[]{:S(2)}) collective-permute-start(bf16[16,4096]{1,0:T(8,128)(2,1)S(1)} %pair_sums.1), channel_id=1, source_target_pairs={{2,0},{3,1},{0,2},{1,3},{6,4},{7,5},{4,6},{5,7},{10,8},{11,9},{8,1... | collective-permute-start | bytes 393224 | tf_op jit(solution)/shard_map/ppermute | solution.py:55
  21.0 1.0 %collective-permute-start.12 = (bf16[64,1152]{1,0:T(8,128)(2,1)S(1)}, bf16[64,1152]{1,0:T(8,128)(2,1)S(1)}, u32[]{:S(2)}, u32[]{:S(2)}) collective-permute-start(bf16[64,1152]{1,0:T(8,128)(2,1)S(1)} %get-tuple-element.40.factors_ref), channel_id=1, source_target_pairs={{0,16},{16,0},{1,17},{17,1},{2,18},{18,2},{3,19},{19,3},{4,20},{20... | collective-permute-start | bytes 442376 | tf_op jit(solution)/shard_map/ppermute | solution.py:44
  22.0 1.7 %collective-permute-done.10.refs_6_ = bf16[32,2048]{1,0:T(8,128)(2,1)S(1)} collective-permute-done((bf16[32,2048]{1,0:T(8,128)(2,1)S(1)}, bf16[32,2048]{1,0:T(8,128)(2,1)S(1)}, u32[]{:S(2)}, u32[]{:S(2)}) %collective-permute-start.10) | collective-permute-done | bytes 131104 | tf_op jit(solution)/shard_map/ppermute | solution.py:44
  23.7 0.0 collective-permute-start.9
  23.7 0.0 collective-permute-done.4.refs_0_
  23.7 0.5 %collective-permute-start.11 = (bf16[32,2048]{1,0:T(8,128)(2,1)S(1)}, bf16[32,2048]{1,0:T(8,128)(2,1)S(1)}, u32[]{:S(2)}, u32[]{:S(2)}) collective-permute-start(bf16[32,2048]{1,0:T(8,128)(2,1)S(1)} %collective-permute-done.10.refs_6_), channel_id=1, source_target_pairs={{0,1},{1,0},{2,3},{3,2},{4,5},{5,4},{6,7},{7,6},{8,9},{9,8},{10,11... | collective-permute-start | bytes 393224 | tf_op jit(solution)/shard_map/ppermute | solution.py:48
  24.2 1.1 %collective-permute-done.7.refs_1_ = bf16[16,4096]{1,0:T(8,128)(2,1)S(1)} collective-permute-done((bf16[16,4096]{1,0:T(8,128)(2,1)S(1)}, bf16[16,4096]{1,0:T(8,128)(2,1)S(1)}, u32[]{:S(2)}, u32[]{:S(2)}) %collective-permute-start.7) | collective-permute-done | bytes 131104 | tf_op jit(solution)/shard_map/ppermute | solution.py:55
  25.3 0.1 sum_returned.1
  25.4 0.8 %collective-permute-start.8 = (bf16[16,4224]{1,0:T(8,128)(2,1)S(1)}, bf16[16,4224]{1,0:T(8,128)(2,1)S(1)}, u32[]{:S(2)}, u32[]{:S(2)}) collective-permute-start(bf16[16,4224]{1,0:T(8,128)(2,1)S(1)} %sum_returned.1), channel_id=1, source_target_pairs={{0,12},{4,0},{8,4},{12,8},{1,13},{5,1},{9,5},{13,9},{2,14},{6,2},{... | collective-permute-start | bytes 405512 | tf_op jit(solution)/shard_map/ppermute | solution.py:60
  26.2 0.0 collective-permute-done.9.refs_5_
  26.2 0.0 collective-permute-done.11.refs_7_
  26.2 0.7 %collective-permute-done.12.refs_8_ = bf16[64,1152]{1,0:T(8,128)(2,1)S(1)} collective-permute-done((bf16[64,1152]{1,0:T(8,128)(2,1)S(1)}, bf16[64,1152]{1,0:T(8,128)(2,1)S(1)}, u32[]{:S(2)}, u32[]{:S(2)}) %collective-permute-start.12) | collective-permute-done | bytes 147488 | tf_op jit(solution)/shard_map/ppermute | solution.py:44
  26.9 2.6 %weight_grads.1 = bf16[1,3,384,2048]{3,2,1,0:T(8,128)(2,1)} custom-call(bf16[64,1152]{1,0:T(8,128)(2,1)S(1)} %get-tuple-element.40.factors_ref, bf16[64,4096]{1,0:T(8,128)(2,1)S(1)} %get-tuple-element.41.inputs_ref, bf16[16,4096]{1,0:T(8,128)(2,1)S(1)} %get-tuple-element.30.refs_0_, bf16[16,4096]{1,0:T(8,128)(2,1)S(1)} %collective-permute-done.1.refs_1_, ...), custom_call_target="tpu_custom_call" | custom-call | flops 603979776 | bytes 1867776 | tf_op jit(solution)/shard_map/weight_grads/pallas_call | solution.py:71
  29.5 1.1 %collective-permute-done.8.changed_ref = bf16[16,4224]{1,0:T(8,128)(2,1)S(1)} collective-permute-done((bf16[16,4224]{1,0:T(8,128)(2,1)S(1)}, bf16[16,4224]{1,0:T(8,128)(2,1)S(1)}, u32[]{:S(2)}, u32[]{:S(2)}) %collective-permute-start.8) | collective-permute-done | bytes 135200 | tf_op jit(solution)/shard_map/ppermute | solution.py:60
  30.6 0.0 collective-permute-done.early_ref
  30.6 1.3 %merge.1 = bf16[1,1,128,4096]{3,2,1,0:T(8,128)(2,1)} custom-call(bf16[112,4096]{1,0:T(8,128)(2,1)S(1)} %collective-permute-done.early_ref, bf16[16,4224]{1,0:T(8,128)(2,1)S(1)} %collective-permute-done.8.changed_ref), custom_call_target="tpu_custom_call" | custom-call | flops 16777216 | bytes 1052672 | tf_op jit(solution)/shard_map/merge/pallas_call | solution.py:71
  (4 shorter events, 0.0 us)
Async XLA Ops:
  0.6 8.5 %slice-start = ((s8[9437184]{0:T(1024)(128)(4,1)}), s8[4194304]{0:T(1024)(128)(4,1)S(1)}, s32[]{:S(2)}) async-start(s8[9437184]{0:T(1024)(128)(4,1)} %bitcast.9), calls=%async_computation | async-start | bytes 8388608
  2.7 27.9 %collective-permute-start = (bf16[112,4096]{1,0:T(8,128)(2,1)S(1)}, bf16[112,4096]{1,0:T(8,128)(2,1)S(1)}, u32[]{:S(2)}, u32[]{:S(2)}) collective-permute-start(bf16[112,4096]{1,0:T(8,128)(2,1)S(1)} %get-tuple-element.22), channel_id=1, source_target_pairs={{0,12},{4,0},{8,4},{12,8},{1,13},{5,1},{9,5},{13,9},{2,14},{6,2},{... | collective-permute-start | bytes 2752520 | tf_op jit(solution)/shard_map/ppermute | solution.py:60
  7.6 2.2 %slice-start.1 = ((s8[9437184]{0:T(1024)(128)(4,1)}), s8[4194304]{0:T(1024)(128)(4,1)S(1)}, s32[]{:S(2)}) async-start(s8[9437184]{0:T(1024)(128)(4,1)} %bitcast.9), calls=%async_computation.1 | async-start | bytes 8388608
  7.6 2.5 %slice-start.2 = ((s8[9437184]{0:T(1024)(128)(4,1)}), s8[1048576]{0:T(1024)(128)(4,1)S(1)}, s32[]{:S(2)}) async-start(s8[9437184]{0:T(1024)(128)(4,1)} %bitcast.9), calls=%async_computation.2 | async-start | bytes 2097152
  7.6 2.6 %copy-start = (bf16[1,1,1,4,16,4096]{5,4,3,2,1,0:T(8,128)(2,1)S(1)}, bf16[1,1,1,4,16,4096]{5,4,3,2,1,0:T(8,128)(2,1)}, u32[]{:S(2)}) copy-start(bf16[1,1,1,4,16,4096]{5,4,3,2,1,0:T(8,128)(2,1)} %param.8) | copy-start | bytes 1572868
  7.6 5.0 %collective-permute-start.2 = (bf16[16,4096]{1,0:T(8,128)(2,1)S(1)}, bf16[16,4096]{1,0:T(8,128)(2,1)S(1)}, u32[]{:S(2)}, u32[]{:S(2)}) collective-permute-start(bf16[16,4096]{1,0:T(8,128)(2,1)S(1)} %get-tuple-element.30.refs_0_), channel_id=1, source_target_pairs={{0,2},{1,3},{2,0},{3,1},{4,6},{5,7},{6,4},{7,5},{8,10},{9,11},{10,... | collective-permute-start | bytes 393224 | tf_op jit(solution)/shard_map/ppermute | solution.py:55
  9.1 5.0 %collective-permute-start.1 = (bf16[16,4096]{1,0:T(8,128)(2,1)S(1)}, bf16[16,4096]{1,0:T(8,128)(2,1)S(1)}, u32[]{:S(2)}, u32[]{:S(2)}) collective-permute-start(bf16[16,4096]{1,0:T(8,128)(2,1)S(1)} %get-tuple-element.30.refs_0_), channel_id=1, source_target_pairs={{0,1},{1,0},{2,3},{3,2},{4,5},{5,4},{6,7},{7,6},{8,9},{9,8},{10,11... | collective-permute-start | bytes 393224 | tf_op jit(solution)/shard_map/ppermute | solution.py:48
  12.6 1.5 %collective-permute-start.3 = (bf16[16,4096]{1,0:T(8,128)(2,1)S(1)}, bf16[16,4096]{1,0:T(8,128)(2,1)S(1)}, u32[]{:S(2)}, u32[]{:S(2)}) collective-permute-start(bf16[16,4096]{1,0:T(8,128)(2,1)S(1)} %collective-permute-done.2.refs_2_.refs_1_), channel_id=1, source_target_pairs={{0,1},{1,0},{2,3},{3,2},{4,5},{5,4},{6,7},{7,6},{8,9},{9,8},{10,11... | collective-permute-start | bytes 393224 | tf_op jit(solution)/shard_map/ppermute | solution.py:48
  12.6 6.8 %collective-permute-start.6 = (bf16[32,2048]{1,0:T(8,128)(2,1)S(1)}, bf16[32,2048]{1,0:T(8,128)(2,1)S(1)}, u32[]{:S(2)}, u32[]{:S(2)}) collective-permute-start(bf16[32,2048]{1,0:T(8,128)(2,1)S(1)} %get-tuple-element.39), channel_id=1, source_target_pairs={{0,16},{16,0},{1,17},{17,1},{2,18},{18,2},{3,19},{19,3},{4,20},{20... | collective-permute-start | bytes 393224 | tf_op jit(solution)/shard_map/ppermute | solution.py:44
  17.7 1.7 %collective-permute-start.5 = (bf16[16,4096]{1,0:T(8,128)(2,1)S(1)}, bf16[16,4096]{1,0:T(8,128)(2,1)S(1)}, u32[]{:S(2)}, u32[]{:S(2)}) collective-permute-start(bf16[16,4096]{1,0:T(8,128)(2,1)S(1)} %get-tuple-element.38), channel_id=1, source_target_pairs={{0,1},{1,0},{2,3},{3,2},{4,5},{5,4},{6,7},{7,6},{8,9},{9,8},{10,11... | collective-permute-start | bytes 393224 | tf_op jit(solution)/shard_map/ppermute | solution.py:48
  18.0 5.8 %collective-permute-start.10 = (bf16[32,2048]{1,0:T(8,128)(2,1)S(1)}, bf16[32,2048]{1,0:T(8,128)(2,1)S(1)}, u32[]{:S(2)}, u32[]{:S(2)}) collective-permute-start(bf16[32,2048]{1,0:T(8,128)(2,1)S(1)} %pack.1), channel_id=1, source_target_pairs={{0,16},{16,0},{1,17},{17,1},{2,18},{18,2},{3,19},{19,3},{4,20},{20... | collective-permute-start | bytes 393224 | tf_op jit(solution)/shard_map/ppermute | solution.py:44
  19.3 4.4 %collective-permute-start.4 = (bf16[16,4096]{1,0:T(8,128)(2,1)S(1)}, bf16[16,4096]{1,0:T(8,128)(2,1)S(1)}, u32[]{:S(2)}, u32[]{:S(2)}) collective-permute-start(bf16[16,4096]{1,0:T(8,128)(2,1)S(1)} %get-tuple-element.37), channel_id=1, source_target_pairs={{0,1},{1,0},{2,3},{3,2},{4,5},{5,4},{6,7},{7,6},{8,9},{9,8},{10,11... | collective-permute-start | bytes 393224 | tf_op jit(solution)/shard_map/ppermute | solution.py:48
  19.4 5.9 %collective-permute-start.7 = (bf16[16,4096]{1,0:T(8,128)(2,1)S(1)}, bf16[16,4096]{1,0:T(8,128)(2,1)S(1)}, u32[]{:S(2)}, u32[]{:S(2)}) collective-permute-start(bf16[16,4096]{1,0:T(8,128)(2,1)S(1)} %pair_sums.1), channel_id=1, source_target_pairs={{2,0},{3,1},{0,2},{1,3},{6,4},{7,5},{4,6},{5,7},{10,8},{11,9},{8,1... | collective-permute-start | bytes 393224 | tf_op jit(solution)/shard_map/ppermute | solution.py:55
  21.0 5.9 %collective-permute-start.12 = (bf16[64,1152]{1,0:T(8,128)(2,1)S(1)}, bf16[64,1152]{1,0:T(8,128)(2,1)S(1)}, u32[]{:S(2)}, u32[]{:S(2)}) collective-permute-start(bf16[64,1152]{1,0:T(8,128)(2,1)S(1)} %get-tuple-element.40.factors_ref), channel_id=1, source_target_pairs={{0,16},{16,0},{1,17},{17,1},{2,18},{18,2},{3,19},{19,3},{4,20},{20... | collective-permute-start | bytes 442376 | tf_op jit(solution)/shard_map/ppermute | solution.py:44
  23.7 2.5 %collective-permute-start.9 = (bf16[32,2048]{1,0:T(8,128)(2,1)S(1)}, bf16[32,2048]{1,0:T(8,128)(2,1)S(1)}, u32[]{:S(2)}, u32[]{:S(2)}) collective-permute-start(bf16[32,2048]{1,0:T(8,128)(2,1)S(1)} %collective-permute-done.6.refs_1_.refs_4_), channel_id=1, source_target_pairs={{0,1},{1,0},{2,3},{3,2},{4,5},{5,4},{6,7},{7,6},{8,9},{9,8},{10,11... | collective-permute-start | bytes 393224 | tf_op jit(solution)/shard_map/ppermute | solution.py:48
  23.7 2.5 %collective-permute-start.11 = (bf16[32,2048]{1,0:T(8,128)(2,1)S(1)}, bf16[32,2048]{1,0:T(8,128)(2,1)S(1)}, u32[]{:S(2)}, u32[]{:S(2)}) collective-permute-start(bf16[32,2048]{1,0:T(8,128)(2,1)S(1)} %collective-permute-done.10.refs_6_), channel_id=1, source_target_pairs={{0,1},{1,0},{2,3},{3,2},{4,5},{5,4},{6,7},{7,6},{8,9},{9,8},{10,11... | collective-permute-start | bytes 393224 | tf_op jit(solution)/shard_map/ppermute | solution.py:48
  25.4 5.2 %collective-permute-start.8 = (bf16[16,4224]{1,0:T(8,128)(2,1)S(1)}, bf16[16,4224]{1,0:T(8,128)(2,1)S(1)}, u32[]{:S(2)}, u32[]{:S(2)}) collective-permute-start(bf16[16,4224]{1,0:T(8,128)(2,1)S(1)} %sum_returned.1), channel_id=1, source_target_pairs={{0,12},{4,0},{8,4},{12,8},{1,13},{5,1},{9,5},{13,9},{2,14},{6,2},{... | collective-permute-start | bytes 405512 | tf_op jit(solution)/shard_map/ppermute | solution.py:60

commit v10 on v9

--- a/solution.py
+++ b/solution.py
@@ -294,20 +294,25 @@
         c.wait()
 
 
+def merge_pieces(width):
+    return [width // 8] * 2 + [width // 4] * 3
+
+
 def merge_body(early_ref, changed_ref, out_hbm, held, sems):
     early, width = early_ref.shape
     capacity = changed_ref.shape[0]
     tokens = early + capacity
     digits = [changed_ref[:, width:][i : i + 1].astype(F32) for i in range(4)]
     both = sorting(digits[0] * 128.0 + digits[1], digits[2] * 128.0 + digits[3], tokens, capacity)
-    step = held.shape[2]
     copies = []
-    for c in range(width // step):
-        at = slice(c * step, (c + 1) * step)
+    first = 0
+    for n, piece in enumerate(merge_pieces(width)):
+        at = pl.ds(first, piece)
         rows = jnp.concatenate([early_ref[:, at], changed_ref[:, at]], axis=0)
-        held[c] = mm(both, rows, FIRST_FIRST).astype(BF16)
-        copies.append(pltpu.make_async_copy(held.at[c], out_hbm.at[0, 0, :, pl.ds(c * step, step)], sems.at[c]))
+        held[:, at] = mm(both, rows, FIRST_FIRST).astype(BF16)
+        copies.append(pltpu.make_async_copy(held.at[:, at], out_hbm.at[0, 0, :, at], sems.at[n]))
         copies[-1].start()
+        first += piece
     for c in copies:
         c.wait()
 
@@ -428,7 +433,6 @@
         scratch=[pltpu.VMEM((pieces, hid, columns), BF16), pltpu.SemaphoreType.DMA((pieces,))],
     )[0]
 
-    step = min(width, 1024)
     passed_grads = run(
         merge_body,
         "merge",
@@ -436,7 +440,7 @@
         [shifted, next_changed],
         2 * capacity * tokens * width,
         out_specs=[hbm],
-        scratch=[pltpu.VMEM((width // step, tokens, step), BF16), pltpu.SemaphoreType.DMA((width // step,))],
+        scratch=[pltpu.VMEM((tokens, width), BF16), pltpu.SemaphoreType.DMA((len(merge_pieces(width)),))],
     )[0]
     return (passed_grads, weight_grads)
 

time: 32 us -> 32 us (level)
  no operation moved by 1% of the time
where the time goes in v10:
time: 32 us; the launch traced here: 31.8 us
  starting transfers between devices  13.5 us (42%)
  Pallas kernels  11.4 us (36%)
  waiting for transfers between devices  5.13 us (16%)
  local copies, waits for them, and re-layouts  1.09 us (3%)
  between operations  0.7 us (2%)
    pallas_call x9, Pallas kernels, run(): pl.pallas_call(body, name=name, out_shape=outs, in_specs=in_specs or [vme...  11.4 us
    ppermute x2, starting transfers between devices, to_previous(): lax.ppermute(value, 'pipe', [(i, (i - 1) % count) for i in range(count)])  5.67 us
    ppermute x3, starting transfers between devices, exchange(): lax.ppermute(value, axis, [(i, partner(i, step, count)) for i in range(co...  3.86 us
    ppermute x2, starting transfers between devices, to_pair(): lax.ppermute(value, 'expert', [(j, i) for i, j in hops] if back else hops)  3.1 us
    ppermute x3, waiting for transfers between devices, exchange(): lax.ppermute(value, axis, [(i, partner(i, step, count)) for i in range(co...  2.38 us
    ppermute x2, waiting for transfers between devices, to_pair(): lax.ppermute(value, 'expert', [(j, i) for i, j in hops] if back else hops)  1.62 us
    ppermute x2, waiting for transfers between devices, to_previous(): lax.ppermute(value, 'pipe', [(i, (i - 1) % count) for i in range(count)])  1.11 us
    unnamed x8, local copies, waits for them, and re-layouts  1.09 us
  transfers between devices with their start and end apart: 13, of which 5 were waited for; matrix products, arithmetic and copies ran while one was open for 0% of the time, Pallas kernels for 25%

profile of v10, /device:TPU:0, one launch (start us, length us, event | category | flops | bytes accessed | tf_op | source)
XLA Modules:
  0.0 31.8 jit_solution(2464444812083733023)
XLA Ops:
  0.6 0.0 slice-start
  0.6 2.1 %route.1 = (bf16[112,4096]{1,0:T(8,128)(2,1)S(1)}, bf16[16,4096]{1,0:T(8,128)(2,1)S(1)}, bf16[16,4096]{1,0:T(8,128)(2,1)S(1)}, bf16[128,128]{1,0:T(8,128)(2,1)S(...) custom-call(s32[8,128]{1,0:T(8,128)} %bitcast.15, f32[8,128]{1,0:T(8,128)} %bitcast.16, ...), custom_call_target="tpu_custom_call" | custom-call | tf_op jit(solution)/shard_map/route/pallas_call | solution.py:71
  2.7 4.9 %collective-permute-start = (bf16[112,4096]{1,0:T(8,128)(2,1)S(1)}, bf16[112,4096]{1,0:T(8,128)(2,1)S(1)}, u32[]{:S(2)}, u32[]{:S(2)}) collective-permute-start(bf16[112,4096]{1,0:T(8,128)(2,1)S(1)} %get-tuple-element.22), channel_id=1, source_target_pairs={{0,12},{4,0},{8,4},{12,8},{1,13},{5,1},{9,5},{13,9},{2,14},{6,2},{... | collective-permute-start | bytes 2752520 | tf_op jit(solution)/shard_map/ppermute | solution.py:60
  7.6 0.0 slice-start.1
  7.6 0.0 slice-start.2
  7.6 0.0 copy-start
  7.6 1.5 %collective-permute-start.2 = (bf16[16,4096]{1,0:T(8,128)(2,1)S(1)}, bf16[16,4096]{1,0:T(8,128)(2,1)S(1)}, u32[]{:S(2)}, u32[]{:S(2)}) collective-permute-start(bf16[16,4096]{1,0:T(8,128)(2,1)S(1)} %get-tuple-element.30.refs_0_), channel_id=1, source_target_pairs={{0,2},{1,3},{2,0},{3,1},{4,6},{5,7},{6,4},{7,5},{8,10},{9,11},{10,... | collective-permute-start | bytes 393224 | tf_op jit(solution)/shard_map/ppermute | solution.py:55
  9.1 0.0 collective-permute-start.1
  9.1 0.0 slice-done
  9.1 0.7 %slice-done.1 = s8[4194304]{0:T(1024)(128)(4,1)S(1)} async-done(((s8[9437184]{0:T(1024)(128)(4,1)}), s8[4194304]{0:T(1024)(128)(4,1)S(1)}, s32[]{:S(2)}) %slice-start.1) | async-done | bytes 4194328
  9.8 0.3 slice-done.2
  10.1 0.1 copy-done
  10.2 1.8 %forward.1 = (f32[384,64]{1,0:T(8,128)S(1)}, f32[384,64]{1,0:T(8,128)S(1)}, bf16[64,384]{1,0:T(8,128)(2,1)S(1)}, bf16[64,4096]{1,0:T(8,128)(2,1)S(1)}, bf16[32,2048]{1,0:T(8,128)(2,1)S(1)}) custom-call(bf16[4,16,4096]{2,1,0:T(8,128)(2,1)S(1)} %bitcast.13, bf16[3,384,4096]{2,1,0:T(8,128)(2,1)S(1)} %bitcast.11), custom_call_target="tpu_custom_call" | custom-call | flops 402653184 | bytes 9961472 | tf_op jit(solution)/shard_map/forward/pallas_call | solution.py:71
  12.0 0.5 %collective-permute-done.2.refs_2_.refs_1_ = bf16[16,4096]{1,0:T(8,128)(2,1)S(1)} collective-permute-done((bf16[16,4096]{1,0:T(8,128)(2,1)S(1)}, bf16[16,4096]{1,0:T(8,128)(2,1)S(1)}, u32[]{:S(2)}, u32[]{:S(2)}) %collective-permute-start.2) | collective-permute-done | bytes 131104 | tf_op jit(solution)/shard_map/ppermute | solution.py:55
  12.6 0.0 collective-permute-start.3
  12.6 1.5 %collective-permute-start.6 = (bf16[32,2048]{1,0:T(8,128)(2,1)S(1)}, bf16[32,2048]{1,0:T(8,128)(2,1)S(1)}, u32[]{:S(2)}, u32[]{:S(2)}) collective-permute-start(bf16[32,2048]{1,0:T(8,128)(2,1)S(1)} %get-tuple-element.39), channel_id=1, source_target_pairs={{0,16},{16,0},{1,17},{17,1},{2,18},{18,2},{3,19},{19,3},{4,20},{20... | collective-permute-start | bytes 393224 | tf_op jit(solution)/shard_map/ppermute | solution.py:44
  14.0 0.0 collective-permute-done.1.refs_1_
  14.1 0.0 collective-permute-done.3.refs_3_
  14.1 3.6 %backward.1 = (bf16[32,4096]{1,0:T(8,128)(2,1)S(1)}, bf16[64,1152]{1,0:T(8,128)(2,1)S(1)}, bf16[16,4096]{1,0:T(8,128)(2,1)S(1)}, bf16[16,4096]{1,0:T(8,128)(2,1)S(1)}) custom-call(bf16[16,4096]{1,0:T(8,128)(2,1)S(1)} %get-tuple-element.30.refs_0_, bf16[16,4096]{1,0:T(8,128)(2,1)S(1)} %collective-permute-done.1.refs_1_, ...), custom_call_target="tpu_custom_call" | custom-call | flops 603979776 | bytes 10207232 | tf_op jit(solution)/shard_map/backward/pallas_call | solution.py:71
  17.7 0.3 collective-permute-start.5
  18.0 1.3 %collective-permute-start.10 = (bf16[32,2048]{1,0:T(8,128)(2,1)S(1)}, bf16[32,2048]{1,0:T(8,128)(2,1)S(1)}, u32[]{:S(2)}, u32[]{:S(2)}) collective-permute-start(bf16[32,2048]{1,0:T(8,128)(2,1)S(1)} %pack.1), channel_id=1, source_target_pairs={{0,16},{16,0},{1,17},{17,1},{2,18},{18,2},{3,19},{19,3},{4,20},{20... | collective-permute-start | bytes 393224 | tf_op jit(solution)/shard_map/ppermute | solution.py:44
  19.3 0.1 collective-permute-start.4
  19.4 0.0 collective-permute-done.6.refs_1_.refs_4_
  19.4 0.0 collective-permute-done.5.refs_0_
  19.4 1.6 %collective-permute-start.7 = (bf16[16,4096]{1,0:T(8,128)(2,1)S(1)}, bf16[16,4096]{1,0:T(8,128)(2,1)S(1)}, u32[]{:S(2)}, u32[]{:S(2)}) collective-permute-start(bf16[16,4096]{1,0:T(8,128)(2,1)S(1)} %pair_sums.1), channel_id=1, source_target_pairs={{2,0},{3,1},{0,2},{1,3},{6,4},{7,5},{4,6},{5,7},{10,8},{11,9},{8,1... | collective-permute-start | bytes 393224 | tf_op jit(solution)/shard_map/ppermute | solution.py:55
  21.0 1.0 %collective-permute-start.12 = (bf16[64,1152]{1,0:T(8,128)(2,1)S(1)}, bf16[64,1152]{1,0:T(8,128)(2,1)S(1)}, u32[]{:S(2)}, u32[]{:S(2)}) collective-permute-start(bf16[64,1152]{1,0:T(8,128)(2,1)S(1)} %get-tuple-element.40.factors_ref), channel_id=1, source_target_pairs={{0,16},{16,0},{1,17},{17,1},{2,18},{18,2},{3,19},{19,3},{4,20},{20... | collective-permute-start | bytes 442376 | tf_op jit(solution)/shard_map/ppermute | solution.py:44
  22.0 1.7 %collective-permute-done.10.refs_6_ = bf16[32,2048]{1,0:T(8,128)(2,1)S(1)} collective-permute-done((bf16[32,2048]{1,0:T(8,128)(2,1)S(1)}, bf16[32,2048]{1,0:T(8,128)(2,1)S(1)}, u32[]{:S(2)}, u32[]{:S(2)}) %collective-permute-start.10) | collective-permute-done | bytes 131104 | tf_op jit(solution)/shard_map/ppermute | solution.py:44
  23.7 0.0 collective-permute-start.9
  23.7 0.0 collective-permute-done.4.refs_0_
  23.7 0.5 %collective-permute-start.11 = (bf16[32,2048]{1,0:T(8,128)(2,1)S(1)}, bf16[32,2048]{1,0:T(8,128)(2,1)S(1)}, u32[]{:S(2)}, u32[]{:S(2)}) collective-permute-start(bf16[32,2048]{1,0:T(8,128)(2,1)S(1)} %collective-permute-done.10.refs_6_), channel_id=1, source_target_pairs={{0,1},{1,0},{2,3},{3,2},{4,5},{5,4},{6,7},{7,6},{8,9},{9,8},{10,11... | collective-permute-start | bytes 393224 | tf_op jit(solution)/shard_map/ppermute | solution.py:48
  24.2 1.1 %collective-permute-done.7.refs_1_ = bf16[16,4096]{1,0:T(8,128)(2,1)S(1)} collective-permute-done((bf16[16,4096]{1,0:T(8,128)(2,1)S(1)}, bf16[16,4096]{1,0:T(8,128)(2,1)S(1)}, u32[]{:S(2)}, u32[]{:S(2)}) %collective-permute-start.7) | collective-permute-done | bytes 131104 | tf_op jit(solution)/shard_map/ppermute | solution.py:55
  25.3 0.1 sum_returned.1
  25.4 0.8 %collective-permute-start.8 = (bf16[16,4224]{1,0:T(8,128)(2,1)S(1)}, bf16[16,4224]{1,0:T(8,128)(2,1)S(1)}, u32[]{:S(2)}, u32[]{:S(2)}) collective-permute-start(bf16[16,4224]{1,0:T(8,128)(2,1)S(1)} %sum_returned.1), channel_id=1, source_target_pairs={{0,12},{4,0},{8,4},{12,8},{1,13},{5,1},{9,5},{13,9},{2,14},{6,2},{... | collective-permute-start | bytes 405512 | tf_op jit(solution)/shard_map/ppermute | solution.py:60
  26.2 0.0 collective-permute-done.9.refs_5_
  26.2 0.0 collective-permute-done.11.refs_7_
  26.2 0.7 %collective-permute-done.12.refs_8_ = bf16[64,1152]{1,0:T(8,128)(2,1)S(1)} collective-permute-done((bf16[64,1152]{1,0:T(8,128)(2,1)S(1)}, bf16[64,1152]{1,0:T(8,128)(2,1)S(1)}, u32[]{:S(2)}, u32[]{:S(2)}) %collective-permute-start.12) | collective-permute-done | bytes 147488 | tf_op jit(solution)/shard_map/ppermute | solution.py:44
  26.9 2.6 %weight_grads.1 = bf16[1,3,384,2048]{3,2,1,0:T(8,128)(2,1)} custom-call(bf16[64,1152]{1,0:T(8,128)(2,1)S(1)} %get-tuple-element.40.factors_ref, bf16[64,4096]{1,0:T(8,128)(2,1)S(1)} %get-tuple-element.41.inputs_ref, bf16[16,4096]{1,0:T(8,128)(2,1)S(1)} %get-tuple-element.30.refs_0_, bf16[16,4096]{1,0:T(8,128)(2,1)S(1)} %collective-permute-done.1.refs_1_, ...), custom_call_target="tpu_custom_call" | custom-call | flops 603979776 | bytes 1867776 | tf_op jit(solution)/shard_map/weight_grads/pallas_call | solution.py:71
  29.5 1.1 %collective-permute-done.8.changed_ref = bf16[16,4224]{1,0:T(8,128)(2,1)S(1)} collective-permute-done((bf16[16,4224]{1,0:T(8,128)(2,1)S(1)}, bf16[16,4224]{1,0:T(8,128)(2,1)S(1)}, u32[]{:S(2)}, u32[]{:S(2)}) %collective-permute-start.8) | collective-permute-done | bytes 135200 | tf_op jit(solution)/shard_map/ppermute | solution.py:60
  30.6 0.0 collective-permute-done.early_ref
  30.6 1.2 %merge.1 = bf16[1,1,128,4096]{3,2,1,0:T(8,128)(2,1)} custom-call(bf16[112,4096]{1,0:T(8,128)(2,1)S(1)} %collective-permute-done.early_ref, bf16[16,4224]{1,0:T(8,128)(2,1)S(1)} %collective-permute-done.8.changed_ref), custom_call_target="tpu_custom_call" | custom-call | flops 16777216 | bytes 1052672 | tf_op jit(solution)/shard_map/merge/pallas_call | solution.py:71
  (4 shorter events, 0.0 us)
Async XLA Ops:
  0.6 8.5 %slice-start = ((s8[9437184]{0:T(1024)(128)(4,1)}), s8[4194304]{0:T(1024)(128)(4,1)S(1)}, s32[]{:S(2)}) async-start(s8[9437184]{0:T(1024)(128)(4,1)} %bitcast.9), calls=%async_computation | async-start | bytes 8388608
  2.7 27.9 %collective-permute-start = (bf16[112,4096]{1,0:T(8,128)(2,1)S(1)}, bf16[112,4096]{1,0:T(8,128)(2,1)S(1)}, u32[]{:S(2)}, u32[]{:S(2)}) collective-permute-start(bf16[112,4096]{1,0:T(8,128)(2,1)S(1)} %get-tuple-element.22), channel_id=1, source_target_pairs={{0,12},{4,0},{8,4},{12,8},{1,13},{5,1},{9,5},{13,9},{2,14},{6,2},{... | collective-permute-start | bytes 2752520 | tf_op jit(solution)/shard_map/ppermute | solution.py:60
  7.6 2.2 %slice-start.1 = ((s8[9437184]{0:T(1024)(128)(4,1)}), s8[4194304]{0:T(1024)(128)(4,1)S(1)}, s32[]{:S(2)}) async-start(s8[9437184]{0:T(1024)(128)(4,1)} %bitcast.9), calls=%async_computation.1 | async-start | bytes 8388608
  7.6 2.5 %slice-start.2 = ((s8[9437184]{0:T(1024)(128)(4,1)}), s8[1048576]{0:T(1024)(128)(4,1)S(1)}, s32[]{:S(2)}) async-start(s8[9437184]{0:T(1024)(128)(4,1)} %bitcast.9), calls=%async_computation.2 | async-start | bytes 2097152
  7.6 2.6 %copy-start = (bf16[1,1,1,4,16,4096]{5,4,3,2,1,0:T(8,128)(2,1)S(1)}, bf16[1,1,1,4,16,4096]{5,4,3,2,1,0:T(8,128)(2,1)}, u32[]{:S(2)}) copy-start(bf16[1,1,1,4,16,4096]{5,4,3,2,1,0:T(8,128)(2,1)} %param.8) | copy-start | bytes 1572868
  7.6 5.0 %collective-permute-start.2 = (bf16[16,4096]{1,0:T(8,128)(2,1)S(1)}, bf16[16,4096]{1,0:T(8,128)(2,1)S(1)}, u32[]{:S(2)}, u32[]{:S(2)}) collective-permute-start(bf16[16,4096]{1,0:T(8,128)(2,1)S(1)} %get-tuple-element.30.refs_0_), channel_id=1, source_target_pairs={{0,2},{1,3},{2,0},{3,1},{4,6},{5,7},{6,4},{7,5},{8,10},{9,11},{10,... | collective-permute-start | bytes 393224 | tf_op jit(solution)/shard_map/ppermute | solution.py:55
  9.1 5.0 %collective-permute-start.1 = (bf16[16,4096]{1,0:T(8,128)(2,1)S(1)}, bf16[16,4096]{1,0:T(8,128)(2,1)S(1)}, u32[]{:S(2)}, u32[]{:S(2)}) collective-permute-start(bf16[16,4096]{1,0:T(8,128)(2,1)S(1)} %get-tuple-element.30.refs_0_), channel_id=1, source_target_pairs={{0,1},{1,0},{2,3},{3,2},{4,5},{5,4},{6,7},{7,6},{8,9},{9,8},{10,11... | collective-permute-start | bytes 393224 | tf_op jit(solution)/shard_map/ppermute | solution.py:48
  12.6 1.5 %collective-permute-start.3 = (bf16[16,4096]{1,0:T(8,128)(2,1)S(1)}, bf16[16,4096]{1,0:T(8,128)(2,1)S(1)}, u32[]{:S(2)}, u32[]{:S(2)}) collective-permute-start(bf16[16,4096]{1,0:T(8,128)(2,1)S(1)} %collective-permute-done.2.refs_2_.refs_1_), channel_id=1, source_target_pairs={{0,1},{1,0},{2,3},{3,2},{4,5},{5,4},{6,7},{7,6},{8,9},{9,8},{10,11... | collective-permute-start | bytes 393224 | tf_op jit(solution)/shard_map/ppermute | solution.py:48
  12.6 6.8 %collective-permute-start.6 = (bf16[32,2048]{1,0:T(8,128)(2,1)S(1)}, bf16[32,2048]{1,0:T(8,128)(2,1)S(1)}, u32[]{:S(2)}, u32[]{:S(2)}) collective-permute-start(bf16[32,2048]{1,0:T(8,128)(2,1)S(1)} %get-tuple-element.39), channel_id=1, source_target_pairs={{0,16},{16,0},{1,17},{17,1},{2,18},{18,2},{3,19},{19,3},{4,20},{20... | collective-permute-start | bytes 393224 | tf_op jit(solution)/shard_map/ppermute | solution.py:44
  17.7 1.7 %collective-permute-start.5 = (bf16[16,4096]{1,0:T(8,128)(2,1)S(1)}, bf16[16,4096]{1,0:T(8,128)(2,1)S(1)}, u32[]{:S(2)}, u32[]{:S(2)}) collective-permute-start(bf16[16,4096]{1,0:T(8,128)(2,1)S(1)} %get-tuple-element.38), channel_id=1, source_target_pairs={{0,1},{1,0},{2,3},{3,2},{4,5},{5,4},{6,7},{7,6},{8,9},{9,8},{10,11... | collective-permute-start | bytes 393224 | tf_op jit(solution)/shard_map/ppermute | solution.py:48
  18.0 5.8 %collective-permute-start.10 = (bf16[32,2048]{1,0:T(8,128)(2,1)S(1)}, bf16[32,2048]{1,0:T(8,128)(2,1)S(1)}, u32[]{:S(2)}, u32[]{:S(2)}) collective-permute-start(bf16[32,2048]{1,0:T(8,128)(2,1)S(1)} %pack.1), channel_id=1, source_target_pairs={{0,16},{16,0},{1,17},{17,1},{2,18},{18,2},{3,19},{19,3},{4,20},{20... | collective-permute-start | bytes 393224 | tf_op jit(solution)/shard_map/ppermute | solution.py:44
  19.3 4.4 %collective-permute-start.4 = (bf16[16,4096]{1,0:T(8,128)(2,1)S(1)}, bf16[16,4096]{1,0:T(8,128)(2,1)S(1)}, u32[]{:S(2)}, u32[]{:S(2)}) collective-permute-start(bf16[16,4096]{1,0:T(8,128)(2,1)S(1)} %get-tuple-element.37), channel_id=1, source_target_pairs={{0,1},{1,0},{2,3},{3,2},{4,5},{5,4},{6,7},{7,6},{8,9},{9,8},{10,11... | collective-permute-start | bytes 393224 | tf_op jit(solution)/shard_map/ppermute | solution.py:48
  19.4 5.9 %collective-permute-start.7 = (bf16[16,4096]{1,0:T(8,128)(2,1)S(1)}, bf16[16,4096]{1,0:T(8,128)(2,1)S(1)}, u32[]{:S(2)}, u32[]{:S(2)}) collective-permute-start(bf16[16,4096]{1,0:T(8,128)(2,1)S(1)} %pair_sums.1), channel_id=1, source_target_pairs={{2,0},{3,1},{0,2},{1,3},{6,4},{7,5},{4,6},{5,7},{10,8},{11,9},{8,1... | collective-permute-start | bytes 393224 | tf_op jit(solution)/shard_map/ppermute | solution.py:55
  21.0 5.9 %collective-permute-start.12 = (bf16[64,1152]{1,0:T(8,128)(2,1)S(1)}, bf16[64,1152]{1,0:T(8,128)(2,1)S(1)}, u32[]{:S(2)}, u32[]{:S(2)}) collective-permute-start(bf16[64,1152]{1,0:T(8,128)(2,1)S(1)} %get-tuple-element.40.factors_ref), channel_id=1, source_target_pairs={{0,16},{16,0},{1,17},{17,1},{2,18},{18,2},{3,19},{19,3},{4,20},{20... | collective-permute-start | bytes 442376 | tf_op jit(solution)/shard_map/ppermute | solution.py:44
  23.7 2.5 %collective-permute-start.9 = (bf16[32,2048]{1,0:T(8,128)(2,1)S(1)}, bf16[32,2048]{1,0:T(8,128)(2,1)S(1)}, u32[]{:S(2)}, u32[]{:S(2)}) collective-permute-start(bf16[32,2048]{1,0:T(8,128)(2,1)S(1)} %collective-permute-done.6.refs_1_.refs_4_), channel_id=1, source_target_pairs={{0,1},{1,0},{2,3},{3,2},{4,5},{5,4},{6,7},{7,6},{8,9},{9,8},{10,11... | collective-permute-start | bytes 393224 | tf_op jit(solution)/shard_map/ppermute | solution.py:48
  23.7 2.5 %collective-permute-start.11 = (bf16[32,2048]{1,0:T(8,128)(2,1)S(1)}, bf16[32,2048]{1,0:T(8,128)(2,1)S(1)}, u32[]{:S(2)}, u32[]{:S(2)}) collective-permute-start(bf16[32,2048]{1,0:T(8,128)(2,1)S(1)} %collective-permute-done.10.refs_6_), channel_id=1, source_target_pairs={{0,1},{1,0},{2,3},{3,2},{4,5},{5,4},{6,7},{7,6},{8,9},{9,8},{10,11... | collective-permute-start | bytes 393224 | tf_op jit(solution)/shard_map/ppermute | solution.py:48
  25.4 5.2 %collective-permute-start.8 = (bf16[16,4224]{1,0:T(8,128)(2,1)S(1)}, bf16[16,4224]{1,0:T(8,128)(2,1)S(1)}, u32[]{:S(2)}, u32[]{:S(2)}) collective-permute-start(bf16[16,4224]{1,0:T(8,128)(2,1)S(1)} %sum_returned.1), channel_id=1, source_target_pairs={{0,12},{4,0},{8,4},{12,8},{1,13},{5,1},{9,5},{13,9},{2,14},{6,2},{... | collective-permute-start | bytes 405512 | tf_op jit(solution)/shard_map/ppermute | solution.py:60
